TPU v7x, 32 devices: a whole 2x2x4 slice. The times are simulated.
32 devices in a mesh: dp: 4 (over y, core), ctx: 8 (over z, x).
Axes of the slice: x: 2, y: 2, z: 4, core: 2. Of those that a mesh axis runs over, the one named last changes fastest.
Arguments:
- tokens: bfloat16 [16, 2048, 1024], P('dp', 'ctx'), may hold values from -6 to 6
- cotangent: bfloat16 [16, 2048, 1024], P('dp', 'ctx'), may hold values from -6 to 6
- segments: int32 [16, 2048], P('dp', 'ctx'), may hold values from 0 to 3, as said below
- w_in: float32 [1024, 4384], P(('dp', 'ctx')), may hold values from -0.1875 to 0.1875
- w_out: float32 [2048, 1024], P(('dp', 'ctx')), may hold values from -0.125 to 0.125
- conv: float32 [2304, 5], P(('dp', 'ctx')), may hold values from -3 to 3
- gains: float32 [3072], P(('dp', 'ctx')), may hold values from 0.25 to 1.75
- heads: float32 [3, 32], replicated, may hold values from -9 to 3, as said below
- in_first: float32 [1024, 4384], P(('dp', 'ctx'))
- in_second: float32 [1024, 4384], P(('dp', 'ctx')), may hold values from 147 to 595
- out_first: float32 [2048, 1024], P(('dp', 'ctx'))
- out_second: float32 [2048, 1024], P(('dp', 'ctx')), may hold values from 1638 to 6553
- conv_first: float32 [2304, 5], P(('dp', 'ctx'))
- conv_second: float32 [2304, 5], P(('dp', 'ctx')), may hold values from 147 to 595
- gain_first: float32 [3072], P(('dp', 'ctx'))
- gain_second: float32 [3072], P(('dp', 'ctx')), may hold values from 595 to 2340
- head_first: float32 [3, 32], replicated
- head_second: float32 [3, 32], replicated, may hold values from 9362 to 37449
Outputs:
- output: bfloat16 [16, 2048, 1024], P('dp', 'ctx')
- grad_tokens: float32 [16, 2048, 1024], P('dp', 'ctx')
- in_first_new: float32 [1024, 4384], P(('dp', 'ctx'))
- in_second_new: float32 [1024, 4384], P(('dp', 'ctx'))
- in_weight_new: float32 [1024, 4384], P(('dp', 'ctx'))
- out_first_new: float32 [2048, 1024], P(('dp', 'ctx'))
- out_second_new: float32 [2048, 1024], P(('dp', 'ctx'))
- out_weight_new: float32 [2048, 1024], P(('dp', 'ctx'))
- conv_first_new: float32 [2304, 5], P(('dp', 'ctx'))
- conv_second_new: float32 [2304, 5], P(('dp', 'ctx'))
- conv_weight_new: float32 [2304, 5], P(('dp', 'ctx'))
- gain_first_new: float32 [3072], P(('dp', 'ctx'))
- gain_second_new: float32 [3072], P(('dp', 'ctx'))
- gain_vector_new: float32 [3072], P(('dp', 'ctx'))
- head_first_new: float32 [3, 32], replicated
- head_second_new: float32 [3, 32], replicated
- head_params_new: float32 [3, 32], replicated
Inputs may be any that keep to these rules, and one draw needn't show every extreme that they name: `segments`: each row starts at 0, never falls and rises by one at exactly three tokens or never; among the 4 rows of one index of dp, one holds a single document. `heads`: row 0 holds the logarithms of the decay rates, row 1 the skip gains, row 2 the step biases.
All inputs are finite; a program needn't handle non-finite values.
Results may differ from a plain program's by a relative error of at most 0.004.
The roundings to bfloat16 on the way count: a program that leaves them out, or rounds other values in their place, can miss the bound.
Values may be sent and summed in bfloat16 or wider, within the bound.
No kernel may reach another device: no remote copies, remote signals or barrier semaphores. Data moves between devices by JAX's collectives and lax.ppermute only.
A program may use at most 256 MiB of HBM per device.

v0:
```python
import jax
import jax.numpy as jnp
from jax import lax
from jax.sharding import PartitionSpec as P

STEP = 10


EPSILON = 1e-05
BETA_ONE = 0.9
BETA_TWO = 0.95
ADAM_EPS = 1e-08
DECAY_RATE = 0.1
RATE_IN = 0.03
RATE_OUT = 0.02
RATE_CONV = 0.3
RATE_GAIN = 0.2
RATE_HEAD = 0.5


def shifted(value, axis, steps):
    count = lax.axis_size(axis)
    first, last = (max(0, -steps), min(count, count - steps))
    return lax.ppermute(value, axis, [(source, source + steps) for source in range(first, last)])


def inverse_rms(values):
    return lax.rsqrt(jnp.mean(values * values, axis=-1, keepdims=True) + EPSILON)


def silu_slope(values):
    sigmoid_val = jax.nn.sigmoid(values)
    return sigmoid_val * (1.0 + values * (1.0 - sigmoid_val))


def block_mixing(b_state, c_state, step_size, decay_sum, segment):
    length = segment.shape[0]
    positions = lax.iota(jnp.int32, length)
    causal = (positions[:, None] >= positions[None, :]) & (segment[:, None] == segment[None, :])
    span_sums = decay_sum.T[:, :, None] - decay_sum.T[:, None, :]
    decay_mat = jnp.where(causal[None], jnp.exp(jnp.where(causal[None], span_sums, 0.0)), 0.0)
    scores = jnp.dot(c_state, b_state.T, preferred_element_type=jnp.float32)
    mixing = scores[None] * decay_mat * step_size.T[:, None, :]
    return (scores, decay_mat, mixing)


def block_forward(block_item):
    x_heads, b_state, c_state, step_size, decay_sum, segment = block_item
    scores, decay_mat, mixing = block_mixing(b_state, c_state, step_size, decay_sum, segment)
    return jnp.einsum(
        "hts,shp->thp", mixing.astype(jnp.bfloat16), x_heads, preferred_element_type=jnp.float32
    )


def block_backward(block_item):
    x_heads, b_state, c_state, step_size, decay_sum, segment, grad_ssd = block_item
    scores, decay_mat, mixing = block_mixing(b_state, c_state, step_size, decay_sum, segment)
    grad_mixing = jnp.einsum("thp,shp->hts", grad_ssd, x_heads, preferred_element_type=jnp.float32)
    grad_x = jnp.einsum(
        "hts,thp->shp", mixing.astype(jnp.bfloat16), grad_ssd, preferred_element_type=jnp.float32
    )
    grad_scores = jnp.sum(grad_mixing * decay_mat * step_size.T[:, None, :], axis=0).astype(
        jnp.bfloat16
    )
    grad_step = jnp.sum(grad_mixing * scores[None] * decay_mat, axis=1).T
    spread_grad = grad_mixing * mixing
    grad_decay = (jnp.sum(spread_grad, axis=2) - jnp.sum(spread_grad, axis=1)).T
    grad_c = jnp.dot(grad_scores, b_state, preferred_element_type=jnp.float32)
    grad_b = jnp.dot(grad_scores.T, c_state, preferred_element_type=jnp.float32)
    return (grad_x, grad_b, grad_c, grad_step, grad_decay)


def adamw(weight, gradient, first_moment, second_moment, step_rate):
    first_new = BETA_ONE * first_moment + (1.0 - BETA_ONE) * gradient
    second_new = BETA_TWO * second_moment + (1.0 - BETA_TWO) * gradient * gradient
    corrected = first_new / (1.0 - BETA_ONE**STEP)
    spread = jnp.sqrt(second_new / (1.0 - BETA_TWO**STEP))
    weight_new = weight - step_rate * (corrected / (spread + ADAM_EPS) + DECAY_RATE * weight)
    return (first_new, second_new, weight_new)


def local(
    tokens,
    cotangent,
    segments,
    w_in,
    w_out,
    conv,
    gains,
    heads,
    in_first,
    in_second,
    out_first,
    out_second,
    conv_first,
    conv_second,
    gain_first,
    gain_second,
    head_first,
    head_second,
):
    owned = (
        w_in.astype(jnp.bfloat16),
        w_out.astype(jnp.bfloat16),
        conv.astype(jnp.bfloat16),
        gains.astype(jnp.bfloat16),
    )
    input_weight, output_weight, conv_weight, gain_vector = (
        lax.all_gather(owned[0], ("dp", "ctx"), axis=0, tiled=True),
        lax.all_gather(owned[1], ("dp", "ctx"), axis=0, tiled=True),
        lax.all_gather(owned[2], ("dp", "ctx"), axis=0, tiled=True),
        lax.all_gather(owned[3], ("dp", "ctx"), axis=0, tiled=True),
    )
    seq_count, length, model_width = tokens.shape
    inner_width = output_weight.shape[0]
    channels = conv_weight.shape[0]
    kernel_taps = conv_weight.shape[1] - 1
    state_dim = (channels - inner_width) // 2
    heads_count = heads.shape[1]
    head_dim = inner_width // heads_count
    input_float = tokens.astype(jnp.float32)
    gain_float = gain_vector.astype(jnp.float32)
    gain_in = gain_float[:model_width]
    gain_out = gain_float[model_width:]
    scale_in = inverse_rms(input_float)
    unit_in = input_float * scale_in
    normalized_rows = (unit_in * gain_in).astype(jnp.bfloat16)
    projected_rows = jnp.einsum(
        "aok,ku->aou", normalized_rows, input_weight, preferred_element_type=jnp.float32
    )
    gate_raw = projected_rows[:, :, :inner_width]
    conv_in = projected_rows[:, :, inner_width : inner_width + channels].astype(jnp.bfloat16)
    step_raw = projected_rows[:, :, inner_width + channels :]
    rim_x, rim_seg = shifted(
        (conv_in[:, length - kernel_taps + 1 :], segments[:, length - kernel_taps + 1 :]), "ctx", 1
    )
    wide_x = jnp.concatenate([rim_x, conv_in], axis=1)
    wide_seg = jnp.concatenate([rim_seg, segments], axis=1)
    conv_float = conv_weight.astype(jnp.float32)
    same_doc = [
        (wide_seg[:, offset : offset + length] == segments).astype(jnp.float32)[:, :, None]
        for offset in range(kernel_taps)
    ]
    pre_act = jnp.broadcast_to(conv_float[:, kernel_taps], (seq_count, length, channels))
    for offset in range(kernel_taps):
        pre_act = (
            pre_act + conv_float[:, offset] * wide_x[:, offset : offset + length] * same_doc[offset]
        )
    activated = jax.nn.silu(pre_act).astype(jnp.bfloat16)
    x_heads = activated[:, :, :inner_width].reshape(seq_count, length, heads_count, head_dim)
    b_state = activated[:, :, inner_width : inner_width + state_dim]
    c_state = activated[:, :, inner_width + state_dim :]
    step_size = jax.nn.softplus(step_raw + heads[2])
    head_rate = -jnp.exp(heads[0])
    decay_sum = jnp.cumsum(step_size * head_rate, axis=1)
    within_block = lax.map(
        block_forward, (x_heads, b_state, c_state, step_size, decay_sum, segments)
    )
    tail_doc = (segments == segments[:, length - 1 :]).astype(jnp.float32)[:, :, None]
    fall_off = jnp.exp(decay_sum[:, length - 1 :] - decay_sum) * tail_doc
    end_weight = fall_off * step_size
    scaled = (end_weight[..., None] * x_heads).astype(jnp.bfloat16)
    local_state = jnp.einsum("slhp,sln->shpn", scaled, b_state, preferred_element_type=jnp.float32)
    link_doc = (segments == rim_seg[:, kernel_taps - 2 :]).astype(jnp.float32)[:, :, None]
    entry_decay = jnp.exp(decay_sum) * link_doc
    passing = entry_decay[:, length - 1]

    def forward_hop(hop_index, carried):
        return shifted(passing[:, :, None, None] * carried + local_state, "ctx", 1)

    incoming = lax.fori_loop(0, lax.axis_size("ctx") - 1, forward_hop, jnp.zeros_like(local_state))
    incoming_low = incoming.astype(jnp.bfloat16)
    from_before = jnp.einsum(
        "sln,shpn->slhp", c_state, incoming_low, preferred_element_type=jnp.float32
    )
    ssd_out = within_block + heads[1][:, None] * x_heads + entry_decay[..., None] * from_before
    ssd_flat = ssd_out.reshape(seq_count, length, inner_width)
    gate_silu = jax.nn.silu(gate_raw)
    gated = ssd_flat * gate_silu
    scale_out = inverse_rms(gated)
    unit_out = gated * scale_out
    mixer_output = (unit_out * gain_out).astype(jnp.bfloat16)
    output = (
        input_float
        + jnp.einsum("exp,pk->exk", mixer_output, output_weight, preferred_element_type=jnp.float32)
    ).astype(jnp.bfloat16)
    grad_out_weight = jnp.einsum(
        "gva,gvk->ak", mixer_output, cotangent, preferred_element_type=jnp.float32
    )
    grad_mixed = jnp.einsum(
        "pjy,hy->pjh", cotangent, output_weight, preferred_element_type=jnp.float32
    )
    grad_gain_out = jnp.sum(grad_mixed * unit_out, axis=(0, 1))
    grad_unit = grad_mixed * gain_out
    grad_gated = scale_out * (
        grad_unit - unit_out * jnp.mean(grad_unit * unit_out, axis=-1, keepdims=True)
    )
    grad_ssd = (
        (grad_gated * gate_silu)
        .astype(jnp.bfloat16)
        .reshape(seq_count, length, heads_count, head_dim)
    )
    grad_gate = grad_gated * ssd_flat * silu_slope(gate_raw)
    grad_skip = jnp.einsum("slhp,slhp->h", grad_ssd, x_heads, preferred_element_type=jnp.float32)
    grad_entry = jnp.sum(grad_ssd * from_before, axis=3)
    grad_before = (grad_ssd * entry_decay[..., None]).astype(jnp.bfloat16)
    grad_c_outer = jnp.einsum(
        "slhp,shpn->sln", grad_before, incoming_low, preferred_element_type=jnp.float32
    )
    grad_incoming = jnp.einsum(
        "slhp,sln->shpn", grad_before, c_state, preferred_element_type=jnp.float32
    )

    def backward_hop(hop_index, carried):
        return shifted(passing[:, :, None, None] * carried + grad_incoming, "ctx", -1)

    grad_leaving = lax.fori_loop(
        0, lax.axis_size("ctx") - 1, backward_hop, jnp.zeros_like(grad_incoming)
    )
    grad_passing = jnp.sum(grad_leaving * incoming, axis=(2, 3))
    grad_local = grad_leaving.astype(jnp.bfloat16)
    grad_scaled = jnp.einsum(
        "shpn,sln->slhp", grad_local, b_state, preferred_element_type=jnp.float32
    )
    grad_b_state = jnp.einsum(
        "slhp,shpn->sln", scaled, grad_local, preferred_element_type=jnp.float32
    )
    grad_end = jnp.sum(grad_scaled * x_heads, axis=3)
    inner_x, inner_b, inner_c, inner_step, inner_decay = lax.map(
        block_backward, (x_heads, b_state, c_state, step_size, decay_sum, segments, grad_ssd)
    )
    spread_end = grad_end * end_weight
    grad_decay = inner_decay + grad_entry * entry_decay - spread_end
    grad_decay = grad_decay.at[:, length - 1].add(
        jnp.sum(spread_end, axis=1) + grad_passing * passing
    )
    grad_later = jnp.flip(jnp.cumsum(jnp.flip(grad_decay, 1), axis=1), 1)
    grad_step = inner_step + grad_end * fall_off + grad_later * head_rate
    grad_log_rate = jnp.sum(grad_later * step_size, axis=(0, 1)) * head_rate
    grad_step_raw = grad_step * jax.nn.sigmoid(step_raw + heads[2])
    grad_step_bias = jnp.sum(grad_step_raw, axis=(0, 1))
    grad_x = inner_x + heads[1][:, None] * grad_ssd + end_weight[..., None] * grad_scaled
    grad_act = jnp.concatenate(
        [
            grad_x.reshape(seq_count, length, inner_width),
            inner_b + grad_b_state,
            inner_c + grad_c_outer,
        ],
        axis=2,
    )
    grad_pre = grad_act * silu_slope(pre_act)
    grad_bias = jnp.sum(grad_pre, axis=(0, 1))
    grad_taps = []
    grad_wide = jnp.zeros((seq_count, length + kernel_taps - 1, channels), jnp.float32)
    for offset in range(kernel_taps):
        masked = grad_pre * same_doc[offset]
        grad_taps.append(jnp.sum(masked * wide_x[:, offset : offset + length], axis=(0, 1)))
        grad_wide = grad_wide + jnp.pad(
            masked * conv_float[:, offset], ((0, 0), (offset, kernel_taps - 1 - offset), (0, 0))
        )
    rim_back = shifted(grad_wide[:, : kernel_taps - 1].astype(jnp.bfloat16), "ctx", -1).astype(
        jnp.float32
    )
    grad_conv_in = grad_wide[:, kernel_taps - 1 :].at[:, length - kernel_taps + 1 :].add(rim_back)
    projection_gradient = jnp.concatenate([grad_gate, grad_conv_in, grad_step_raw], axis=2).astype(
        jnp.bfloat16
    )
    grad_in_weight = jnp.einsum(
        "nay,nag->yg", normalized_rows, projection_gradient, preferred_element_type=jnp.float32
    )
    grad_normed = jnp.einsum(
        "hou,qu->hoq", projection_gradient, input_weight, preferred_element_type=jnp.float32
    )
    grad_gain_in = jnp.sum(grad_normed * unit_in, axis=(0, 1))
    grad_unit_in = grad_normed * gain_in
    grad_tokens = cotangent.astype(jnp.float32) + scale_in * (
        grad_unit_in - unit_in * jnp.mean(grad_unit_in * unit_in, axis=-1, keepdims=True)
    )
    grad_conv = jnp.stack(grad_taps + [grad_bias], axis=1)
    grad_gains = jnp.concatenate([grad_gain_in, grad_gain_out])
    grad_heads = jnp.stack([grad_log_rate, grad_skip, grad_step_bias])
    grad_terms = (grad_in_weight, grad_out_weight, grad_conv, grad_gains)
    owned_grads = (
        lax.psum_scatter(grad_terms[0], ("dp", "ctx"), scatter_dimension=0, tiled=True),
        lax.psum_scatter(grad_terms[1], ("dp", "ctx"), scatter_dimension=0, tiled=True),
        lax.psum_scatter(grad_terms[2], ("dp", "ctx"), scatter_dimension=0, tiled=True),
        lax.psum_scatter(grad_terms[3], ("dp", "ctx"), scatter_dimension=0, tiled=True),
    )
    head_grad = lax.psum(grad_heads, ("dp", "ctx"))
    in_new = adamw(w_in, owned_grads[0], in_first, in_second, RATE_IN)
    out_new = adamw(w_out, owned_grads[1], out_first, out_second, RATE_OUT)
    conv_new = adamw(conv, owned_grads[2], conv_first, conv_second, RATE_CONV)
    gain_new = adamw(gains, owned_grads[3], gain_first, gain_second, RATE_GAIN)
    head_new = adamw(heads, head_grad, head_first, head_second, RATE_HEAD)
    return (
        output,
        grad_tokens,
        in_new[0],
        in_new[1],
        in_new[2],
        out_new[0],
        out_new[1],
        out_new[2],
        conv_new[0],
        conv_new[1],
        conv_new[2],
        gain_new[0],
        gain_new[1],
        gain_new[2],
        head_new[0],
        head_new[1],
        head_new[2],
    )


def solution(mesh):
    placed = (
        P("dp", "ctx", None),
        P("dp", "ctx", None),
        P("dp", "ctx"),
        P(("dp", "ctx"), None),
        P(("dp", "ctx"), None),
        P(("dp", "ctx"), None),
        P(("dp", "ctx")),
        P(),
        P(("dp", "ctx"), None),
        P(("dp", "ctx"), None),
        P(("dp", "ctx"), None),
        P(("dp", "ctx"), None),
        P(("dp", "ctx"), None),
        P(("dp", "ctx"), None),
        P(("dp", "ctx")),
        P(("dp", "ctx")),
        P(),
        P(),
    )
    return jax.shard_map(
        local,
        mesh=mesh,
        in_specs=placed,
        out_specs=(
            P("dp", "ctx", None),
            P("dp", "ctx", None),
            P(("dp", "ctx"), None),
            P(("dp", "ctx"), None),
            P(("dp", "ctx"), None),
            P(("dp", "ctx"), None),
            P(("dp", "ctx"), None),
            P(("dp", "ctx"), None),
            P(("dp", "ctx"), None),
            P(("dp", "ctx"), None),
            P(("dp", "ctx"), None),
            P(("dp", "ctx")),
            P(("dp", "ctx")),
            P(("dp", "ctx")),
            P(),
            P(),
            P(),
        ),
        check_vma=False,
    )
```

profile of v0, /device:TPU:0, one launch (start us, length us, event | category | flops | bytes accessed | tf_op | source)
XLA Modules:
  0.0 2558.5 jit_solution(2056484875849800275)
XLA Ops:
  15.6 41.1 %all-reduce.4 = bf16[3072]{0:T(1024)(128)(2,1)S(1)} all-reduce(bf16[3072]{0:T(1024)(128)(2,1)S(1)} %dynamic-update-slice.6), channel_id=1, replica_groups=mesh['dp'=4,'ctx'=8] {'dp','ctx'}, use_global_device_ids=true, to_apply=%add.4 | all-reduce | flops 3072 | bytes 12288
  57.4 67.2 %all-gather = bf16[32,72,5]{1,2,0:T(8,128)(2,1)S(1)} all-gather(bf16[1,72,5]{1,2,0:T(8,128)(2,1)S(1)} %convert_bitcast_fusion), channel_id=1, replica_groups=mesh['dp'=4,'ctx'=8] {'dp','ctx'}, dimensions={0}, use_global_device_ids=true | all-gather | bytes 23760 | tf_op jit(solution)/shard_map/all_gather | solution.py:111
  219.5 681.7 %while.51 = (s32[]{:T(128)}, f32[4,32,64,128]{3,2,1,0:T(8,128)}, f32[4,1,32]{2,0,1:T(4,128)S(1)}, f32[4,32,64,128]{3,2,1,0:T(8,128)}, s32[]{:T(128)}) while((s32[]{:T(128)}, f32[4,32,64,128]{3,2,1,0:T(8,128)}, f32[4,1,32]{2,0,1:T(4,128)S(1)}, f32[4,32,64,128]{3,2,1,0:T(8,128)}, s32[]{:T(128)}) %tuple.147), condition=%wide.region_6.7_spmd, body=%wide.region_5.6_spmd.sunk | while | flops 2097154 | bytes 29360740 | solution.py:171
  230.1 82.0 %collective-permute-done = f32[4,32,64,128]{3,2,1,0:T(8,128)} collective-permute-done((f32[4,32,64,128]{3,2,1,0:T(8,128)}, f32[4,32,64,128]{3,2,1,0:T(8,128)}, u32[]{:S(2)}, u32[]{:S(2)}) %collective-permute-start) | collective-permute-done | bytes 4194336 | tf_op jit(solution)/shard_map/while/body/eval_jaxpr/ppermute | solution.py:24
  324.5 81.1 %collective-permute-done = f32[4,32,64,128]{3,2,1,0:T(8,128)} collective-permute-done((f32[4,32,64,128]{3,2,1,0:T(8,128)}, f32[4,32,64,128]{3,2,1,0:T(8,128)}, u32[]{:S(2)}, u32[]{:S(2)}) %collective-permute-start) | collective-permute-done | bytes 4194336 | tf_op jit(solution)/shard_map/while/body/eval_jaxpr/ppermute | solution.py:24
  418.6 82.2 %collective-permute-done = f32[4,32,64,128]{3,2,1,0:T(8,128)} collective-permute-done((f32[4,32,64,128]{3,2,1,0:T(8,128)}, f32[4,32,64,128]{3,2,1,0:T(8,128)}, u32[]{:S(2)}, u32[]{:S(2)}) %collective-permute-start) | collective-permute-done | bytes 4194336 | tf_op jit(solution)/shard_map/while/body/eval_jaxpr/ppermute | solution.py:24
  516.8 83.5 %collective-permute-done = f32[4,32,64,128]{3,2,1,0:T(8,128)} collective-permute-done((f32[4,32,64,128]{3,2,1,0:T(8,128)}, f32[4,32,64,128]{3,2,1,0:T(8,128)}, u32[]{:S(2)}, u32[]{:S(2)}) %collective-permute-start) | collective-permute-done | bytes 4194336 | tf_op jit(solution)/shard_map/while/body/eval_jaxpr/ppermute | solution.py:24
  620.4 85.0 %collective-permute-done = f32[4,32,64,128]{3,2,1,0:T(8,128)} collective-permute-done((f32[4,32,64,128]{3,2,1,0:T(8,128)}, f32[4,32,64,128]{3,2,1,0:T(8,128)}, u32[]{:S(2)}, u32[]{:S(2)}) %collective-permute-start) | collective-permute-done | bytes 4194336 | tf_op jit(solution)/shard_map/while/body/eval_jaxpr/ppermute | solution.py:24
  718.7 84.1 %collective-permute-done = f32[4,32,64,128]{3,2,1,0:T(8,128)} collective-permute-done((f32[4,32,64,128]{3,2,1,0:T(8,128)}, f32[4,32,64,128]{3,2,1,0:T(8,128)}, u32[]{:S(2)}, u32[]{:S(2)}) %collective-permute-start) | collective-permute-done | bytes 4194336 | tf_op jit(solution)/shard_map/while/body/eval_jaxpr/ppermute | solution.py:24
  817.5 83.7 %collective-permute-done = f32[4,32,64,128]{3,2,1,0:T(8,128)} collective-permute-done((f32[4,32,64,128]{3,2,1,0:T(8,128)}, f32[4,32,64,128]{3,2,1,0:T(8,128)}, u32[]{:S(2)}, u32[]{:S(2)}) %collective-permute-start) | collective-permute-done | bytes 4194336 | tf_op jit(solution)/shard_map/while/body/eval_jaxpr/ppermute | solution.py:24
  930.6 198.9 %reduce-scatter.6.cloned.1.call-done = f32[64,1024]{1,0:T(8,128)} async-done(((f32[2048,1024]{1,0:T(8,128)}), f32[64,1024]{1,0:T(8,128)}) %reduce-scatter.6.cloned.1.call-update) | async-done | bytes 262160 | tf_op jit(solution)/shard_map/reduce_scatter | solution.py:285
  1131.6 62.6 %all-gather.6.cloned.1.call-done = bf16[2048,1024]{1,0:T(8,128)(2,1)} async-done(((bf16[64,1024]{1,0:T(8,128)(2,1)}), bf16[2048,1024]{1,0:T(8,128)(2,1)}) %all-gather.6.cloned.1.call-update) | async-done | bytes 4194320 | tf_op jit(solution)/shard_map/all_gather | solution.py:110
  1241.7 67.4 %while.52 = (s32[]{:T(128)}, f32[4,256,32,64]{1,3,2,0:T(8,128)}, f32[4,256,128]{1,2,0:T(8,128)}, f32[4,256,128]{1,2,0:T(8,128)}, f32[4,256,32]{1,2,0:T(8,128)}, ...) while((s32[]{:T(128)}, f32[4,256,32,64]{1,3,2,0:T(8,128)}, ...), condition=%wide.region_14.15_spmd, body=%wide.region_9.14_spmd.sunk | while | flops 629260288 | bytes 7741597 | solution.py:229
  1311.7 691.9 %while.53 = (s32[]{:T(128)}, f32[4,32,64,128]{3,2,1,0:T(8,128)}, f32[4,1,32]{2,0,1:T(4,128)S(1)}, f32[4,32,64,128]{3,2,1,0:T(8,128)}, s32[]{:T(128)}) while((s32[]{:T(128)}, f32[4,32,64,128]{3,2,1,0:T(8,128)}, f32[4,1,32]{2,0,1:T(4,128)S(1)}, f32[4,32,64,128]{3,2,1,0:T(8,128)}, s32[]{:T(128)}) %tuple.171), condition=%wide.region_16.17_spmd, body=%wide.region_15.16_spmd.sunk | while | flops 2097154 | bytes 29360740 | solution.py:217
  1318.8 93.6 %collective-permute-done.1 = f32[4,32,64,128]{3,2,1,0:T(8,128)} collective-permute-done((f32[4,32,64,128]{3,2,1,0:T(8,128)}, f32[4,32,64,128]{3,2,1,0:T(8,128)}, u32[]{:S(2)}, u32[]{:S(2)}) %collective-permute-start.1) | collective-permute-done | bytes 4194336 | tf_op jit(solution)/shard_map/while/body/eval_jaxpr/ppermute | solution.py:24
  1419.7 93.3 %collective-permute-done.1 = f32[4,32,64,128]{3,2,1,0:T(8,128)} collective-permute-done((f32[4,32,64,128]{3,2,1,0:T(8,128)}, f32[4,32,64,128]{3,2,1,0:T(8,128)}, u32[]{:S(2)}, u32[]{:S(2)}) %collective-permute-start.1) | collective-permute-done | bytes 4194336 | tf_op jit(solution)/shard_map/while/body/eval_jaxpr/ppermute | solution.py:24
  1520.1 92.8 %collective-permute-done.1 = f32[4,32,64,128]{3,2,1,0:T(8,128)} collective-permute-done((f32[4,32,64,128]{3,2,1,0:T(8,128)}, f32[4,32,64,128]{3,2,1,0:T(8,128)}, u32[]{:S(2)}, u32[]{:S(2)}) %collective-permute-start.1) | collective-permute-done | bytes 4194336 | tf_op jit(solution)/shard_map/while/body/eval_jaxpr/ppermute | solution.py:24
  1620.1 91.9 %collective-permute-done.1 = f32[4,32,64,128]{3,2,1,0:T(8,128)} collective-permute-done((f32[4,32,64,128]{3,2,1,0:T(8,128)}, f32[4,32,64,128]{3,2,1,0:T(8,128)}, u32[]{:S(2)}, u32[]{:S(2)}) %collective-permute-start.1) | collective-permute-done | bytes 4194336 | tf_op jit(solution)/shard_map/while/body/eval_jaxpr/ppermute | solution.py:24
  1719.1 91.0 %collective-permute-done.1 = f32[4,32,64,128]{3,2,1,0:T(8,128)} collective-permute-done((f32[4,32,64,128]{3,2,1,0:T(8,128)}, f32[4,32,64,128]{3,2,1,0:T(8,128)}, u32[]{:S(2)}, u32[]{:S(2)}) %collective-permute-start.1) | collective-permute-done | bytes 4194336 | tf_op jit(solution)/shard_map/while/body/eval_jaxpr/ppermute | solution.py:24
  1817.3 90.0 %collective-permute-done.1 = f32[4,32,64,128]{3,2,1,0:T(8,128)} collective-permute-done((f32[4,32,64,128]{3,2,1,0:T(8,128)}, f32[4,32,64,128]{3,2,1,0:T(8,128)}, u32[]{:S(2)}, u32[]{:S(2)}) %collective-permute-start.1) | collective-permute-done | bytes 4194336 | tf_op jit(solution)/shard_map/while/body/eval_jaxpr/ppermute | solution.py:24
  1914.5 89.1 %collective-permute-done.1 = f32[4,32,64,128]{3,2,1,0:T(8,128)} collective-permute-done((f32[4,32,64,128]{3,2,1,0:T(8,128)}, f32[4,32,64,128]{3,2,1,0:T(8,128)}, u32[]{:S(2)}, u32[]{:S(2)}) %collective-permute-start.1) | collective-permute-done | bytes 4194336 | tf_op jit(solution)/shard_map/while/body/eval_jaxpr/ppermute | solution.py:24
  2110.3 26.5 %scatter-add.6 = bf16[4,256,2304]{1,2,0:T(8,128)(2,1)} dynamic-update-slice(bf16[4,256,2304]{1,2,0:T(8,128)(2,1)} %slice.223, bf16[4,3,2304]{1,2,0:T(8,128)(2,1)S(1)} %slice_add_fusion, s32[]{:T(128)} %constant.179.clone.1, s32[]{:T(128)} %constant.185.clone.1, s32[]{:T(128)} %constant.179.clone.1) | dynamic-update-slice | bytes 110596 | tf_op jit(solution)/shard_map/scatter-add | solution.py:264
  2188.3 49.3 %all-reduce.7 = (f32[2304,5]{0,1:T(8,128)S(1)}, f32[3072]{0:T(1024)S(1)}, f32[3,32]{1,0:T(4,128)S(1)}) all-reduce(f32[2304,5]{0,1:T(8,128)S(1)} %stack.33, f32[3072]{0:T(1024)S(1)} %pad_maximum_fusion.4, f32[3,32]{1,0:T(4,128)S(1)} %pad_maximum_fusion.5), channel_id=4, replica_groups=mesh['dp'=4,'ctx'=8] {'dp','ctx'}, use_global_device_ids=true, to_apply=%region_31.32.clone | all-reduce | flops 14688 | bytes 117504
  2244.4 304.4 %reduce-scatter.4.cloned.1.call-done = f32[32,4384]{1,0:T(8,128)} async-done(((f32[1024,4384]{1,0:T(8,128)}), f32[32,4384]{1,0:T(8,128)}) %reduce-scatter.4.cloned.1.call-update) | async-done | bytes 561168 | tf_op jit(solution)/shard_map/reduce_scatter | solution.py:284
  (382 shorter events, 589.5 us)
Async XLA Ops:
  7.2 123.0 %all-gather.4.cloned.1.call-start = ((), (), s32[]{:S(2)}) async-start(), calls=%async_computation.2 | async-start | bytes 9461760 | tf_op jit(solution)/shard_map/all_gather | solution.py:109
  9.1 1120.4 %reduce-scatter.6.cloned.1.call-start = ((), (), s32[]{:S(2)}) async-start(), calls=%async_computation.5 | async-start | bytes 8650752 | tf_op jit(solution)/shard_map/reduce_scatter | solution.py:285
  9.9 118.9 %collective-permute-start.3 = (s32[4,3]{1,0:T(4,128)S(1)}, s32[4,3]{1,0:T(4,128)S(1)}, u32[]{:S(2)}, u32[]{:S(2)}) collective-permute-start(s32[4,3]{1,0:T(4,128)S(1)} %slice.167), channel_id=1, source_target_pairs={{0,1},{1,2},{2,3},{3,4},{4,5},{5,6},{6,7},{8,9},{9,10},{10,11},{11... | collective-permute-start | bytes 152 | tf_op jit(solution)/shard_map/ppermute | solution.py:24
  56.7 1164.8 %copy-start.44 = (f32[2048]{0:T(1024)}, f32[2048]{0:T(1024)S(1)}, u32[]{:S(2)}) copy-start(f32[2048]{0:T(1024)S(1)} %slice.222) | copy-start | bytes 24580
  126.6 774.6 %copy-start.66 = (f32[32]{0:T(128)}, f32[32]{0:T(128)S(1)}, u32[]{:S(2)}) copy-start(f32[32]{0:T(128)S(1)} %get-tuple-element.466) | copy-start | bytes 388
  152.3 13.4 collective-permute-start.2
  225.5 86.6 %collective-permute-start = (f32[4,32,64,128]{3,2,1,0:T(8,128)}, f32[4,32,64,128]{3,2,1,0:T(8,128)}, u32[]{:S(2)}, u32[]{:S(2)}) collective-permute-start(f32[4,32,64,128]{3,2,1,0:T(8,128)} %multiply_add_fusion.14), channel_id=1, source_target_pairs={{0,1},{1,2},{2,3},{3,4},{4,5},{5,6},{6,7},{8,9},{9,10},{10,11},{11... | collective-permute-start | bytes 12582920 | tf_op jit(solution)/shard_map/while/body/eval_jaxpr/ppermute | solution.py:24
  318.1 87.5 %collective-permute-start = (f32[4,32,64,128]{3,2,1,0:T(8,128)}, f32[4,32,64,128]{3,2,1,0:T(8,128)}, u32[]{:S(2)}, u32[]{:S(2)}) collective-permute-start(f32[4,32,64,128]{3,2,1,0:T(8,128)} %multiply_add_fusion.14), channel_id=1, source_target_pairs={{0,1},{1,2},{2,3},{3,4},{4,5},{5,6},{6,7},{8,9},{9,10},{10,11},{11... | collective-permute-start | bytes 12582920 | tf_op jit(solution)/shard_map/while/body/eval_jaxpr/ppermute | solution.py:24
  411.5 89.3 %collective-permute-start = (f32[4,32,64,128]{3,2,1,0:T(8,128)}, f32[4,32,64,128]{3,2,1,0:T(8,128)}, u32[]{:S(2)}, u32[]{:S(2)}) collective-permute-start(f32[4,32,64,128]{3,2,1,0:T(8,128)} %multiply_add_fusion.14), channel_id=1, source_target_pairs={{0,1},{1,2},{2,3},{3,4},{4,5},{5,6},{6,7},{8,9},{9,10},{10,11},{11... | collective-permute-start | bytes 12582920 | tf_op jit(solution)/shard_map/while/body/eval_jaxpr/ppermute | solution.py:24
  506.8 93.5 %collective-permute-start = (f32[4,32,64,128]{3,2,1,0:T(8,128)}, f32[4,32,64,128]{3,2,1,0:T(8,128)}, u32[]{:S(2)}, u32[]{:S(2)}) collective-permute-start(f32[4,32,64,128]{3,2,1,0:T(8,128)} %multiply_add_fusion.14), channel_id=1, source_target_pairs={{0,1},{1,2},{2,3},{3,4},{4,5},{5,6},{6,7},{8,9},{9,10},{10,11},{11... | collective-permute-start | bytes 12582920 | tf_op jit(solution)/shard_map/while/body/eval_jaxpr/ppermute | solution.py:24
  606.3 99.2 %collective-permute-start = (f32[4,32,64,128]{3,2,1,0:T(8,128)}, f32[4,32,64,128]{3,2,1,0:T(8,128)}, u32[]{:S(2)}, u32[]{:S(2)}) collective-permute-start(f32[4,32,64,128]{3,2,1,0:T(8,128)} %multiply_add_fusion.14), channel_id=1, source_target_pairs={{0,1},{1,2},{2,3},{3,4},{4,5},{5,6},{6,7},{8,9},{9,10},{10,11},{11... | collective-permute-start | bytes 12582920 | tf_op jit(solution)/shard_map/while/body/eval_jaxpr/ppermute | solution.py:24
  711.4 91.3 %collective-permute-start = (f32[4,32,64,128]{3,2,1,0:T(8,128)}, f32[4,32,64,128]{3,2,1,0:T(8,128)}, u32[]{:S(2)}, u32[]{:S(2)}) collective-permute-start(f32[4,32,64,128]{3,2,1,0:T(8,128)} %multiply_add_fusion.14), channel_id=1, source_target_pairs={{0,1},{1,2},{2,3},{3,4},{4,5},{5,6},{6,7},{8,9},{9,10},{10,11},{11... | collective-permute-start | bytes 12582920 | tf_op jit(solution)/shard_map/while/body/eval_jaxpr/ppermute | solution.py:24
  808.7 92.5 %collective-permute-start = (f32[4,32,64,128]{3,2,1,0:T(8,128)}, f32[4,32,64,128]{3,2,1,0:T(8,128)}, u32[]{:S(2)}, u32[]{:S(2)}) collective-permute-start(f32[4,32,64,128]{3,2,1,0:T(8,128)} %multiply_add_fusion.14), channel_id=1, source_target_pairs={{0,1},{1,2},{2,3},{3,4},{4,5},{5,6},{6,7},{8,9},{9,10},{10,11},{11... | collective-permute-start | bytes 12582920 | tf_op jit(solution)/shard_map/while/body/eval_jaxpr/ppermute | solution.py:24
  930.6 263.6 %all-gather.6.cloned.1.call-start = ((), (), s32[]{:S(2)}) async-start(), calls=%async_computation.3 | async-start | bytes 4325376 | tf_op jit(solution)/shard_map/all_gather | solution.py:110
  1131.5 1417.3 %reduce-scatter.4.cloned.1.call-start = ((), (), s32[]{:S(2)}) async-start(), calls=%async_computation.4 | async-start | bytes 18923520 | tf_op jit(solution)/shard_map/reduce_scatter | solution.py:284
  1317.6 94.9 %collective-permute-start.1 = (f32[4,32,64,128]{3,2,1,0:T(8,128)}, f32[4,32,64,128]{3,2,1,0:T(8,128)}, u32[]{:S(2)}, u32[]{:S(2)}) collective-permute-start(f32[4,32,64,128]{3,2,1,0:T(8,128)} %multiply_add_fusion.15), channel_id=1, source_target_pairs={{1,0},{2,1},{3,2},{4,3},{5,4},{6,5},{7,6},{9,8},{10,9},{11,10},{12... | collective-permute-start | bytes 12582920 | tf_op jit(solution)/shard_map/while/body/eval_jaxpr/ppermute | solution.py:24
  1418.4 94.5 %collective-permute-start.1 = (f32[4,32,64,128]{3,2,1,0:T(8,128)}, f32[4,32,64,128]{3,2,1,0:T(8,128)}, u32[]{:S(2)}, u32[]{:S(2)}) collective-permute-start(f32[4,32,64,128]{3,2,1,0:T(8,128)} %multiply_add_fusion.15), channel_id=1, source_target_pairs={{1,0},{2,1},{3,2},{4,3},{5,4},{6,5},{7,6},{9,8},{10,9},{11,10},{12... | collective-permute-start | bytes 12582920 | tf_op jit(solution)/shard_map/while/body/eval_jaxpr/ppermute | solution.py:24
  1518.8 94.1 %collective-permute-start.1 = (f32[4,32,64,128]{3,2,1,0:T(8,128)}, f32[4,32,64,128]{3,2,1,0:T(8,128)}, u32[]{:S(2)}, u32[]{:S(2)}) collective-permute-start(f32[4,32,64,128]{3,2,1,0:T(8,128)} %multiply_add_fusion.15), channel_id=1, source_target_pairs={{1,0},{2,1},{3,2},{4,3},{5,4},{6,5},{7,6},{9,8},{10,9},{11,10},{12... | collective-permute-start | bytes 12582920 | tf_op jit(solution)/shard_map/while/body/eval_jaxpr/ppermute | solution.py:24
  1618.8 93.2 %collective-permute-start.1 = (f32[4,32,64,128]{3,2,1,0:T(8,128)}, f32[4,32,64,128]{3,2,1,0:T(8,128)}, u32[]{:S(2)}, u32[]{:S(2)}) collective-permute-start(f32[4,32,64,128]{3,2,1,0:T(8,128)} %multiply_add_fusion.15), channel_id=1, source_target_pairs={{1,0},{2,1},{3,2},{4,3},{5,4},{6,5},{7,6},{9,8},{10,9},{11,10},{12... | collective-permute-start | bytes 12582920 | tf_op jit(solution)/shard_map/while/body/eval_jaxpr/ppermute | solution.py:24
  1717.8 92.3 %collective-permute-start.1 = (f32[4,32,64,128]{3,2,1,0:T(8,128)}, f32[4,32,64,128]{3,2,1,0:T(8,128)}, u32[]{:S(2)}, u32[]{:S(2)}) collective-permute-start(f32[4,32,64,128]{3,2,1,0:T(8,128)} %multiply_add_fusion.15), channel_id=1, source_target_pairs={{1,0},{2,1},{3,2},{4,3},{5,4},{6,5},{7,6},{9,8},{10,9},{11,10},{12... | collective-permute-start | bytes 12582920 | tf_op jit(solution)/shard_map/while/body/eval_jaxpr/ppermute | solution.py:24
  1816.0 91.3 %collective-permute-start.1 = (f32[4,32,64,128]{3,2,1,0:T(8,128)}, f32[4,32,64,128]{3,2,1,0:T(8,128)}, u32[]{:S(2)}, u32[]{:S(2)}) collective-permute-start(f32[4,32,64,128]{3,2,1,0:T(8,128)} %multiply_add_fusion.15), channel_id=1, source_target_pairs={{1,0},{2,1},{3,2},{4,3},{5,4},{6,5},{7,6},{9,8},{10,9},{11,10},{12... | collective-permute-start | bytes 12582920 | tf_op jit(solution)/shard_map/while/body/eval_jaxpr/ppermute | solution.py:24
  1913.2 90.4 %collective-permute-start.1 = (f32[4,32,64,128]{3,2,1,0:T(8,128)}, f32[4,32,64,128]{3,2,1,0:T(8,128)}, u32[]{:S(2)}, u32[]{:S(2)}) collective-permute-start(f32[4,32,64,128]{3,2,1,0:T(8,128)} %multiply_add_fusion.15), channel_id=1, source_target_pairs={{1,0},{2,1},{3,2},{4,3},{5,4},{6,5},{7,6},{9,8},{10,9},{11,10},{12... | collective-permute-start | bytes 12582920 | tf_op jit(solution)/shard_map/while/body/eval_jaxpr/ppermute | solution.py:24
  2090.1 13.0 collective-permute-start.4
  2188.3 360.5 %copy-start.28 = (f32[32,4384]{1,0:T(8,128)S(1)}, f32[32,4384]{1,0:T(8,128)}, u32[]{:S(2)}) copy-start(f32[32,4384]{1,0:T(8,128)} %param.39) | copy-start | bytes 1683460
  (77 other events, 2875.2 us)
Sparse Core Ops, SparseCore 0:
  11.4 84.2 all-gather.3
  930.7 198.7 reduce-scatter.5
  1132.5 61.6 all-gather.5
  2155.2 393.5 reduce-scatter.3
where the time goes:
time: 2570 us; the launch traced here: 2560 us
  waiting for transfers between devices  1790 us (70%)
  other arithmetic  225 us (9%)
  matrix products  203 us (8%)
  blocking collectives  158 us (6%)
  local copies, waits for them, and re-layouts  92.2 us (4%)
  starting transfers between devices  74.9 us (3%)
    ppermute x17, waiting for transfers between devices, shifted(): lax.ppermute(value, axis, [(source, source + steps) for source in range(f...  1220 us
    reduce_scatter x1, waiting for transfers between devices, local(): lax.psum_scatter(grad_terms[0], ('dp', 'ctx'), scatter_dimension=0, tiled...  304 us
    reduce_scatter x1, waiting for transfers between devices, local(): lax.psum_scatter(grad_terms[1], ('dp', 'ctx'), scatter_dimension=0, tiled...  199 us
    unnamed x2, blocking collectives  90.4 us
    ppermute x17, starting transfers between devices, shifted(): lax.ppermute(value, axis, [(source, source + steps) for source in range(f...  74.7 us
    all_gather x1, blocking collectives, local(): lax.all_gather(owned[2], ('dp', 'ctx'), axis=0, tiled=True)  67.2 us
    all_gather x1, waiting for transfers between devices, local(): lax.all_gather(owned[1], ('dp', 'ctx'), axis=0, tiled=True)  62.6 us
  transfers between devices with their start and end apart: 21, of which 17 were waited for; matrix products, arithmetic and copies ran while one was open for 3% of the time, Pallas kernels for 0%

commit v1 on v0

--- a/solution.py
+++ b/solution.py
@@ -22,6 +22,67 @@
     count = lax.axis_size(axis)
     first, last = (max(0, -steps), min(count, count - steps))
     return lax.ppermute(value, axis, [(source, source + steps) for source in range(first, last)])
+
+
+def split_parts(values):
+    high = values.astype(jnp.bfloat16)
+    rest = values - high.astype(jnp.float32)
+    middle = rest.astype(jnp.bfloat16)
+    low = (rest - middle.astype(jnp.float32)).astype(jnp.bfloat16)
+    return high, middle, low
+
+
+def bit_count(axis):
+    return lax.axis_size(axis).bit_length() - 1
+
+
+def halve(values, axis, bit, dim, sent_type):
+    mine = (lax.axis_index(axis) >> bit) & 1
+    kept = lax.dynamic_index_in_dim(values, mine, dim, keepdims=False)
+    away = lax.dynamic_index_in_dim(values, 1 - mine, dim, keepdims=False).astype(sent_type)
+    count = lax.axis_size(axis)
+    away = lax.ppermute(away, axis, [(place, place ^ (1 << bit)) for place in range(count)])
+    return kept + away.astype(jnp.float32)
+
+
+def sum_to_owner(values, y_first):
+    dp_bits, ctx_bits = bit_count("dp"), bit_count("ctx")
+    x_bits = dp_bits - 1
+    names = [("dp", bit) for bit in reversed(range(dp_bits))]
+    names += [("ctx", bit) for bit in reversed(range(ctx_bits))]
+    rows = values.shape[0] >> len(names)
+    values = values.reshape((2,) * len(names) + (rows, values.shape[1]))
+    y_part = [("dp", bit) for bit in reversed(range(1, dp_bits))]
+    x_part = [("ctx", bit) for bit in reversed(range(x_bits))]
+    z_part = [("ctx", bit) for bit in reversed(range(x_bits, ctx_bits))]
+    order = [("dp", 0)] + (y_part + x_part if y_first else x_part + y_part) + z_part
+    for item in order:
+        sent_type = jnp.float32 if item == ("dp", 0) else jnp.bfloat16
+        values = halve(values, item[0], item[1], names.index(item), sent_type)
+        names.remove(item)
+    return values
+
+
+def sum_small(values, shared):
+    dp_bits, ctx_bits = bit_count("dp"), bit_count("ctx")
+    names = [("dp", bit) for bit in reversed(range(dp_bits))]
+    names += [("ctx", bit) for bit in reversed(range(ctx_bits))]
+    values = values.reshape((2,) * len(names) + (values.shape[1],))
+    for axis, bit in list(names):
+        dim = names.index((axis, bit))
+        mine = (lax.axis_index(axis) >> bit) & 1
+        kept = lax.dynamic_index_in_dim(values, mine, dim, keepdims=False)
+        away = lax.dynamic_index_in_dim(values, 1 - mine, dim, keepdims=False)
+        count = lax.axis_size(axis)
+        away = lax.ppermute(
+            jnp.concatenate([away.reshape(-1), shared]),
+            axis,
+            [(place, place ^ (1 << bit)) for place in range(count)],
+        )
+        values = kept + away[: kept.size].reshape(kept.shape)
+        shared = shared + away[kept.size :]
+        names.remove((axis, bit))
+    return values, shared
 
 
 def inverse_rms(values):
@@ -99,20 +160,25 @@
     head_first,
     head_second,
 ):
-    owned = (
-        w_in.astype(jnp.bfloat16),
-        w_out.astype(jnp.bfloat16),
-        conv.astype(jnp.bfloat16),
-        gains.astype(jnp.bfloat16),
-    )
-    input_weight, output_weight, conv_weight, gain_vector = (
-        lax.all_gather(owned[0], ("dp", "ctx"), axis=0, tiled=True),
-        lax.all_gather(owned[1], ("dp", "ctx"), axis=0, tiled=True),
-        lax.all_gather(owned[2], ("dp", "ctx"), axis=0, tiled=True),
-        lax.all_gather(owned[3], ("dp", "ctx"), axis=0, tiled=True),
-    )
+    inner_width = w_out.shape[0] * lax.axis_size(("dp", "ctx"))
+    own_rows = w_in.shape[0]
+    small = jnp.concatenate([conv.reshape(-1), gains])
+    spare = -(w_in.shape[1] - inner_width) % 128
+    small = jnp.pad(small, (0, own_rows * spare - small.shape[0])).reshape(own_rows, spare)
+    first_send = jnp.concatenate([w_in[:, inner_width:], small], axis=1).astype(jnp.bfloat16)
+    first_weights = lax.all_gather(first_send, ("dp", "ctx"), axis=0, tiled=True)
+    second_send = jnp.concatenate(
+        [w_in[:, :inner_width], w_out.reshape(own_rows, -1)], axis=1
+    ).astype(jnp.bfloat16)
+    first_weights, second_send = lax.optimization_barrier((first_weights, second_send))
+    second_weights = lax.all_gather(second_send, ("dp", "ctx"), axis=0, tiled=True)
+    gate_weight = second_weights[:, :inner_width]
+    output_weight = second_weights[:, inner_width:].reshape(inner_width, -1)
+    mixer_weight = first_weights[:, : w_in.shape[1] - inner_width]
+    small = first_weights[:, w_in.shape[1] - inner_width :].reshape(-1, own_rows * spare)
+    conv_weight = small[:, : conv.size].reshape(-1, conv.shape[1])
+    gain_vector = small[:, conv.size : conv.size + gains.size].reshape(-1)
     seq_count, length, model_width = tokens.shape
-    inner_width = output_weight.shape[0]
     channels = conv_weight.shape[0]
     kernel_taps = conv_weight.shape[1] - 1
     state_dim = (channels - inner_width) // 2
@@ -126,11 +192,13 @@
     unit_in = input_float * scale_in
     normalized_rows = (unit_in * gain_in).astype(jnp.bfloat16)
     projected_rows = jnp.einsum(
-        "aok,ku->aou", normalized_rows, input_weight, preferred_element_type=jnp.float32
-    )
-    gate_raw = projected_rows[:, :, :inner_width]
-    conv_in = projected_rows[:, :, inner_width : inner_width + channels].astype(jnp.bfloat16)
-    step_raw = projected_rows[:, :, inner_width + channels :]
+        "aok,ku->aou", normalized_rows, mixer_weight, preferred_element_type=jnp.float32
+    )
+    conv_in = projected_rows[:, :, :channels].astype(jnp.bfloat16)
+    step_raw = projected_rows[:, :, channels:]
+    gate_raw = jnp.einsum(
+        "aok,ku->aou", normalized_rows, gate_weight, preferred_element_type=jnp.float32
+    )
     rim_x, rim_seg = shifted(
         (conv_in[:, length - kernel_taps + 1 :], segments[:, length - kernel_taps + 1 :]), "ctx", 1
     )
@@ -160,19 +228,43 @@
     fall_off = jnp.exp(decay_sum[:, length - 1 :] - decay_sum) * tail_doc
     end_weight = fall_off * step_size
     scaled = (end_weight[..., None] * x_heads).astype(jnp.bfloat16)
-    local_state = jnp.einsum("slhp,sln->shpn", scaled, b_state, preferred_element_type=jnp.float32)
+    scaled = scaled.reshape(seq_count, length, inner_width)
+    local_state = jnp.einsum("sln,slc->snc", b_state, scaled, preferred_element_type=jnp.float32)
     link_doc = (segments == rim_seg[:, kernel_taps - 2 :]).astype(jnp.float32)[:, :, None]
     entry_decay = jnp.exp(decay_sum) * link_doc
     passing = entry_decay[:, length - 1]
 
-    def forward_hop(hop_index, carried):
-        return shifted(passing[:, :, None, None] * carried + local_state, "ctx", 1)
-
-    incoming = lax.fori_loop(0, lax.axis_size("ctx") - 1, forward_hop, jnp.zeros_like(local_state))
-    incoming_low = incoming.astype(jnp.bfloat16)
+    ctx_count = lax.axis_size("ctx")
+    groups = ctx_count // seq_count
+    lanes = inner_width // groups
+
+    def to_owners(states, extra):
+        parts = list(split_parts(extra)) + [jnp.zeros_like(extra, jnp.bfloat16)] * 13
+        packed = jnp.concatenate([states.astype(jnp.bfloat16), jnp.stack(parts, axis=1)], axis=1)
+        packed = packed.reshape(seq_count, -1, groups, lanes).transpose(0, 2, 1, 3)
+        packed = packed.reshape(ctx_count, -1, lanes)
+        return lax.all_to_all(packed, "ctx", 0, 0, tiled=True)
+
+    def to_blocks(states, extra):
+        parts = list(split_parts(extra)) + [jnp.zeros_like(extra, jnp.bfloat16)] * 13
+        packed = jnp.concatenate([states.astype(jnp.bfloat16), jnp.stack(parts, axis=1)], axis=1)
+        packed = lax.all_to_all(packed, "ctx", 0, 0, tiled=True)
+        packed = packed.reshape(seq_count, groups, -1, lanes).transpose(0, 2, 1, 3)
+        return packed.reshape(seq_count, -1, inner_width)
+
+    received = to_owners(local_state, jnp.repeat(passing, head_dim, axis=1))
+    received = received.astype(jnp.float32)
+    owner_passing = jnp.sum(received[:, state_dim : state_dim + 3], axis=1)
+    carried = jnp.zeros_like(received[0, :state_dim])
+    owner_incoming = []
+    for block in range(ctx_count):
+        owner_incoming.append(carried)
+        carried = owner_passing[block] * carried + received[block, :state_dim]
+    owner_incoming = jnp.stack(owner_incoming)
+    incoming_low = to_blocks(owner_incoming, jnp.zeros_like(owner_passing))[:, :state_dim]
     from_before = jnp.einsum(
-        "sln,shpn->slhp", c_state, incoming_low, preferred_element_type=jnp.float32
-    )
+        "sln,snc->slc", c_state, incoming_low, preferred_element_type=jnp.float32
+    ).reshape(seq_count, length, heads_count, head_dim)
     ssd_out = within_block + heads[1][:, None] * x_heads + entry_decay[..., None] * from_before
     ssd_flat = ssd_out.reshape(seq_count, length, inner_width)
     gate_silu = jax.nn.silu(gate_raw)
@@ -204,26 +296,34 @@
     grad_skip = jnp.einsum("slhp,slhp->h", grad_ssd, x_heads, preferred_element_type=jnp.float32)
     grad_entry = jnp.sum(grad_ssd * from_before, axis=3)
     grad_before = (grad_ssd * entry_decay[..., None]).astype(jnp.bfloat16)
+    grad_before = grad_before.reshape(seq_count, length, inner_width)
     grad_c_outer = jnp.einsum(
-        "slhp,shpn->sln", grad_before, incoming_low, preferred_element_type=jnp.float32
+        "slc,snc->sln", grad_before, incoming_low, preferred_element_type=jnp.float32
     )
     grad_incoming = jnp.einsum(
-        "slhp,sln->shpn", grad_before, c_state, preferred_element_type=jnp.float32
-    )
-
-    def backward_hop(hop_index, carried):
-        return shifted(passing[:, :, None, None] * carried + grad_incoming, "ctx", -1)
-
-    grad_leaving = lax.fori_loop(
-        0, lax.axis_size("ctx") - 1, backward_hop, jnp.zeros_like(grad_incoming)
-    )
-    grad_passing = jnp.sum(grad_leaving * incoming, axis=(2, 3))
-    grad_local = grad_leaving.astype(jnp.bfloat16)
+        "sln,slc->snc", c_state, grad_before, preferred_element_type=jnp.float32
+    )
+    received = to_owners(grad_incoming, jnp.zeros((seq_count, inner_width), jnp.float32))
+    received = received[:, :state_dim].astype(jnp.float32)
+    carried = jnp.zeros_like(received[0])
+    owner_leaving = []
+    for block in reversed(range(ctx_count)):
+        owner_leaving.append(carried)
+        carried = owner_passing[block] * carried + received[block]
+    owner_leaving = jnp.stack(owner_leaving[::-1])
+    returned = to_blocks(owner_leaving, jnp.sum(owner_leaving * owner_incoming, axis=1))
+    grad_local = returned[:, :state_dim]
+    grad_passing = jnp.sum(
+        returned[:, state_dim : state_dim + 3]
+        .astype(jnp.float32)
+        .reshape(seq_count, 3, heads_count, head_dim),
+        axis=(1, 3),
+    )
     grad_scaled = jnp.einsum(
-        "shpn,sln->slhp", grad_local, b_state, preferred_element_type=jnp.float32
-    )
+        "snc,sln->slc", grad_local, b_state, preferred_element_type=jnp.float32
+    ).reshape(seq_count, length, heads_count, head_dim)
     grad_b_state = jnp.einsum(
-        "slhp,shpn->sln", scaled, grad_local, preferred_element_type=jnp.float32
+        "slc,snc->sln", scaled, grad_local, preferred_element_type=jnp.float32
     )
     grad_end = jnp.sum(grad_scaled * x_heads, axis=3)
     inner_x, inner_b, inner_c, inner_step, inner_decay = lax.map(
@@ -262,14 +362,18 @@
         jnp.float32
     )
     grad_conv_in = grad_wide[:, kernel_taps - 1 :].at[:, length - kernel_taps + 1 :].add(rim_back)
-    projection_gradient = jnp.concatenate([grad_gate, grad_conv_in, grad_step_raw], axis=2).astype(
-        jnp.bfloat16
-    )
-    grad_in_weight = jnp.einsum(
-        "nay,nag->yg", normalized_rows, projection_gradient, preferred_element_type=jnp.float32
+    grad_gate = grad_gate.astype(jnp.bfloat16)
+    grad_mixer = jnp.concatenate([grad_conv_in, grad_step_raw], axis=2).astype(jnp.bfloat16)
+    grad_gate_weight = jnp.einsum(
+        "nay,nag->yg", normalized_rows, grad_gate, preferred_element_type=jnp.float32
+    )
+    grad_mixer_weight = jnp.einsum(
+        "nay,nag->yg", normalized_rows, grad_mixer, preferred_element_type=jnp.float32
     )
     grad_normed = jnp.einsum(
-        "hou,qu->hoq", projection_gradient, input_weight, preferred_element_type=jnp.float32
+        "hou,qu->hoq", grad_gate, gate_weight, preferred_element_type=jnp.float32
+    ) + jnp.einsum(
+        "hou,qu->hoq", grad_mixer, mixer_weight, preferred_element_type=jnp.float32
     )
     grad_gain_in = jnp.sum(grad_normed * unit_in, axis=(0, 1))
     grad_unit_in = grad_normed * gain_in
@@ -279,14 +383,25 @@
     grad_conv = jnp.stack(grad_taps + [grad_bias], axis=1)
     grad_gains = jnp.concatenate([grad_gain_in, grad_gain_out])
     grad_heads = jnp.stack([grad_log_rate, grad_skip, grad_step_bias])
-    grad_terms = (grad_in_weight, grad_out_weight, grad_conv, grad_gains)
+    devices = lax.axis_size(("dp", "ctx"))
+    small_sum, head_grad = sum_small(
+        jnp.concatenate(
+            [grad_conv.reshape(devices, -1), grad_gains.reshape(devices, -1)], axis=1
+        ),
+        grad_heads.reshape(-1),
+    )
+    middle = grad_mixer_weight.shape[1] // 256 * 128
+    gate_sum = sum_to_owner(grad_gate_weight, True)
+    out_sum = sum_to_owner(grad_out_weight.reshape(devices * own_rows, -1), False)
+    left_sum = sum_to_owner(grad_mixer_weight[:, :middle], True)
+    right_sum = sum_to_owner(grad_mixer_weight[:, middle:], False)
     owned_grads = (
-        lax.psum_scatter(grad_terms[0], ("dp", "ctx"), scatter_dimension=0, tiled=True),
-        lax.psum_scatter(grad_terms[1], ("dp", "ctx"), scatter_dimension=0, tiled=True),
-        lax.psum_scatter(grad_terms[2], ("dp", "ctx"), scatter_dimension=0, tiled=True),
-        lax.psum_scatter(grad_terms[3], ("dp", "ctx"), scatter_dimension=0, tiled=True),
-    )
-    head_grad = lax.psum(grad_heads, ("dp", "ctx"))
+        jnp.concatenate([gate_sum, left_sum, right_sum], axis=1),
+        out_sum.reshape(w_out.shape),
+        small_sum[: conv.size].reshape(conv.shape),
+        small_sum[conv.size :],
+    )
+    head_grad = head_grad.reshape(heads.shape)
     in_new = adamw(w_in, owned_grads[0], in_first, in_second, RATE_IN)
     out_new = adamw(w_out, owned_grads[1], out_first, out_second, RATE_OUT)
     conv_new = adamw(conv, owned_grads[2], conv_first, conv_second, RATE_CONV)

time: 2570 us -> 914 us (0.36)
  waiting for transfers between devices: 1790 us -> 211 us
  blocking collectives: 158 us -> 0 us
  local copies, waits for them, and re-layouts: 92.2 us -> 247 us
  other arithmetic: 225 us -> 174 us
    ppermute x17 -> x3, waiting for transfers between devices: 1220 us -> 0.01 us  [shifted(): lax.ppermute(value, axis, [(source, source + steps) for source in range(f...]
    reduce_scatter x2 -> x0, waiting for transfers between devices: 503 us -> none  [the longest x1 304 us: local(): lax.psum_scatter(grad_terms[0], ('dp', 'ctx'), scatter_dimension=0, tiled...]
    ppermute x0 -> x25, waiting for transfers between devices: none -> 96.7 us  [the longest x20 95.1 us: halve(): lax.ppermute(away, axis, [(place, place ^ 1 << bit) for place in range(co...]
    unnamed x2 -> x0, blocking collectives: 90.4 us -> none
    all_gather x1 -> x0, blocking collectives: 67.2 us -> none  [local(): lax.all_gather(owned[2], ('dp', 'ctx'), axis=0, tiled=True)]
    ppermute x17 -> x3, starting transfers between devices: 74.7 us -> 10.3 us  [shifted(): lax.ppermute(value, axis, [(source, source + steps) for source in range(f...]
    all_to_all x0 -> x4, waiting for transfers between devices: none -> 60.7 us  [the longest x2 31.7 us: to_owners(): return lax.all_to_all(packed, 'ctx', 0, 0, tiled=True)]
    add x14 -> x27, other arithmetic: 83 us -> 38.9 us  [the longest x20 18.5 us: halve(): return kept + away.astype(jnp.float32)]
  transfers between devices with their start and end apart: 21 -> 34, of which waited for: 17 -> 18; matrix products, arithmetic and copies ran while one was open for 3% -> 41% of each run, Pallas kernels for 0% -> 0%
where the time goes in v1:
time: 914 us; the launch traced here: 905 us
  local copies, waits for them, and re-layouts  247 us (27%)
  waiting for transfers between devices  211 us (23%)
  matrix products  195 us (21%)
  other arithmetic  174 us (19%)
  starting transfers between devices  59.6 us (7%)
  between operations  16.5 us (2%)
    ppermute x20, waiting for transfers between devices, halve(): lax.ppermute(away, axis, [(place, place ^ 1 << bit) for place in range(co...  95.1 us
    all_gather x1, waiting for transfers between devices, local(): lax.all_gather(first_send, ('dp', 'ctx'), axis=0, tiled=True)  53.9 us
    all_to_all x2, waiting for transfers between devices, to_owners(): return lax.all_to_all(packed, 'ctx', 0, 0, tiled=True)  31.7 us
    dot_general x4, matrix products, block_backward(): jnp.einsum('thp,shp->hts', grad_ssd, x_heads, preferred_element_type=jnp....  30.4 us
    all_to_all x2, waiting for transfers between devices, to_blocks(): packed = lax.all_to_all(packed, 'ctx', 0, 0, tiled=True)  29 us
    scatter-add x1, local copies, waits for them, and re-layouts, local(): grad_wide[:, kernel_taps - 1:].at[:, length - kernel_taps + 1:]  26.6 us
    ppermute x20, starting transfers between devices, halve(): lax.ppermute(away, axis, [(place, place ^ 1 << bit) for place in range(co...  24 us
    unnamed x243, local copies, waits for them, and re-layouts  20.7 us
  transfers between devices with their start and end apart: 34, of which 18 were waited for; matrix products, arithmetic and copies ran while one was open for 41% of the time, Pallas kernels for 0%

profile of v1, /device:TPU:0, one launch (start us, length us, event | category | flops | bytes accessed | tf_op | source)
XLA Modules:
  0.0 904.6 jit_solution(12939634392011915919)
XLA Ops:
  25.1 53.9 %all-gather.3.cloned.1.call-done = bf16[1024,2432]{1,0:T(8,128)(2,1)} async-done(((bf16[32,2432]{1,0:T(8,128)(2,1)}), bf16[1024,2432]{1,0:T(8,128)(2,1)}) %all-gather.3.cloned.1.call-update) | async-done | bytes 4980752 | tf_op jit(solution)/shard_map/all_gather | solution.py:169
  88.6 10.2 %fusion.196 = (bf16[4,256,2336]{1,2,0:T(8,128)(2,1)S(1)}, f32[4,256,2336]{1,2,0:T(8,128)}) fusion(bf16[1024,2432]{0,1:T(8,128)(2,1)} %copy.365, bf16[4,256,1024]{2,1,0:T(8,128)(2,1)S(1)} %copy-done.24, f32[1024]{0:T(1024)S(1)} %slice.458, f32[4,256]{1,0:T(4,128)S(1)} %add_rsqrt_fusion.1), kind=kOutput, calls=%fused_computation.410 | convolution fusion | flops 4905533440 | bytes 21241856 | tf_op jit(solution)/shard_map/aok,ku->aou/dot_general | solution.py:194
  124.7 16.9 %multiply_convert_fusion.4 = (bf16[4,256,2304]{1,2,0:T(8,128)(2,1)S(1)}, f32[4,256,2304]{1,2,0:T(8,128)}) fusion(bf16[4,256,2304]{1,2,0:T(8,128)(2,1)} %slice.461, f32[2304]{0:T(1024)S(1)} %get-tuple-element.393, f32[4,256]{1,0:T(4,128)} %get-tuple-element.518, bf16[4,3,2304]{1,2,0:T(8,128)(2,1)S(1)} %copy.367, f32[2304]{0:T(1024)} %get-tuple-element.394, ...), kind=kLoop, calls=%fused_computation.100 | loop fusion | flops 68419584 | bytes 18988032 | tf_op jit(solution)/shard_map/convert_element_type | solution.py:217
  186.0 31.7 %all-to-all-done = bf16[8,144,1024]{2,1,0:T(8,128)(2,1)S(1)} async-done(((bf16[8,144,1024]{2,1,0:T(8,128)(2,1)}), bf16[8,144,1024]{2,1,0:T(8,128)(2,1)S(1)}, u32[]{:S(2)}, u32[]{:S(2)}) %all-to-all-start) | async-done | bytes 2359328 | tf_op jit(solution)/shard_map/all_to_all | solution.py:246
  233.2 20.7 %while.30 = (s32[]{:T(128)}, f32[4,256,32,64]{1,3,2,0:T(8,128)}, bf16[4,256,32,64]{1,3,2,0:T(8,128)(2,1)}, bf16[4,256,128]{2,1,0:T(8,128)(2,1)S(1)}, bf16[4,256,...) while((s32[]{:T(128)}, f32[4,256,32,64]{1,3,2,0:T(8,128)}, ...), condition=%wide.region_4.5_spmd, body=%wide.region_3.4_spmd.sunk | while | flops 297992192 | bytes 4166765 | solution.py:224
  253.9 29.0 %all-to-all-done.1 = bf16[8,144,1024]{2,1,0:T(8,128)(2,1)S(1)} async-done(((bf16[8,144,1024]{2,1,0:T(8,128)(2,1)}), bf16[8,144,1024]{2,1,0:T(8,128)(2,1)S(1)}, u32[]{:S(2)}, u32[]{:S(2)}) %all-to-all-start.1) | async-done | bytes 2359328 | tf_op jit(solution)/shard_map/all_to_all | solution.py:251
  295.4 10.0 %fusion.71 = f32[4,256,32,64]{1,3,2,0:T(8,128)} fusion(f32[4,256,32,64]{1,3,2,0:T(8,128)} %get-tuple-element.157, bf16[4,256,32,64]{1,3,2,0:T(8,128)(2,1)S(1)} %copy-done.7, f32[4,256,32,64]{1,3,2,0:T(8,128)S(1)} %bitcast.356, f32[4,256,32]{1,2,0:T(8,128)S(1)} %copy.378, f32[32]{0:T(128)S(1)} %copy-done.98), kind=kLoop, calls=%fused_computation.108 | loop fusion | flops 10485760 | bytes 29491328 | tf_op jit(solution)/shard_map/add | solution.py:268
  326.2 11.9 %multiply_reduce_fusion.3 = (f32[4,256]{1,0:T(4,128)S(1)}, f32[4,256,2048]{2,1,0:T(8,128)S(1)}, f32[4,256,2048]{2,1,0:T(8,128)}) fusion(f32[4,256,2048]{2,1,0:T(8,128)} %copy.385, bf16[1024,4096]{1,0:T(8,128)(2,1)} %all-gather.5.cloned.1.call-done, bf16[4,256,1024]{2,1,0:T(8,128)(2,1)S(1)} %copy-done.25, f32[1024]{0:T(1024)S(1)} %copy-done.88, ...), kind=kOutput, calls=%fused_computation.126 | convolution fusion | flops 4313840640 | bytes 31469568 | tf_op jit(solution)/shard_map/aok,ku->aou/dot_general | solution.py:199
  338.1 14.9 %fusion.77 = (f32[2048]{0:T(1024)}, f32[4,256]{1,0:T(4,128)S(1)}, f32[2048,4,256]{0,2,1:T(8,128)}) fusion(f32[4,256,2048]{2,1,0:T(8,128)S(1)} %get-tuple-element.462, f32[4,256]{1,0:T(4,128)S(1)} %add_rsqrt_fusion, f32[2048]{0:T(1024)S(1)} %copy-done.81, bf16[2048,1024,1]{1,0,2:T(8,128)(2,1)} %reshape.870, bf16[4,256,1024]{2,1,0:T(8,128)(2,1)} %param.27), kind=kOutput, calls=%fused_computation.117 | convolution fusion | flops 4307547136 | bytes 23093248 | tf_op jit(solution)/shard_map/pjy,hy->pjh/dot_general | solution.py:282
  353.1 13.2 %multiply_convert_fusion.7 = (bf16[4,256,2048]{2,1,0:T(8,128)(2,1)}, bf16[4,256,2048]{2,1,0:T(8,128)(2,1)}) fusion(f32[4,256,2048]{2,1,0:T(8,128)} %get-tuple-element.531, f32[4,256,2048]{2,1,0:T(8,128)S(1)} %bitcast.367, f32[4,256]{1,0:T(4,128)S(1)} %broadcast_multiply_fusion.2, f32[4,256,2048]{2,1,0:T(8,128)} %copy-done.23, f32[2048]{0:T(1024)S(1)} %copy-done.81, ...), kind=kLoop, calls=%fused_computation.122 | loop fusion | flops 37748736 | bytes 41959424 | tf_op jit(solution)/shard_map/convert_element_type | solution.py:365
  389.0 58.8 %while.31 = (s32[]{:T(128)}, f32[4,256,32,64]{1,3,2,0:T(8,128)}, f32[4,256,128]{1,2,0:T(8,128)}, f32[4,256,128]{1,2,0:T(8,128)}, f32[4,256,32]{1,2,0:T(8,128)S(1...) while((s32[]{:T(128)}, f32[4,256,32,64]{1,3,2,0:T(8,128)}, ...), condition=%wide.region_13.14_spmd, body=%wide.region_8.13_spmd.sunk | while | flops 629260288 | bytes 7741597 | solution.py:329
  447.9 9.3 %fusion.118 = f32[1024,2048,1]{1,0,2:T(8,128)} fusion(bf16[4,256,2048]{2,1,0:T(8,128)(2,1)} %get-tuple-element.477, bf16[4,256,1024]{2,1,0:T(8,128)(2,1)S(1)} %copy-done.26, f32[1024]{0:T(1024)S(1)} %copy-done.88, f32[4,256]{1,0:T(4,128)S(1)} %copy-done.85), kind=kOutput, calls=%fused_computation.215 | convolution fusion | flops 4299161600 | bytes 14688256 | tf_op jit(solution)/shard_map/nay,nag->yg/dot_general | solution.py:367
  473.3 10.3 %reshape_reshape.3 = f32[2,2,2,2,2,32,2048]{6,5,4,3,2,1,0:T(8,128)} reshape(f32[2048,1024]{1,0:T(8,128)} %convolution_bitcast_fusion.3) | data formatting | bytes 16777216 | tf_op jit(solution)/shard_map/reshape;reshape | solution.py:54
  504.6 10.5 %fusion.93 = bf16[4,256,1024]{2,1,0:T(8,128)(2,1)} fusion(bf16[4,256,1024]{2,1,0:T(8,128)(2,1)S(1)} %copy-done.27, bf16[2048,1024,1]{1,0,2:T(8,128)(2,1)} %reshape.870, f32[4,256,2048]{2,1,0:T(8,128)} %copy-done.23, f32[2048]{0:T(1024)S(1)} %copy-done.81, f32[4,256]{1,0:T(4,128)S(1)} %add_rsqrt_fusion), kind=kOutput, calls=%fused_computation.155 | convolution fusion | flops 4304404480 | bytes 16789504 | tf_op jit(solution)/shard_map/exp,pk->exk/dot_general | solution.py:277
  544.3 15.9 %collective-permute-done.19 = bf16[2,2,2,32,2048]{4,3,2,1,0:T(8,128)(2,1)} collective-permute-done((bf16[2,2,2,32,2048]{4,3,2,1,0:T(8,128)(2,1)S(1)}, bf16[2,2,2,32,2048]{4,3,2,1,0:T(8,128)(2,1)}, u32[]{:S(2)}, u32[]{:S(2)}) %collective-permute-start.19) | collective-permute-done | bytes 1048608 | tf_op jit(solution)/shard_map/ppermute | solution.py:44
  587.5 28.9 %collective-permute-done.21 = bf16[2,32,2048]{2,1,0:T(8,128)(2,1)S(1)} collective-permute-done((bf16[2,32,2048]{2,1,0:T(8,128)(2,1)S(1)}, bf16[2,32,2048]{2,1,0:T(8,128)(2,1)S(1)}, u32[]{:S(2)}, u32[]{:S(2)}) %collective-permute-start.21) | collective-permute-done | bytes 262176 | tf_op jit(solution)/shard_map/ppermute | solution.py:44
  659.0 10.2 %fusion.74 = f32[4,256,32,64]{1,3,2,0:T(8,128)} fusion(f32[4,256,32,64]{1,3,2,0:T(8,128)} %get-tuple-element.159, bf16[4,256,32,64]{1,3,2,0:T(8,128)(2,1)S(1)} %copy-done.3, f32[4,256,32,64]{1,3,2,0:T(8,128)} %bitcast.371, f32[4,256,32]{1,2,0:T(8,128)S(1)} %copy-done.42, f32[32]{0:T(128)S(1)} %copy-done.99), kind=kLoop, calls=%fused_computation.111 | loop fusion | flops 10485760 | bytes 29491328 | tf_op jit(solution)/shard_map/add | solution.py:342
  669.3 20.7 %fusion.68 = (f32[2304]{0:T(1024)}, f32[2304]{0:T(1024)}, f32[2304]{0:T(1024)}, f32[2304]{0:T(1024)S(1)}, f32[2304]{0:T(1024)}, /*index=5*/f32[4,256,2304]{1,2,0:T(8,128)}) fusion(f32[4,256]{1,0:T(4,128)S(1)} %copy-done.60, bf16[4,256,2304]{1,2,0:T(8,128)(2,1)S(1)} %bitcast.363, bf16[4,3,2304]{1,2,0:T(8,128)(2,1)} %copy-done.10, f32[4,256]{1,0:T(4,128)S(1)} %copy-done.59, ...), kind=kLoop, calls=%fused_computation.97 | loop fusion | flops 82563840 | bytes 37862400 | tf_op jit(solution)/shard_map/reduce_sum | solution.py:357
  690.0 12.9 %multiply_multiply_fusion.3 = (f32[4,256,2304]{1,2,0:T(8,128)S(1)}, f32[4,256,2304]{1,2,0:T(8,128)}, f32[4,256,2304]{1,2,0:T(8,128)}, f32[4,256,2304]{1,2,0:T(8,128)}) fusion(f32[4,256,2304]{1,2,0:T(8,128)} %get-tuple-element.448, f32[4,256]{1,0:T(4,128)S(1)} %copy-done.59, f32[2304]{0:T(1024)S(1)} %copy-done.57, f32[2304]{0:T(1024)S(1)} %copy-done.54, ...), kind=kLoop, calls=%fused_computation.104 | loop fusion | flops 16515072 | bytes 47235072 | tf_op jit(solution)/shard_map/mul | solution.py:359
  703.0 14.8 %pad_add_fusion = f32[4,259,2304]{1,2,0:T(8,128)S(1)} fusion(f32[4,256,2304]{1,2,0:T(8,128)} %get-tuple-element.480, f32[4,256,2304]{1,2,0:T(8,128)} %get-tuple-element.481, f32[4,256,2304]{1,2,0:T(8,128)} %get-tuple-element.482, f32[4,256,2304]{1,2,0:T(8,128)S(1)} %get-tuple-element.479), kind=kLoop, calls=%fused_computation.75 | loop fusion | flops 7160832 | bytes 47296512 | tf_op jit(solution)/shard_map/add | solution.py:358
  747.5 26.6 %scatter-add.6 = bf16[4,256,2304]{1,2,0:T(8,128)(2,1)} dynamic-update-slice(bf16[4,256,2304]{1,2,0:T(8,128)(2,1)} %slice.512, bf16[4,3,2304]{1,2,0:T(8,128)(2,1)S(1)} %slice_add_fusion, s32[]{:T(128)} %constant.338.clone.1, s32[]{:T(128)} %constant.345.clone.1, s32[]{:T(128)} %constant.338.clone.1) | dynamic-update-slice | bytes 110596 | tf_op jit(solution)/shard_map/scatter-add | solution.py:364
  774.1 9.1 %fusion.94 = f32[4,256,1024]{2,1,0:T(8,128)S(1)} fusion(bf16[1024,2432]{0,1:T(8,128)(2,1)} %copy.365, bf16[4,256,32]{1,2,0:T(8,128)(2,1)S(1)} %copy.413, bf16[4,256,2304]{1,2,0:T(8,128)(2,1)} %scatter-add.6), kind=kOutput, calls=%fused_computation.162 | convolution fusion | flops 4908515328 | bytes 13762560 | tf_op jit(solution)/shard_map/hou,qu->hoq/dot_general | solution.py:375
  783.2 9.0 fusion.91
  856.2 9.4 %collective-permute-done.9 = bf16[2,2,2,32,1152]{4,3,2,1,0:T(8,128)(2,1)S(1)} collective-permute-done((bf16[2,2,2,32,1152]{4,3,2,1,0:T(8,128)(2,1)S(1)}, bf16[2,2,2,32,1152]{4,3,2,1,0:T(8,128)(2,1)S(1)}, u32[]{:S(2)}, u32[]{:S(2)}) %collective-permute-start.9) | collective-permute-done | bytes 589856 | tf_op jit(solution)/shard_map/ppermute | solution.py:44
  (623 shorter events, 508.4 us)
Async XLA Ops:
  7.2 71.7 %all-gather.3.cloned.1.call-start = ((), (), s32[]{:S(2)}) async-start(), calls=%async_computation.4 | async-start | bytes 5136384 | tf_op jit(solution)/shard_map/all_gather | solution.py:169
  10.9 303.2 %all-gather.5.cloned.1.call-start = ((), (), s32[]{:S(2)}) async-start(), calls=%async_computation.5 | async-start | bytes 8650752 | tf_op jit(solution)/shard_map/all_gather | solution.py:174
  103.4 19.3 %collective-permute-start = (bf16[4,3,2304]{2,0,1:T(4,128)(2,1)}, bf16[4,3,2304]{2,0,1:T(4,128)(2,1)}, u32[]{:S(2)}, u32[]{:S(2)}) collective-permute-start(bf16[4,3,2304]{2,0,1:T(4,128)(2,1)} %copy.366), channel_id=1, source_target_pairs={{0,1},{1,2},{2,3},{3,4},{4,5},{5,6},{6,7},{8,9},{9,10},{10,11},{11... | collective-permute-start | bytes 165896 | tf_op jit(solution)/shard_map/ppermute | solution.py:24
  159.8 57.9 %all-to-all-start = ((bf16[8,144,1024]{2,1,0:T(8,128)(2,1)}), bf16[8,144,1024]{2,1,0:T(8,128)(2,1)S(1)}, u32[]{:S(2)}, u32[]{:S(2)}) async-start(bf16[8,144,1024]{2,1,0:T(8,128)(2,1)} %bitcast.380), calls=%async_computation | async-start | bytes 4718592 | tf_op jit(solution)/shard_map/all_to_all | solution.py:246
  224.7 58.2 %all-to-all-start.1 = ((bf16[8,144,1024]{2,1,0:T(8,128)(2,1)}), bf16[8,144,1024]{2,1,0:T(8,128)(2,1)S(1)}, u32[]{:S(2)}, u32[]{:S(2)}) async-start(bf16[8,144,1024]{2,1,0:T(8,128)(2,1)} %concatenate.99), calls=%async_computation.1 | async-start | bytes 4718592 | tf_op jit(solution)/shard_map/all_to_all | solution.py:251
  380.0 135.2 %all-to-all-start.2 = ((bf16[8,144,1024]{2,1,0:T(8,128)(2,1)}), bf16[8,144,1024]{2,1,0:T(8,128)(2,1)}, u32[]{:S(2)}, u32[]{:S(2)}) async-start(bf16[8,144,1024]{2,1,0:T(8,128)(2,1)} %bitcast.62), calls=%async_computation.2 | async-start | bytes 4718592 | tf_op jit(solution)/shard_map/all_to_all | solution.py:246
  465.8 59.2 %collective-permute-start.3 = (f32[2,2,2,2,32,2048]{5,4,2,1,3,0:T(8,128)}, f32[2,2,2,2,32,2048]{5,4,2,1,3,0:T(8,128)}, u32[]{:S(2)}, u32[]{:S(2)}) collective-permute-start(f32[2,2,2,2,32,2048]{5,4,2,1,3,0:T(8,128)} %bitcast.304), channel_id=1, source_target_pairs={{0,8},{8,0},{16,24},{24,16},{1,9},{9,1},{17,25},{25,17},{2,10},{10... | collective-permute-start | bytes 12582920 | tf_op jit(solution)/shard_map/ppermute | solution.py:44
  488.5 29.8 %collective-permute-start.18 = (f32[2,2,2,2,32,2048]{5,4,3,2,1,0:T(8,128)}, f32[2,2,2,2,32,2048]{5,4,3,2,1,0:T(8,128)}, u32[]{:S(2)}, u32[]{:S(2)}) collective-permute-start(f32[2,2,2,2,32,2048]{5,4,3,2,1,0:T(8,128)} %dynamic-slice_bitcast_fusion.4), channel_id=1, source_target_pairs={{0,8},{8,0},{16,24},{24,16},{1,9},{9,1},{17,25},{25,17},{2,10},{10... | collective-permute-start | bytes 12582920 | tf_op jit(solution)/shard_map/ppermute | solution.py:44
  523.0 37.2 %collective-permute-start.19 = (bf16[2,2,2,32,2048]{4,3,2,1,0:T(8,128)(2,1)S(1)}, bf16[2,2,2,32,2048]{4,3,2,1,0:T(8,128)(2,1)}, u32[]{:S(2)}, u32[]{:S(2)}) collective-permute-start(bf16[2,2,2,32,2048]{4,3,2,1,0:T(8,128)(2,1)S(1)} %fusion.115), channel_id=1, source_target_pairs={{0,1},{1,0},{2,3},{3,2},{4,5},{5,4},{6,7},{7,6},{8,9},{9,8},{10,11... | collective-permute-start | bytes 3145736 | tf_op jit(solution)/shard_map/ppermute | solution.py:44
  529.4 33.2 %collective-permute-start.4 = (bf16[2,2,2,32,2048]{4,3,1,0,2:T(8,128)(2,1)}, bf16[2,2,2,32,2048]{4,3,1,0,2:T(8,128)(2,1)}, u32[]{:S(2)}, u32[]{:S(2)}) collective-permute-start(bf16[2,2,2,32,2048]{4,3,1,0,2:T(8,128)(2,1)} %fusion.114), channel_id=1, source_target_pairs={{0,16},{8,24},{16,0},{24,8},{1,17},{9,25},{17,1},{25,9},{2,18},{10... | collective-permute-start | bytes 3145736 | tf_op jit(solution)/shard_map/ppermute | solution.py:44
  538.6 90.5 %all-to-all-start.3 = ((bf16[8,144,1024]{2,1,0:T(8,128)(2,1)}), bf16[8,144,1024]{2,1,0:T(8,128)(2,1)S(1)}, u32[]{:S(2)}, u32[]{:S(2)}) async-start(bf16[8,144,1024]{2,1,0:T(8,128)(2,1)} %concatenate.104), calls=%async_computation.3 | async-start | bytes 4718592 | tf_op jit(solution)/shard_map/all_to_all | solution.py:251
  564.3 20.8 %collective-permute-start.5 = (bf16[2,2,32,2048]{3,2,1,0:T(8,128)(2,1)S(1)}, bf16[2,2,32,2048]{3,2,1,0:T(8,128)(2,1)S(1)}, u32[]{:S(2)}, u32[]{:S(2)}) collective-permute-start(bf16[2,2,32,2048]{3,2,1,0:T(8,128)(2,1)S(1)} %fusion.124), channel_id=1, source_target_pairs={{0,1},{1,0},{2,3},{3,2},{4,5},{5,4},{6,7},{7,6},{8,9},{9,8},{10,11... | collective-permute-start | bytes 1572872 | tf_op jit(solution)/shard_map/ppermute | solution.py:44
  571.9 44.5 %collective-permute-start.21 = (bf16[2,32,2048]{2,1,0:T(8,128)(2,1)S(1)}, bf16[2,32,2048]{2,1,0:T(8,128)(2,1)S(1)}, u32[]{:S(2)}, u32[]{:S(2)}) collective-permute-start(bf16[2,32,2048]{2,1,0:T(8,128)(2,1)S(1)} %fusion.135), channel_id=1, source_target_pairs={{0,4},{1,5},{2,6},{3,7},{4,0},{5,1},{6,2},{7,3},{8,12},{9,13},{10,... | collective-permute-start | bytes 786440 | tf_op jit(solution)/shard_map/ppermute | solution.py:44
  585.3 35.6 %collective-permute-start.6 = (bf16[2,32,2048]{2,1,0:T(8,128)(2,1)S(1)}, bf16[2,32,2048]{2,1,0:T(8,128)(2,1)S(1)}, u32[]{:S(2)}, u32[]{:S(2)}) collective-permute-start(bf16[2,32,2048]{2,1,0:T(8,128)(2,1)S(1)} %fusion.134), channel_id=1, source_target_pairs={{0,4},{1,5},{2,6},{3,7},{4,0},{5,1},{6,2},{7,3},{8,12},{9,13},{10,... | collective-permute-start | bytes 786440 | tf_op jit(solution)/shard_map/ppermute | solution.py:44
  724.8 15.5 %collective-permute-start.2 = (bf16[4,3,2304]{2,0,1:T(4,128)(2,1)}, bf16[4,3,2304]{2,0,1:T(4,128)(2,1)S(1)}, u32[]{:S(2)}, u32[]{:S(2)}) collective-permute-start(bf16[4,3,2304]{2,0,1:T(4,128)(2,1)} %copy.402), channel_id=1, source_target_pairs={{1,0},{2,1},{3,2},{4,3},{5,4},{6,5},{7,6},{9,8},{10,9},{11,10},{12... | collective-permute-start | bytes 165896 | tf_op jit(solution)/shard_map/ppermute | solution.py:24
  792.5 21.4 %collective-permute-start.23 = (f32[7392]{0:T(1024)S(1)}, f32[7392]{0:T(1024)S(1)}, u32[]{:S(2)}, u32[]{:S(2)}) collective-permute-start(f32[7392]{0:T(1024)S(1)} %pad_maximum_fusion.9), channel_id=1, source_target_pairs={{0,16},{8,24},{16,0},{24,8},{1,17},{9,25},{17,1},{25,9},{2,18},{10... | collective-permute-start | bytes 88712 | tf_op jit(solution)/shard_map/ppermute | solution.py:77
  814.3 14.9 %collective-permute-start.24 = (f32[3744]{0:T(1024)S(1)}, f32[3744]{0:T(1024)S(1)}, u32[]{:S(2)}, u32[]{:S(2)}) collective-permute-start(f32[3744]{0:T(1024)S(1)} %pad_maximum_fusion.10), channel_id=1, source_target_pairs={{0,8},{8,0},{16,24},{24,16},{1,9},{9,1},{17,25},{25,17},{2,10},{10... | collective-permute-start | bytes 44936 | tf_op jit(solution)/shard_map/ppermute | solution.py:77
  835.4 13.3 %collective-permute-start.8 = (f32[2,2,2,2,32,1152]{5,4,3,2,1,0:T(8,128)}, f32[2,2,2,2,32,1152]{5,4,3,2,1,0:T(8,128)}, u32[]{:S(2)}, u32[]{:S(2)}) collective-permute-start(f32[2,2,2,2,32,1152]{5,4,3,2,1,0:T(8,128)} %dynamic-slice_bitcast_fusion.6), channel_id=1, source_target_pairs={{0,8},{8,0},{16,24},{24,16},{1,9},{9,1},{17,25},{25,17},{2,10},{10... | collective-permute-start | bytes 7077896 | tf_op jit(solution)/shard_map/ppermute | solution.py:44
  838.0 14.3 %collective-permute-start.13 = (f32[2,2,2,2,32,1184]{5,4,3,2,1,0:T(8,128)}, f32[2,2,2,2,32,1184]{5,4,3,2,1,0:T(8,128)}, u32[]{:S(2)}, u32[]{:S(2)}) collective-permute-start(f32[2,2,2,2,32,1184]{5,4,3,2,1,0:T(8,128)} %dynamic-slice_bitcast_fusion.5), channel_id=1, source_target_pairs={{0,8},{8,0},{16,24},{24,16},{1,9},{9,1},{17,25},{25,17},{2,10},{10... | collective-permute-start | bytes 7274504 | tf_op jit(solution)/shard_map/ppermute | solution.py:44
  851.4 14.1 %collective-permute-start.9 = (bf16[2,2,2,32,1152]{4,3,2,1,0:T(8,128)(2,1)S(1)}, bf16[2,2,2,32,1152]{4,3,2,1,0:T(8,128)(2,1)S(1)}, u32[]{:S(2)}, u32[]{:S(2)}) collective-permute-start(bf16[2,2,2,32,1152]{4,3,2,1,0:T(8,128)(2,1)S(1)} %fusion.122), channel_id=1, source_target_pairs={{0,16},{8,24},{16,0},{24,8},{1,17},{9,25},{17,1},{25,9},{2,18},{10... | collective-permute-start | bytes 1769480 | tf_op jit(solution)/shard_map/ppermute | solution.py:44
  855.2 17.7 %collective-permute-start.14 = (bf16[2,2,2,32,1184]{4,3,2,1,0:T(8,128)(2,1)S(1)}, bf16[2,2,2,32,1184]{4,3,2,1,0:T(8,128)(2,1)S(1)}, u32[]{:S(2)}, u32[]{:S(2)}) collective-permute-start(bf16[2,2,2,32,1184]{4,3,2,1,0:T(8,128)(2,1)S(1)} %fusion.116), channel_id=1, source_target_pairs={{0,1},{1,0},{2,3},{3,2},{4,5},{5,4},{6,7},{7,6},{8,9},{9,8},{10,11... | collective-permute-start | bytes 1818632 | tf_op jit(solution)/shard_map/ppermute | solution.py:44
  865.8 11.0 %collective-permute-start.10 = (bf16[2,2,32,1152]{3,2,1,0:T(8,128)(2,1)S(1)}, bf16[2,2,32,1152]{3,2,1,0:T(8,128)(2,1)S(1)}, u32[]{:S(2)}, u32[]{:S(2)}) collective-permute-start(bf16[2,2,32,1152]{3,2,1,0:T(8,128)(2,1)S(1)} %fusion.132), channel_id=1, source_target_pairs={{0,1},{1,0},{2,3},{3,2},{4,5},{5,4},{6,7},{7,6},{8,9},{9,8},{10,11... | collective-permute-start | bytes 884744 | tf_op jit(solution)/shard_map/ppermute | solution.py:44
  876.9 12.4 %collective-permute-start.11 = (bf16[2,32,1152]{2,1,0:T(8,128)(2,1)S(1)}, bf16[2,32,1152]{2,1,0:T(8,128)(2,1)S(1)}, u32[]{:S(2)}, u32[]{:S(2)}) collective-permute-start(bf16[2,32,1152]{2,1,0:T(8,128)(2,1)S(1)} %fusion.141), channel_id=1, source_target_pairs={{0,4},{1,5},{2,6},{3,7},{4,0},{5,1},{6,2},{7,3},{8,12},{9,13},{10,... | collective-permute-start | bytes 442376 | tf_op jit(solution)/shard_map/ppermute | solution.py:44
  880.4 11.1 %collective-permute-start.16 = (bf16[2,32,1184]{2,1,0:T(8,128)(2,1)S(1)}, bf16[2,32,1184]{2,1,0:T(8,128)(2,1)S(1)}, u32[]{:S(2)}, u32[]{:S(2)}) collective-permute-start(bf16[2,32,1184]{2,1,0:T(8,128)(2,1)S(1)} %fusion.140), channel_id=1, source_target_pairs={{0,4},{1,5},{2,6},{3,7},{4,0},{5,1},{6,2},{7,3},{8,12},{9,13},{10,... | collective-permute-start | bytes 454664 | tf_op jit(solution)/shard_map/ppermute | solution.py:44
  (129 other events, 1505.2 us)
Sparse Core Ops, SparseCore 0:
  11.5 67.3 all-gather.2
  88.2 76.1 all-gather.4

commit v2 on v1

v2 whole, which is shorter than its diff:
```python
import functools

import jax
import jax.numpy as jnp
from jax import lax
from jax.experimental import pallas as pl
from jax.experimental.pallas import tpu as pltpu
from jax.sharding import PartitionSpec as P

STEP = 10


EPSILON = 1e-05
BETA_ONE = 0.9
BETA_TWO = 0.95
ADAM_EPS = 1e-08
DECAY_RATE = 0.1
RATE_IN = 0.03
RATE_OUT = 0.02
RATE_CONV = 0.3
RATE_GAIN = 0.2
RATE_HEAD = 0.5
LOG2E = 1.4426950408889634
BELOW = -1e30
LANES = 128
VMEM_BYTES = 58 << 20
NT = (((1,), (1,)), ((), ()))
TN = (((0,), (0,)), ((), ()))


def shifted(value, axis, steps):
    count = lax.axis_size(axis)
    first, last = (max(0, -steps), min(count, count - steps))
    return lax.ppermute(value, axis, [(source, source + steps) for source in range(first, last)])


def bit_count(axis):
    return lax.axis_size(axis).bit_length() - 1


def halve(values, axis, bit, dim, sent_type):
    mine = (lax.axis_index(axis) >> bit) & 1
    kept = lax.dynamic_index_in_dim(values, mine, dim, keepdims=False)
    away = lax.dynamic_index_in_dim(values, 1 - mine, dim, keepdims=False).astype(sent_type)
    count = lax.axis_size(axis)
    away = lax.ppermute(away, axis, [(place, place ^ (1 << bit)) for place in range(count)])
    return kept + away.astype(jnp.float32)


def sum_to_owner(values, y_first):
    dp_bits, ctx_bits = bit_count("dp"), bit_count("ctx")
    x_bits = dp_bits - 1
    names = [("dp", bit) for bit in reversed(range(dp_bits))]
    names += [("ctx", bit) for bit in reversed(range(ctx_bits))]
    rows = values.shape[0] >> len(names)
    values = values.reshape((2,) * len(names) + (rows, values.shape[1]))
    y_part = [("dp", bit) for bit in reversed(range(1, dp_bits))]
    x_part = [("ctx", bit) for bit in reversed(range(x_bits))]
    z_part = [("ctx", bit) for bit in reversed(range(x_bits, ctx_bits))]
    order = [("dp", 0)] + (y_part + x_part if y_first else x_part + y_part) + z_part
    for item in order:
        sent_type = jnp.float32
        values = halve(values, item[0], item[1], names.index(item), sent_type)
        names.remove(item)
    return values


def sum_small(values, shared):
    dp_bits, ctx_bits = bit_count("dp"), bit_count("ctx")
    names = [("dp", bit) for bit in reversed(range(dp_bits))]
    names += [("ctx", bit) for bit in reversed(range(ctx_bits))]
    values = values.reshape((2,) * len(names) + (values.shape[1],))
    for axis, bit in list(names):
        dim = names.index((axis, bit))
        mine = (lax.axis_index(axis) >> bit) & 1
        kept = lax.dynamic_index_in_dim(values, mine, dim, keepdims=False)
        away = lax.dynamic_index_in_dim(values, 1 - mine, dim, keepdims=False)
        count = lax.axis_size(axis)
        away = lax.ppermute(
            jnp.concatenate([away.reshape(-1), shared]),
            axis,
            [(place, place ^ (1 << bit)) for place in range(count)],
        )
        values = kept + away[: kept.size].reshape(kept.shape)
        shared = shared + away[kept.size :]
        names.remove((axis, bit))
    return values, shared


def inverse_rms(values):
    return lax.rsqrt(jnp.mean(values * values, axis=-1, keepdims=True) + EPSILON)


def dot(left, right, dims=(((1,), (0,)), ((), ())), precision=None):
    return lax.dot_general(
        left, right, dims, precision=precision, preferred_element_type=jnp.float32
    )


def split_parts(values):
    high = values.astype(jnp.bfloat16)
    rest = values - high.astype(jnp.float32)
    middle = rest.astype(jnp.bfloat16)
    low = (rest - middle.astype(jnp.float32)).astype(jnp.bfloat16)
    return high, middle, low


def spread_heads(values, spread):
    high, middle, low = split_parts(values)
    return dot(high, spread) + dot(middle, spread) + dot(low, spread)


def sum_heads(values, spread):
    high, middle, low = split_parts(values)
    return dot(high, spread, NT) + dot(middle, spread, NT) + dot(low, spread, NT)


def causal(rows, columns):
    at_row = lax.broadcasted_iota(jnp.int32, (rows, columns), 0)
    at_column = lax.broadcasted_iota(jnp.int32, (rows, columns), 1)
    return at_row, at_column


def kernel_call(body, grid, in_specs, out_specs, out_shape, scratch=()):
    return pl.pallas_call(
        body,
        grid=grid,
        in_specs=in_specs,
        out_specs=out_specs,
        out_shape=out_shape,
        scratch_shapes=list(scratch),
        compiler_params=pltpu.CompilerParams(
            dimension_semantics=("arbitrary",) * len(grid), vmem_limit_bytes=VMEM_BYTES
        ),
    )


def per_row(*shape):
    return pl.BlockSpec((1,) + shape, lambda row, *_: (row,) + (0,) * len(shape))


def whole(*shape):
    return pl.BlockSpec(shape, lambda *_: (0,) * len(shape))


def shape_of(shape, dtype):
    return jax.ShapeDtypeStruct(shape, dtype)


def entry_kernel(
    heads_count,
    x_ref,
    rim_ref,
    marks_ref,
    weight_ref,
    gain_ref,
    conv_ref,
    heads_ref,
    spread_ref,
    normed_ref,
    wide_out_ref,
    act_ref,
    raw_ref,
    step_ref,
    decay_ref,
    send_ref,
    wide_ref,
):
    length = x_ref.shape[1]
    inner, channels = spread_ref.shape[1], act_ref.shape[2]
    state = (channels - inner) // 2
    gain = gain_ref[0:1]

    def normalize(values):
        values = values.astype(jnp.float32)
        scale = lax.rsqrt(jnp.mean(values * values, axis=-1, keepdims=True) + EPSILON)
        return (values * scale * gain).astype(jnp.bfloat16)

    normed = normalize(x_ref[0])
    normed_ref[0] = normed
    rim = dot(normalize(rim_ref[0]), weight_ref[:, :channels])
    wide_ref[0:8] = rim[8:16].astype(jnp.bfloat16).astype(jnp.float32)
    part = 768 if channels % 768 == 0 else LANES
    for start in range(0, channels, part):
        piece = dot(normed, weight_ref[:, start : start + part]).astype(jnp.bfloat16)
        wide_ref[8:, start : start + part] = piece.astype(jnp.float32)
    raw = dot(normed, weight_ref[:, channels:])
    raw_ref[0] = raw

    def convolve(tile, carry):
        at = pl.ds(pl.multiple_of(tile * LANES, LANES), LANES)
        pre = jnp.broadcast_to(conv_ref[4:5, at], (length, LANES))
        for tap in range(3):
            taken = wide_ref[5 + tap : 5 + tap + length, at]
            pre = pre + conv_ref[tap : tap + 1, at] * taken * marks_ref[0, :, tap : tap + 1]
        pre = pre + conv_ref[3:4, at] * wide_ref[8:, at]
        act_ref[0, :, at] = (pre * jax.nn.sigmoid(pre)).astype(jnp.bfloat16)
        wide_out_ref[0, :, at] = jnp.concatenate(
            [jnp.zeros((8, LANES), jnp.float32), wide_ref[:, at]], axis=0
        ).astype(jnp.bfloat16)
        return carry

    lax.fori_loop(0, channels // LANES, convolve, 0)

    biased = raw + heads_ref[0:1]
    step = jnp.maximum(biased, 0.0) + jnp.log1p(jnp.exp(-jnp.abs(biased)))
    lane = lax.broadcasted_iota(jnp.int32, step.shape, 1)
    step = jnp.where(lane < heads_count, step, 0.0)
    step_ref[0] = step
    at_row, at_column = causal(length, length)
    lower = jnp.where(at_row >= at_column, 1.0, 0.0)
    decay = dot(lower, step * heads_ref[1:2], precision=lax.Precision.HIGHEST)
    decay_ref[0] = decay
    last = decay[length - 1 : length]
    end_weight = jnp.exp(last - decay) * marks_ref[0, :, 4:5] * step
    spread = spread_ref[...]
    scaled = (spread_heads(end_weight, spread) * act_ref[0, :, :inner].astype(jnp.float32)).astype(
        jnp.bfloat16
    )
    states = dot(act_ref[0, :, inner : inner + state], scaled, TN)
    passing = jnp.exp(last) * marks_ref[0, length - 1 : length, 3:4]
    passing = spread_heads(jnp.broadcast_to(passing, (8, LANES)), spread)
    groups, lanes = send_ref.shape[1], send_ref.shape[3]
    for group in range(groups):
        at = slice(group * lanes, (group + 1) * lanes)
        send_ref[0, group, :state] = states[:, at]
        send_ref[0, group, state:] = passing[:, at]


def pair_masks(pair_lanes, head_dim, rows):
    lane = lax.broadcasted_iota(jnp.int32, (rows, pair_lanes), 1)
    return [
        (lane >= member * head_dim) & (lane < (member + 1) * head_dim)
        for member in range(pair_lanes // head_dim)
    ]


def inner_forward_kernel(
    heads_count, act_ref, step_ref, decay_ref, marks_ref, segment_ref, y_ref
):
    length = act_ref.shape[1]
    inner = y_ref.shape[2]
    state = (act_ref.shape[2] - inner) // 2
    head_dim = inner // heads_count
    b_state = act_ref[0, :, inner : inner + state]
    c_state = act_ref[0, :, inner + state :]
    decay = decay_ref[0] * LOG2E
    lifted = (decay - jnp.log2(step_ref[0])).T
    at_row, at_column = causal(length, length)
    joined = (at_row >= at_column) & (marks_ref[0, :, 5:6] == segment_ref[0, 0:1])
    masked = jnp.where(joined, 0.0, BELOW)
    scores = dot(c_state, b_state, NT)
    chunk = max(length // 2, 16)
    masks = pair_masks(LANES, head_dim, length)
    for pair in range(inner // LANES):
        at = slice(pair * LANES, (pair + 1) * LANES)
        x_pair = act_ref[0, :, at]
        members = [jnp.where(mask, x_pair, jnp.zeros_like(x_pair)) for mask in masks]
        for start in range(0, length, chunk):
            rows, seen = slice(start, start + chunk), start + chunk
            total = jnp.zeros((chunk, LANES), jnp.float32)
            for member, x_member in enumerate(members):
                head = pair * len(masks) + member
                span = decay[rows, head : head + 1] - lifted[head : head + 1, :seen]
                mixing = scores[rows, :seen] * jnp.exp2(span + masked[rows, :seen])
                total = total + dot(mixing.astype(jnp.bfloat16), x_member[:seen])
            y_ref[0, rows, at] = total


def carry_forward_kernel(received_ref, low_ref, incoming_ref):
    blocks, state = low_ref.shape[0], low_ref.shape[1]
    carried = jnp.zeros(low_ref.shape[1:], jnp.float32)
    for block in range(blocks):
        incoming_ref[block] = carried
        low_ref[block] = carried.astype(jnp.bfloat16)
        passing = received_ref[block, state : state + 1]
        carried = passing * carried + received_ref[block, :state].astype(jnp.float32)


def carry_backward_kernel(received_ref, passing_ref, incoming_ref, send_ref):
    blocks, state = received_ref.shape[0], received_ref.shape[1]
    carried = jnp.zeros(received_ref.shape[1:], jnp.float32)
    for block in reversed(range(blocks)):
        send_ref[block, :state] = carried.astype(jnp.bfloat16)
        total = jnp.sum(carried * incoming_ref[block], axis=0, keepdims=True)
        parts = [part.astype(jnp.float32) for part in split_parts(total)]
        parts.append(jnp.zeros((13,) + total.shape[1:], jnp.float32))
        send_ref[block, state:] = jnp.concatenate(parts, axis=0).astype(jnp.bfloat16)
        carried = passing_ref[block, 0:1] * carried + received_ref[block].astype(jnp.float32)


def join_groups(ref, rows):
    return jnp.concatenate([ref[0, group, rows] for group in range(ref.shape[1])], axis=1)


def middle_kernel(
    groups,
    cotangent_ref,
    normed_ref,
    gate_weight_ref,
    out_weight_ref,
    gain_ref,
    skip_ref,
    act_ref,
    y_ref,
    incoming_ref,
    decay_ref,
    marks_ref,
    spread_ref,
    mixed_ref,
    grad_gate_ref,
    grad_ssd_ref,
    send_ref,
    grad_c_ref,
    row_term_ref,
    grad_gain_ref,
    grad_skip_ref,
    total_ref,
):
    row, piece = pl.program_id(0), pl.program_id(1)
    inner = spread_ref.shape[1]
    state = total_ref.shape[0]
    spread = spread_ref[...]
    gain, skip = gain_ref[0:1], skip_ref[0:1]
    x_part = act_ref[0, :, :inner].astype(jnp.float32)
    c_state = act_ref[0, :, inner + state :]
    incoming = join_groups(incoming_ref, slice(None))
    entry = spread_heads(jnp.exp(decay_ref[0]) * marks_ref[0, :, 3:4], spread)
    inner_part = y_ref[0] + entry * dot(c_state, incoming)
    ssd = inner_part + skip * x_part
    gate = dot(normed_ref[0], gate_weight_ref[...])
    sigmoid = jax.nn.sigmoid(gate)
    silu = gate * sigmoid
    gated = ssd * silu
    scale = lax.rsqrt(jnp.mean(gated * gated, axis=-1, keepdims=True) + EPSILON)
    unit = gated * scale
    mixed_ref[0] = (unit * gain).astype(jnp.bfloat16)
    grad_mixed = dot(cotangent_ref[0], out_weight_ref[...], NT)
    grad_unit = grad_mixed * gain
    mean = jnp.mean(grad_unit * unit, axis=-1, keepdims=True)
    grad_gated = scale * (grad_unit - unit * mean)
    slope = sigmoid * (1.0 + gate * (1.0 - sigmoid))
    grad_gate_ref[0] = (grad_gated * ssd * slope).astype(jnp.bfloat16)
    grad_ssd = (grad_gated * silu).astype(jnp.bfloat16)
    grad_ssd_ref[0] = grad_ssd
    grad_ssd = grad_ssd.astype(jnp.float32)
    row_term_ref[0] = sum_heads(grad_ssd * inner_part, spread)
    grad_before = (grad_ssd * entry).astype(jnp.bfloat16)
    grad_c_ref[0] = dot(grad_before, incoming, NT)
    grad_states = dot(c_state, grad_before, TN)
    gain_sum = jnp.sum(grad_mixed * unit, axis=0, keepdims=True)
    skip_sum = jnp.sum(grad_ssd * x_part, axis=0, keepdims=True)

    @pl.when(piece == 0)
    def _():
        total_ref[...] = grad_states

    @pl.when(piece > 0)
    def _():
        total_ref[...] += grad_states

    @pl.when((piece == 0) & (row == 0))
    def _():
        grad_gain_ref[...] = jnp.zeros_like(grad_gain_ref)
        grad_skip_ref[...] = jnp.zeros_like(grad_skip_ref)

    grad_gain_ref[0:1] += gain_sum
    grad_skip_ref[0:1] += skip_sum
    lanes = inner // groups

    @pl.when(piece == pl.num_programs(1) - 1)
    def _():
        for group in range(groups):
            at = slice(group * lanes, (group + 1) * lanes)
            send_ref[0, group] = total_ref[:, at].astype(jnp.bfloat16)


def inner_backward_kernel(
    heads_count,
    act_ref,
    grad_ssd_ref,
    step_ref,
    decay_ref,
    marks_ref,
    segment_ref,
    grad_x_ref,
    grad_b_ref,
    grad_c_ref,
    total_ref,
):
    length = act_ref.shape[1]
    inner = grad_ssd_ref.shape[2]
    state = (act_ref.shape[2] - inner) // 2
    head_dim = inner // heads_count
    b_state = act_ref[0, :, inner : inner + state]
    c_state = act_ref[0, :, inner + state :]
    decay = decay_ref[0] * LOG2E
    lowered = jnp.log2(step_ref[0]) - decay
    decay = decay.T
    at_row, at_column = causal(length, length)
    joined = (at_row <= at_column) & (marks_ref[0, :, 5:6] == segment_ref[0, 0:1])
    masked = jnp.where(joined, 0.0, BELOW)
    scores = dot(b_state, c_state, NT)
    chunk = max(length // 2, 16)
    masks = pair_masks(LANES, head_dim, length)
    total_ref[...] = jnp.zeros_like(total_ref)
    for pair in range(inner // LANES):
        at = slice(pair * LANES, (pair + 1) * LANES)
        x_pair = act_ref[0, :, at]
        grad_pair = grad_ssd_ref[0, :, at]
        members = [jnp.where(mask, grad_pair, jnp.zeros_like(grad_pair)) for mask in masks]
        for start in range(0, length, chunk):
            rows, later = slice(start, start + chunk), slice(start, length)
            grad_x = jnp.zeros((chunk, LANES), jnp.float32)
            for member, grad_member in enumerate(members):
                head = pair * len(masks) + member
                span = decay[head : head + 1, later] + lowered[rows, head : head + 1]
                weight = jnp.exp2(span + masked[rows, later])
                mixing = (scores[rows, later] * weight).astype(jnp.bfloat16)
                grad_x = grad_x + dot(mixing, grad_member[later])
                total_ref[rows, later] += dot(x_pair[rows], grad_member[later], NT) * weight
            grad_x_ref[0, rows, at] = grad_x
    grad_scores = total_ref[...].astype(jnp.bfloat16)
    grad_b_ref[0] = dot(grad_scores, c_state)
    grad_c_ref[0] = dot(grad_scores, b_state, TN)


def exit_kernel(
    act_ref,
    wide_ref,
    grad_ssd_ref,
    inner_x_ref,
    inner_b_ref,
    inner_c_ref,
    outer_c_ref,
    leaving_ref,
    row_term_ref,
    raw_ref,
    step_ref,
    decay_ref,
    marks_ref,
    conv_ref,
    heads_ref,
    skip_ref,
    spread_ref,
    grad_mixer_ref,
    tail_ref,
    rim_ref,
    grad_conv_ref,
    grad_heads_ref,
    grad_act_ref,
    shift_ref,
    taken_ref,
):
    row = pl.program_id(0)
    length, channels = act_ref.shape[1], act_ref.shape[2]
    inner = spread_ref.shape[1]
    state = (channels - inner) // 2
    spread = spread_ref[...]
    step, decay = step_ref[0], decay_ref[0]
    b_state = act_ref[0, :, inner : inner + state]
    leaving = join_groups(leaving_ref, slice(0, state))
    x_part = act_ref[0, :, :inner].astype(jnp.float32)
    last = decay[length - 1 : length]
    end_weight = spread_heads(jnp.exp(last - decay) * marks_ref[0, :, 4:5] * step, spread)
    scaled = (end_weight * x_part).astype(jnp.bfloat16)
    end_part = end_weight * dot(b_state, leaving)
    grad_x = inner_x_ref[0] + end_part
    grad_act_ref[:, :inner] = grad_x + skip_ref[0:1] * grad_ssd_ref[0].astype(jnp.float32)
    grad_act_ref[:, inner : inner + state] = inner_b_ref[0] + dot(scaled, leaving, NT)
    grad_act_ref[:, inner + state :] = inner_c_ref[0] + outer_c_ref[0]
    column_term = sum_heads(x_part * grad_x, spread)
    passed = join_groups(leaving_ref, slice(state, state + 16)).astype(jnp.float32)
    passed = jnp.sum(passed, axis=0, keepdims=True)
    ended = jnp.sum(x_part * end_part, axis=0, keepdims=True)
    ends = sum_heads(jnp.concatenate([passed, ended, jnp.zeros((6, inner), jnp.float32)], 0), spread)
    passing = jnp.exp(last) * marks_ref[0, length - 1 : length, 3:4]
    final = ends[1:2] + ends[0:1] * passing
    at_row, at_column = causal(length, length)
    token = lax.broadcasted_iota(jnp.int32, step.shape, 0)
    grad_decay = row_term_ref[0] - column_term + jnp.where(token == length - 1, final, 0.0)
    upper = jnp.where(at_row <= at_column, 1.0, 0.0)
    grad_later = dot(upper, grad_decay, precision=lax.Precision.HIGHEST)
    rate = heads_ref[1:2]
    grad_step = jnp.where(step > 0.0, column_term / jnp.where(step > 0.0, step, 1.0), 0.0)
    grad_step = grad_step + rate * grad_later
    grad_raw = grad_step * jax.nn.sigmoid(raw_ref[0] + heads_ref[0:1])
    grad_raw = jnp.where(step > 0.0, grad_raw, 0.0)
    grad_mixer_ref[0, :, channels:] = grad_raw.astype(jnp.bfloat16)

    @pl.when(row == 0)
    def _():
        grad_conv_ref[...] = jnp.zeros_like(grad_conv_ref)
        grad_heads_ref[...] = jnp.zeros_like(grad_heads_ref)

    grad_heads_ref[0:1] += jnp.sum(grad_later * step, axis=0, keepdims=True) * rate
    grad_heads_ref[1:2] += jnp.sum(grad_raw, axis=0, keepdims=True)

    def convolve(tile, carry):
        at = pl.ds(pl.multiple_of(tile * LANES, LANES), LANES)
        taken_ref[...] = wide_ref[0, :, at].astype(jnp.float32)
        pre = jnp.broadcast_to(conv_ref[4:5, at], (length, LANES))
        for tap in range(3):
            taken = taken_ref[13 + tap : 13 + tap + length]
            pre = pre + conv_ref[tap : tap + 1, at] * taken * marks_ref[0, :, tap : tap + 1]
        pre = pre + conv_ref[3:4, at] * taken_ref[16:]
        sigmoid = jax.nn.sigmoid(pre)
        grad_pre = grad_act_ref[:, at] * (sigmoid * (1.0 + pre * (1.0 - sigmoid)))
        grad_conv_ref[4:5, at] += jnp.sum(grad_pre, axis=0, keepdims=True)
        grad_conv_ref[3:4, at] += jnp.sum(grad_pre * taken_ref[16:], axis=0, keepdims=True)
        grad_in = grad_pre * conv_ref[3:4, at]
        rim = jnp.zeros((8, LANES), jnp.float32)
        shift_ref[0:8] = jnp.zeros((8, LANES), jnp.float32)
        shift_ref[length + 8 :] = jnp.zeros((8, LANES), jnp.float32)
        for tap in range(3):
            masked = grad_pre * marks_ref[0, :, tap : tap + 1]
            taken = taken_ref[13 + tap : 13 + tap + length]
            grad_conv_ref[tap : tap + 1, at] += jnp.sum(masked * taken, axis=0, keepdims=True)
            shift_ref[8 : length + 8] = masked * conv_ref[tap : tap + 1, at]
            grad_in = grad_in + shift_ref[11 - tap : 11 - tap + length]
            rim = rim + shift_ref[8 - tap : 16 - tap]
        grad_mixer_ref[0, :, at] = grad_in.astype(jnp.bfloat16)
        tail_ref[0, :, at] = grad_in[length - 8 :]
        rim_ref[0, :, at] = rim
        return carry

    lax.fori_loop(0, channels // LANES, convolve, 0)


def adamw(weight, gradient, first_moment, second_moment, step_rate):
    first_new = BETA_ONE * first_moment + (1.0 - BETA_ONE) * gradient
    second_new = BETA_TWO * second_moment + (1.0 - BETA_TWO) * gradient * gradient
    corrected = first_new / (1.0 - BETA_ONE**STEP)
    spread = jnp.sqrt(second_new / (1.0 - BETA_TWO**STEP))
    weight_new = weight - step_rate * (corrected / (spread + ADAM_EPS) + DECAY_RATE * weight)
    return (first_new, second_new, weight_new)


def local(
    tokens,
    cotangent,
    segments,
    w_in,
    w_out,
    conv,
    gains,
    heads,
    in_first,
    in_second,
    out_first,
    out_second,
    conv_first,
    conv_second,
    gain_first,
    gain_second,
    head_first,
    head_second,
):
    devices = lax.axis_size(("dp", "ctx"))
    ctx_count = lax.axis_size("ctx")
    inner_width = w_out.shape[0] * devices
    own_rows, projected_width = w_in.shape
    seq_count, length, model_width = tokens.shape
    channels, taps = conv.shape[0] * devices, conv.shape[1] - 1
    state_dim = (channels - inner_width) // 2
    heads_count = heads.shape[1]
    head_dim = inner_width // heads_count
    mixer_width = projected_width - inner_width
    spare = -mixer_width % LANES
    wide_width = mixer_width + spare
    groups = ctx_count // seq_count
    lanes = inner_width // groups
    f32, bf16 = jnp.float32, jnp.bfloat16

    small = jnp.concatenate([conv.reshape(-1), gains])
    small = jnp.pad(small, (0, own_rows * spare - small.shape[0])).reshape(own_rows, spare)
    first_send = jnp.concatenate([w_in[:, inner_width:], small], axis=1).astype(bf16)
    mixer_weight = lax.all_gather(first_send, ("dp", "ctx"), axis=0, tiled=True)
    second_send = jnp.concatenate([w_in[:, :inner_width], w_out.reshape(own_rows, -1)], axis=1)
    mixer_weight, second_send = lax.optimization_barrier(
        (mixer_weight, second_send.astype(bf16))
    )
    second_weights = lax.all_gather(second_send, ("dp", "ctx"), axis=0, tiled=True)
    gate_weight = second_weights[:, :inner_width]
    output_weight = second_weights[:, inner_width:].reshape(inner_width, model_width)
    small = mixer_weight[:, mixer_width:].reshape(devices, own_rows * spare)
    conv_rows = small[:, : conv.size].reshape(channels, taps + 1).astype(f32).T
    conv_rows = jnp.pad(conv_rows, ((0, 7 - taps), (0, 0)))
    gain_vector = small[:, conv.size : conv.size + gains.size].reshape(-1).astype(f32)
    gain_in, gain_out = gain_vector[:model_width], gain_vector[model_width:]

    rim_x, rim_segment = shifted((tokens[:, length - 16 :], segments[:, length - 16 :]), "ctx", 1)
    rim_segment = jnp.where(lax.axis_index("ctx") == 0, -1, rim_segment)
    wide_segment = jnp.concatenate([rim_segment, segments], axis=1)
    marks = [wide_segment[:, 13 + tap : 13 + tap + length] == segments for tap in range(3)]
    marks.append(segments == rim_segment[:, 15:])
    marks.append(segments == segments[:, length - 1 :])
    marks = [mark.astype(f32) for mark in marks] + [segments.astype(f32)]
    marks = jnp.stack(marks + [jnp.zeros_like(marks[0])] * 2, axis=2)
    segment_rows = jnp.broadcast_to(segments.astype(f32)[:, None], (seq_count, 8, length))
    head_rows = jnp.stack([heads[2], -jnp.exp(heads[0])])
    head_rows = jnp.pad(head_rows, ((0, 6), (0, LANES - heads_count)))
    skip_row = jnp.broadcast_to(jnp.repeat(heads[1], head_dim), (8, inner_width))
    lane_head = lax.broadcasted_iota(jnp.int32, (LANES, inner_width), 1) // head_dim
    spread = lane_head == lax.broadcasted_iota(jnp.int32, (LANES, inner_width), 0)
    spread = spread.astype(bf16)
    gain_rows = jnp.broadcast_to(gain_in, (8, model_width))
    gate_rows = jnp.broadcast_to(gain_out, (8, inner_width))

    normed, wide_in, activated, step_raw, step_size, decay_sum, sent = kernel_call(
        functools.partial(entry_kernel, heads_count),
        (seq_count,),
        [
            per_row(length, model_width),
            per_row(16, model_width),
            per_row(length, 8),
            whole(model_width, wide_width),
            whole(8, model_width),
            whole(8, channels),
            whole(8, LANES),
            whole(LANES, inner_width),
        ],
        [
            per_row(length, model_width),
            per_row(length + 16, channels),
            per_row(length, channels),
            per_row(length, LANES),
            per_row(length, LANES),
            per_row(length, LANES),
            per_row(groups, state_dim + 8, lanes),
        ],
        [
            shape_of((seq_count, length, model_width), bf16),
            shape_of((seq_count, length + 16, channels), bf16),
            shape_of((seq_count, length, channels), bf16),
            shape_of((seq_count, length, LANES), f32),
            shape_of((seq_count, length, LANES), f32),
            shape_of((seq_count, length, LANES), f32),
            shape_of((seq_count, groups, state_dim + 8, lanes), f32),
        ],
        [pltpu.VMEM((length + 8, channels), f32)],
    )(tokens, rim_x, marks, mixer_weight, gain_rows, conv_rows, head_rows, spread)

    received = lax.all_to_all(
        sent.reshape(ctx_count, state_dim + 8, lanes), "ctx", 0, 0, tiled=True
    )
    within = kernel_call(
        functools.partial(inner_forward_kernel, heads_count),
        (seq_count,),
        [
            per_row(length, channels),
            per_row(length, LANES),
            per_row(length, LANES),
            per_row(length, 8),
            per_row(8, length),
        ],
        per_row(length, inner_width),
        shape_of((seq_count, length, inner_width), f32),
    )(activated, step_size, decay_sum, marks, segment_rows)
    tile = min(lanes, 2 * LANES)
    by_lane = lambda rows: pl.BlockSpec((ctx_count, rows, tile), lambda place: (0, 0, place))
    incoming_low, incoming = kernel_call(
        carry_forward_kernel,
        (lanes // tile,),
        [by_lane(state_dim + 8)],
        [by_lane(state_dim), by_lane(state_dim)],
        [
            shape_of((ctx_count, state_dim, lanes), bf16),
            shape_of((ctx_count, state_dim, lanes), f32),
        ],
    )(received)
    incoming_low = lax.all_to_all(incoming_low, "ctx", 0, 0, tiled=True)
    incoming_low = incoming_low.reshape(seq_count, groups, state_dim, lanes)

    half = min(length, 128)
    by_piece = lambda columns: pl.BlockSpec((1, half, columns), lambda row, piece: (row, piece, 0))
    mixed, grad_gate, grad_ssd, sent, outer_c, row_term, grad_gain_out, grad_skip = kernel_call(
        functools.partial(middle_kernel, groups),
        (seq_count, length // half),
        [
            by_piece(model_width),
            by_piece(model_width),
            whole(model_width, inner_width),
            whole(inner_width, model_width),
            whole(8, inner_width),
            whole(8, inner_width),
            by_piece(channels),
            by_piece(inner_width),
            per_row(groups, state_dim, lanes),
            by_piece(LANES),
            by_piece(8),
            whole(LANES, inner_width),
        ],
        [
            by_piece(inner_width),
            by_piece(inner_width),
            by_piece(inner_width),
            per_row(groups, state_dim, lanes),
            by_piece(state_dim),
            by_piece(LANES),
            whole(8, inner_width),
            whole(8, inner_width),
        ],
        [
            shape_of((seq_count, length, inner_width), bf16),
            shape_of((seq_count, length, inner_width), bf16),
            shape_of((seq_count, length, inner_width), bf16),
            shape_of((seq_count, groups, state_dim, lanes), bf16),
            shape_of((seq_count, length, state_dim), f32),
            shape_of((seq_count, length, LANES), f32),
            shape_of((8, inner_width), f32),
            shape_of((8, inner_width), f32),
        ],
        [pltpu.VMEM((state_dim, inner_width), f32)],
    )(
        cotangent,
        normed,
        gate_weight,
        output_weight,
        gate_rows,
        skip_row,
        activated,
        within,
        incoming_low,
        decay_sum,
        marks,
        spread,
    )
    grad_received = lax.all_to_all(
        sent.reshape(ctx_count, state_dim, lanes), "ctx", 0, 0, tiled=True
    )
    inner_x, inner_b, inner_c = kernel_call(
        functools.partial(inner_backward_kernel, heads_count),
        (seq_count,),
        [
            per_row(length, channels),
            per_row(length, inner_width),
            per_row(length, LANES),
            per_row(length, LANES),
            per_row(length, 8),
            per_row(8, length),
        ],
        [per_row(length, inner_width), per_row(length, state_dim), per_row(length, state_dim)],
        [
            shape_of((seq_count, length, inner_width), f32),
            shape_of((seq_count, length, state_dim), f32),
            shape_of((seq_count, length, state_dim), f32),
        ],
        [pltpu.VMEM((length, length), f32)],
    )(activated, grad_ssd, step_size, decay_sum, marks, segment_rows)
    sent = kernel_call(
        carry_backward_kernel,
        (lanes // tile,),
        [
            by_lane(state_dim),
            pl.BlockSpec((ctx_count, 8, tile), lambda place: (0, state_dim // 8, place)),
            by_lane(state_dim),
        ],
        by_lane(state_dim + 16),
        shape_of((ctx_count, state_dim + 16, lanes), bf16),
    )(grad_received, received, incoming)
    leaving = lax.all_to_all(sent, "ctx", 0, 0, tiled=True)
    leaving = leaving.reshape(seq_count, groups, state_dim + 16, lanes)

    def join(left, right):
        return jnp.einsum("nay,nag->yg", left, right, preferred_element_type=f32)

    input_float = tokens.astype(f32)
    output = (
        input_float
        + jnp.einsum("exp,pk->exk", mixed, output_weight, preferred_element_type=f32)
    ).astype(bf16)
    out_sum = sum_to_owner(join(mixed, cotangent).reshape(devices * own_rows, -1), False)
    gate_sum = sum_to_owner(join(normed, grad_gate), True)
    gate_normed = jnp.einsum("hou,qu->hoq", grad_gate, gate_weight, preferred_element_type=f32)

    grad_mixer, tail, rim, grad_conv, grad_heads = kernel_call(
        exit_kernel,
        (seq_count,),
        [
            per_row(length, channels),
            per_row(length + 16, channels),
            per_row(length, inner_width),
            per_row(length, inner_width),
            per_row(length, state_dim),
            per_row(length, state_dim),
            per_row(length, state_dim),
            per_row(groups, state_dim + 16, lanes),
            per_row(length, LANES),
            per_row(length, LANES),
            per_row(length, LANES),
            per_row(length, LANES),
            per_row(length, 8),
            whole(8, channels),
            whole(8, LANES),
            whole(8, inner_width),
            whole(LANES, inner_width),
        ],
        [
            per_row(length, wide_width),
            per_row(8, channels),
            per_row(8, channels),
            whole(8, channels),
            whole(8, LANES),
        ],
        [
            shape_of((seq_count, length, wide_width), bf16),
            shape_of((seq_count, 8, channels), f32),
            shape_of((seq_count, 8, channels), f32),
            shape_of((8, channels), f32),
            shape_of((8, LANES), f32),
        ],
        [
            pltpu.VMEM((length, channels), f32),
            pltpu.VMEM((length + 16, LANES), f32),
            pltpu.VMEM((length + 16, LANES), f32),
        ],
    )(
        activated,
        wide_in,
        grad_ssd,
        inner_x,
        inner_b,
        inner_c,
        outer_c,
        leaving,
        row_term,
        step_raw,
        step_size,
        decay_sum,
        marks,
        conv_rows,
        head_rows,
        skip_row,
        spread,
    )
    rim_back = shifted(rim[:, : taps - 1].astype(bf16), "ctx", -1).astype(f32)
    tail = tail.at[:, 9 - taps :].add(rim_back).astype(bf16)
    grad_mixer = grad_mixer.at[:, length - 8 :, :channels].set(tail)
    grad_mixer_weight = join(normed, grad_mixer)
    middle = wide_width // 256 * 128
    left_sum = sum_to_owner(grad_mixer_weight[:, :middle], True)
    right_sum = sum_to_owner(grad_mixer_weight[:, middle:], False)
    grad_normed = gate_normed + jnp.einsum(
        "hou,qu->hoq", grad_mixer, mixer_weight, preferred_element_type=f32
    )
    scale_in = inverse_rms(input_float)
    unit_in = input_float * scale_in
    grad_gain_in = jnp.sum(grad_normed * unit_in, axis=(0, 1))
    grad_unit_in = grad_normed * gain_in
    grad_tokens = cotangent.astype(f32) + scale_in * (
        grad_unit_in - unit_in * jnp.mean(grad_unit_in * unit_in, axis=-1, keepdims=True)
    )
    grad_conv = grad_conv[: taps + 1].T
    grad_gains = jnp.concatenate([grad_gain_in, grad_gain_out[0]])
    grad_skip = jnp.sum(grad_skip[0].reshape(heads_count, head_dim), axis=1)
    grad_heads = jnp.concatenate(
        [grad_heads[0, :heads_count], grad_skip, grad_heads[1, :heads_count]]
    )
    small_sum, head_grad = sum_small(
        jnp.concatenate(
            [grad_conv.reshape(devices, -1), grad_gains.reshape(devices, -1)], axis=1
        ),
        grad_heads,
    )
    owned_grads = (
        jnp.concatenate([gate_sum, left_sum, right_sum], axis=1)[:, :projected_width],
        out_sum.reshape(w_out.shape),
        small_sum[: conv.size].reshape(conv.shape),
        small_sum[conv.size :],
    )
    head_grad = head_grad.reshape(heads.shape)
    in_new = adamw(w_in, owned_grads[0], in_first, in_second, RATE_IN)
    out_new = adamw(w_out, owned_grads[1], out_first, out_second, RATE_OUT)
    conv_new = adamw(conv, owned_grads[2], conv_first, conv_second, RATE_CONV)
    gain_new = adamw(gains, owned_grads[3], gain_first, gain_second, RATE_GAIN)
    head_new = adamw(heads, head_grad, head_first, head_second, RATE_HEAD)
    return (
        output,
        grad_tokens,
        in_new[0],
        in_new[1],
        in_new[2],
        out_new[0],
        out_new[1],
        out_new[2],
        conv_new[0],
        conv_new[1],
        conv_new[2],
        gain_new[0],
        gain_new[1],
        gain_new[2],
        head_new[0],
        head_new[1],
        head_new[2],
    )


def solution(mesh):
    placed = (
        P("dp", "ctx", None),
        P("dp", "ctx", None),
        P("dp", "ctx"),
        P(("dp", "ctx"), None),
        P(("dp", "ctx"), None),
        P(("dp", "ctx"), None),
        P(("dp", "ctx")),
        P(),
        P(("dp", "ctx"), None),
        P(("dp", "ctx"), None),
        P(("dp", "ctx"), None),
        P(("dp", "ctx"), None),
        P(("dp", "ctx"), None),
        P(("dp", "ctx"), None),
        P(("dp", "ctx")),
        P(("dp", "ctx")),
        P(),
        P(),
    )
    return jax.shard_map(
        local,
        mesh=mesh,
        in_specs=placed,
        out_specs=(
            P("dp", "ctx", None),
            P("dp", "ctx", None),
            P(("dp", "ctx"), None),
            P(("dp", "ctx"), None),
            P(("dp", "ctx"), None),
            P(("dp", "ctx"), None),
            P(("dp", "ctx"), None),
            P(("dp", "ctx"), None),
            P(("dp", "ctx"), None),
            P(("dp", "ctx"), None),
            P(("dp", "ctx"), None),
            P(("dp", "ctx")),
            P(("dp", "ctx")),
            P(("dp", "ctx")),
            P(),
            P(),
            P(),
        ),
        check_vma=False,
    )
```

time: 914 us -> 738 us (0.81)
  Pallas kernels: 0 us -> 168 us
  local copies, waits for them, and re-layouts: 247 us -> 86.4 us
  matrix products: 195 us -> 40.9 us
  other arithmetic: 174 us -> 43.7 us
  blocking collectives: 0 us -> 111 us
  starting transfers between devices: 59.6 us -> 48.1 us
    pallas_call x0 -> x7, Pallas kernels: none -> 168 us  [the longest x1 46.5 us: local(): kernel_call(exit_kernel, (seq_count,), [per_row(length, channels), per_ro...]
    dot_general x41 -> x4, matrix products: 177 us -> 25 us  [the longest x3 19.3 us: join(): return jnp.einsum('nay,nag->yg', left, right, preferred_element_type=f32)]
    all_to_all x0 -> x1, blocking collectives: none -> 111 us  [local(): lax.all_to_all(sent.reshape(ctx_count, state_dim + 8, lanes), 'ctx', 0, 0...]
    add x5 -> x7, other arithmetic: 44.3 us -> 4.33 us  [the longest x1 2.95 us: local(): cotangent.astype(f32)]
    convert_element_type x11 -> x3, other arithmetic: 35.6 us -> 1.67 us  [the longest x1 0.9 us: local(): spread = spread.astype(bf16)]
    reduce_sum x8 -> x1, other arithmetic: 31.8 us -> 0.12 us  [local(): grad_skip = jnp.sum(grad_skip[0].reshape(heads_count, head_dim), axis=1)]
    scatter-add x1, local copies, waits for them, and re-layouts: 26.6 us -> 2.06 us  [local(): tail = tail.at[:, 9 - taps:].add(rim_back).astype(bf16)]
    slice x23 -> x13, local copies, waits for them, and re-layouts: 36.7 us -> 12.7 us  [the longest x1 6.22 us: local(): second_weights[:, inner_width:].reshape(inner_width, model_width)]
  transfers between devices with their start and end apart: 34 -> 33, of which waited for: 18 -> 15; matrix products, arithmetic and copies ran while one was open for 41% -> 18% of each run, Pallas kernels for 0% -> 17%
where the time goes in v2:
time: 738 us; the launch traced here: 731 us
  waiting for transfers between devices  218 us (30%)
  Pallas kernels  168 us (23%)
  blocking collectives  111 us (15%)
  local copies, waits for them, and re-layouts  86.4 us (12%)
  starting transfers between devices  48.1 us (7%)
  other arithmetic  43.7 us (6%)
  matrix products  40.9 us (6%)
  between operations  15.6 us (2%)
    all_to_all x1, blocking collectives, local(): lax.all_to_all(sent.reshape(ctx_count, state_dim + 8, lanes), 'ctx', 0, 0...  111 us
    ppermute x20, waiting for transfers between devices, halve(): lax.ppermute(away, axis, [(place, place ^ 1 << bit) for place in range(co...  92.3 us
    all_gather x1, waiting for transfers between devices, local(): mixer_weight = lax.all_gather(first_send, ('dp', 'ctx'), axis=0, tiled=True)  66.2 us
    pallas_call x1, Pallas kernels, local(): kernel_call(exit_kernel, (seq_count,), [per_row(length, channels), per_ro...  46.5 us
    pallas_call x1, Pallas kernels, local(): kernel_call(functools.partial(middle_kernel, groups), (seq_count, length...  43 us
    pallas_call x1, Pallas kernels, local(): kernel_call(functools.partial(entry_kernel, heads_count), (seq_count,), [...  41.7 us
    all_to_all x1, waiting for transfers between devices, local(): lax.all_to_all(sent.reshape(ctx_count, state_dim, lanes), 'ctx', 0, 0, ti...  26.2 us
    all_to_all x1, waiting for transfers between devices, local(): incoming_low = lax.all_to_all(incoming_low, 'ctx', 0, 0, tiled=True)  23.7 us
  transfers between devices with their start and end apart: 33, of which 15 were waited for; matrix products, arithmetic and copies ran while one was open for 18% of the time, Pallas kernels for 17%

profile of v2, /device:TPU:0, one launch (start us, length us, event | category | flops | bytes accessed | tf_op | source)
XLA Modules:
  0.0 730.6 jit_solution(4570499656824911922)
XLA Ops:
  12.7 66.2 %all-gather.3.cloned.1.call-done.weight_ref = bf16[1024,2432]{1,0:T(8,128)(2,1)} async-done(((bf16[32,2432]{1,0:T(8,128)(2,1)}), bf16[1024,2432]{1,0:T(8,128)(2,1)}) %all-gather.3.cloned.1.call-update) | async-done | bytes 4980752 | tf_op jit(solution)/shard_map/all_gather | solution.py:578
  100.5 41.7 %shard_map.305 = (bf16[4,256,1024]{2,1,0:T(8,128)(2,1)}, bf16[4,272,2304]{2,1,0:T(8,128)(2,1)}, bf16[4,256,2304]{2,1,0:T(8,128)(2,1)}, f32[4,256,128]{2,1,0:T(8,...) custom-call(bf16[4,256,1024]{2,1,0:T(8,128)(2,1)} %x_ref.1, ...), custom_call_target="tpu_custom_call" | custom-call | tf_op jit(solution)/shard_map/pallas_call | solution.py:610
  142.2 110.6 %all_to_all.20.received_ref.passing_ref = f32[8,136,1024]{2,1,0:T(8,128)} all-to-all(f32[8,136,1024]{2,1,0:T(8,128)} %bitcast.167), channel_id=1, replica_groups=mesh['dp'=4,'ctx'=8] {'ctx'}, dimensions={0} | all-to-all | bytes 8912896 | tf_op jit(solution)/shard_map/all_to_all | solution.py:644
  263.1 10.7 %shard_map.306.y_ref = f32[4,256,2048]{2,1,0:T(8,128)} custom-call(bf16[4,256,2304]{2,1,0:T(8,128)(2,1)} %get-tuple-element.71.act_ref, f32[4,256,128]{2,1,0:T(8,128)} %get-tuple-element.72.step_ref, f32[4,256,128]{2,1,0:T(8,128)} %get-tuple-element.73.decay_ref, f32[4,256,8]{2,1,0:T(8,128)} %stack.55.marks_ref, f32[4,8,256]{2,1,0:T(8,128)} %broadcast_in_dim.30.segment_ref), custom_call_target="tpu_custom_call" | custom-call | tf_op jit(solution)/shard_map/pallas_call | solution.py:647
  273.8 6.2 fusion.48
  280.0 7.1 reshape.240.out_weight_ref
  287.1 23.7 %all-to-all-done.1 = bf16[8,128,1024]{2,1,0:T(8,128)(2,1)S(1)} async-done(((bf16[8,128,1024]{2,1,0:T(8,128)(2,1)}), bf16[8,128,1024]{2,1,0:T(8,128)(2,1)S(1)}, u32[]{:S(2)}, u32[]{:S(2)}) %all-to-all-start.1) | async-done | bytes 2097184 | tf_op jit(solution)/shard_map/all_to_all | solution.py:672
  312.2 43.0 %shard_map.308 = (bf16[4,256,2048]{2,1,0:T(8,128)(2,1)}, bf16[4,256,2048]{2,1,0:T(8,128)(2,1)}, bf16[4,256,2048]{2,1,0:T(8,128)(2,1)}, bf16[4,2,128,1024]{3,2,1,...) custom-call(bf16[4,256,1024]{2,1,0:T(8,128)(2,1)} %cotangent_ref.1, ...), custom_call_target="tpu_custom_call" | custom-call | tf_op jit(solution)/shard_map/pallas_call | solution.py:677
  355.2 9.0 %convolution_bitcast_fusion.1 = f32[2048,1024]{1,0:T(8,128)} fusion(bf16[4,256,2048]{2,1,0:T(8,128)(2,1)} %get-tuple-element.76, bf16[4,256,1024]{2,1,0:T(8,128)(2,1)S(1)} %copy-done.4), kind=kOutput, calls=%fused_computation.9 | convolution fusion | flops 4294967296 | bytes 14680064 | tf_op jit(solution)/shard_map/nay,nag->yg/dot_general | solution.py:766
  364.2 10.1 %reshape_reshape.3 = f32[2,2,2,2,2,32,2048]{6,5,4,3,2,1,0:T(8,128)} reshape(f32[2048,1024]{1,0:T(8,128)} %convolution_bitcast_fusion.1) | data formatting | bytes 16777216 | tf_op jit(solution)/shard_map/reshape;reshape | solution.py:56
  408.7 7.1 reshape.266
  415.8 26.2 %all-to-all-done.2.received_ref = bf16[8,128,1024]{2,1,0:T(8,128)(2,1)} async-done(((bf16[8,128,1024]{2,1,0:T(8,128)(2,1)}), bf16[8,128,1024]{2,1,0:T(8,128)(2,1)}, u32[]{:S(2)}, u32[]{:S(2)}) %all-to-all-start.2) | async-done | bytes 2097184 | tf_op jit(solution)/shard_map/all_to_all | solution.py:729
  451.7 24.3 %collective-permute-done.19 = f32[2,2,2,32,2048]{4,3,2,1,0:T(8,128)} collective-permute-done((f32[2,2,2,32,2048]{4,3,2,1,0:T(8,128)}, f32[2,2,2,32,2048]{4,3,2,1,0:T(8,128)}, u32[]{:S(2)}, u32[]{:S(2)}) %collective-permute-start.19) | collective-permute-done | bytes 2097184 | tf_op jit(solution)/shard_map/ppermute | solution.py:46
  487.0 5.7 fusion.10
  492.7 15.3 %shard_map.309 = (f32[4,256,2048]{2,1,0:T(8,128)}, f32[4,256,128]{2,1,0:T(8,128)}, f32[4,256,128]{2,1,0:T(8,128)}) custom-call(bf16[4,256,2304]{2,1,0:T(8,128)(2,1)} %get-tuple-element.71.act_ref, bf16[4,256,2048]{2,1,0:T(8,128)(2,1)} %get-tuple-element.79.grad_ssd_ref, f32[4,256,128]{2,1,0:T(8,128)} %get-tuple-element.72.step_ref, ...), custom_call_target="tpu_custom_call" | custom-call | tf_op jit(solution)/shard_map/pallas_call | solution.py:732
  519.6 46.5 %shard_map.311 = (bf16[4,256,2432]{2,1,0:T(8,128)(2,1)}, f32[4,8,2304]{2,1,0:T(8,128)}, f32[4,8,2304]{2,1,0:T(8,128)}, f32[8,2304]{1,0:T(8,128)}, f32[8,128]{1,0:T(8,128)}) custom-call(bf16[4,256,2304]{2,1,0:T(8,128)(2,1)} %get-tuple-element.71.act_ref, bf16[4,272,2304]{2,1,0:T(8,128)(2,1)} %get-tuple-element.78.wide_ref, ...), custom_call_target="tpu_custom_call" | custom-call | tf_op jit(solution)/shard_map/pallas_call | solution.py:777
  578.1 9.1 %fusion.3 = f32[4,256,1024]{2,1,0:T(8,128)S(1)} fusion(bf16[4,256,2432]{2,1,0:T(8,128)(2,1)} %convert_dynamic-update-slice_fusion, bf16[1024,2432]{1,0:T(8,128)(2,1)} %all-gather.3.cloned.1.call-done.weight_ref), kind=kOutput, calls=%fused_computation.7 | convolution fusion | flops 5100273664 | bytes 14155776 | tf_op jit(solution)/shard_map/hou,qu->hoq/dot_general | solution.py:844
  587.3 5.7 convolution_bitcast_fusion
  601.5 6.8 fusion.9
  647.7 21.3 %collective-permute-done.9 = f32[2,2,2,32,1152]{4,3,2,1,0:T(8,128)S(1)} collective-permute-done((f32[2,2,2,32,1152]{4,3,2,1,0:T(8,128)S(1)}, f32[2,2,2,32,1152]{4,3,2,1,0:T(8,128)S(1)}, u32[]{:S(2)}, u32[]{:S(2)}) %collective-permute-start.9) | collective-permute-done | bytes 1179680 | tf_op jit(solution)/shard_map/ppermute | solution.py:46
  669.6 8.5 %collective-permute-done.14 = f32[2,2,2,32,1280]{4,3,2,1,0:T(8,128)S(1)} collective-permute-done((f32[2,2,2,32,1280]{4,3,2,1,0:T(8,128)S(1)}, f32[2,2,2,32,1280]{4,3,2,1,0:T(8,128)S(1)}, u32[]{:S(2)}, u32[]{:S(2)}) %collective-permute-start.14) | collective-permute-done | bytes 1310752 | tf_op jit(solution)/shard_map/ppermute | solution.py:46
  679.3 8.4 %collective-permute-done.10 = f32[2,2,32,1152]{3,2,1,0:T(8,128)S(1)} collective-permute-done((f32[2,2,32,1152]{3,2,1,0:T(8,128)S(1)}, f32[2,2,32,1152]{3,2,1,0:T(8,128)S(1)}, u32[]{:S(2)}, u32[]{:S(2)}) %collective-permute-start.10) | collective-permute-done | bytes 589856 | tf_op jit(solution)/shard_map/ppermute | solution.py:46
  691.5 17.3 %collective-permute-done.11 = f32[2,32,1152]{2,1,0:T(8,128)S(1)} collective-permute-done((f32[2,32,1152]{2,1,0:T(8,128)S(1)}, f32[2,32,1152]{2,1,0:T(8,128)S(1)}, u32[]{:S(2)}, u32[]{:S(2)}) %collective-permute-start.11) | collective-permute-done | bytes 294944 | tf_op jit(solution)/shard_map/ppermute | solution.py:46
  709.0 6.2 collective-permute-done.16
  (301 shorter events, 178.4 us)
Async XLA Ops:
  7.2 71.8 %all-gather.3.cloned.1.call-start = ((), (), s32[]{:S(2)}) async-start(), calls=%async_computation.4 | async-start | bytes 5136384 | tf_op jit(solution)/shard_map/all_gather | solution.py:578
  10.9 262.9 %all-gather.5.cloned.1.call-start = ((), (), s32[]{:S(2)}) async-start(), calls=%async_computation.5 | async-start | bytes 8650752 | tf_op jit(solution)/shard_map/all_gather | solution.py:583
  79.7 12.2 %collective-permute-start.1 = (s32[4,16]{1,0:T(4,128)S(1)}, s32[4,16]{1,0:T(4,128)S(1)}, u32[]{:S(2)}, u32[]{:S(2)}) collective-permute-start(s32[4,16]{1,0:T(4,128)S(1)} %slice.202), channel_id=1, source_target_pairs={{0,1},{1,2},{2,3},{3,4},{4,5},{5,6},{6,7},{8,9},{9,10},{10,11},{11... | collective-permute-start | bytes 776 | tf_op jit(solution)/shard_map/ppermute | solution.py:34
  83.8 16.0 %collective-permute-start = (bf16[4,16,1024]{2,1,0:T(8,128)(2,1)S(1)}, bf16[4,16,1024]{2,1,0:T(8,128)(2,1)S(1)}, u32[]{:S(2)}, u32[]{:S(2)}) collective-permute-start(bf16[4,16,1024]{2,1,0:T(8,128)(2,1)S(1)} %slice.201), channel_id=1, source_target_pairs={{0,1},{1,2},{2,3},{3,4},{4,5},{5,6},{6,7},{8,9},{9,10},{10,11},{11... | collective-permute-start | bytes 393224 | tf_op jit(solution)/shard_map/ppermute | solution.py:34
  258.1 52.7 %all-to-all-start.1 = ((bf16[8,128,1024]{2,1,0:T(8,128)(2,1)}), bf16[8,128,1024]{2,1,0:T(8,128)(2,1)S(1)}, u32[]{:S(2)}, u32[]{:S(2)}) async-start(bf16[8,128,1024]{2,1,0:T(8,128)(2,1)} %get-tuple-element.75), calls=%async_computation.1 | async-start | bytes 4194304 | tf_op jit(solution)/shard_map/all_to_all | solution.py:672
  379.2 14.1 %collective-permute-start.18 = (f32[2,2,2,2,32,2048]{5,4,3,2,1,0:T(8,128)}, f32[2,2,2,2,32,2048]{5,4,3,2,1,0:T(8,128)}, u32[]{:S(2)}, u32[]{:S(2)}) collective-permute-start(f32[2,2,2,2,32,2048]{5,4,3,2,1,0:T(8,128)} %dynamic-slice_bitcast_fusion), channel_id=1, source_target_pairs={{0,8},{8,0},{16,24},{24,16},{1,9},{9,1},{17,25},{25,17},{2,10},{10... | collective-permute-start | bytes 12582920 | tf_op jit(solution)/shard_map/ppermute | solution.py:46
  388.4 12.7 %collective-permute-start.3 = (f32[2,2,2,2,32,2048]{5,4,3,2,1,0:T(8,128)}, f32[2,2,2,2,32,2048]{5,4,3,2,1,0:T(8,128)}, u32[]{:S(2)}, u32[]{:S(2)}) collective-permute-start(f32[2,2,2,2,32,2048]{5,4,3,2,1,0:T(8,128)} %dynamic-slice_bitcast_fusion.1), channel_id=1, source_target_pairs={{0,8},{8,0},{16,24},{24,16},{1,9},{9,1},{17,25},{25,17},{2,10},{10... | collective-permute-start | bytes 12582920 | tf_op jit(solution)/shard_map/ppermute | solution.py:46
  388.9 53.1 %all-to-all-start.2 = ((bf16[8,128,1024]{2,1,0:T(8,128)(2,1)}), bf16[8,128,1024]{2,1,0:T(8,128)(2,1)}, u32[]{:S(2)}, u32[]{:S(2)}) async-start(bf16[8,128,1024]{2,1,0:T(8,128)(2,1)} %bitcast.11), calls=%async_computation.2 | async-start | bytes 4194304 | tf_op jit(solution)/shard_map/all_to_all | solution.py:729
  399.2 76.8 %collective-permute-start.19 = (f32[2,2,2,32,2048]{4,3,2,1,0:T(8,128)}, f32[2,2,2,32,2048]{4,3,2,1,0:T(8,128)}, u32[]{:S(2)}, u32[]{:S(2)}) collective-permute-start(f32[2,2,2,32,2048]{4,3,2,1,0:T(8,128)} %dynamic-slice_bitcast_fusion.4), channel_id=1, source_target_pairs={{0,1},{1,0},{2,3},{3,2},{4,5},{5,4},{6,7},{7,6},{8,9},{9,8},{10,11... | collective-permute-start | bytes 6291464 | tf_op jit(solution)/shard_map/ppermute | solution.py:46
  406.8 73.2 %collective-permute-start.4 = (f32[2,2,2,32,2048]{4,3,2,1,0:T(8,128)}, f32[2,2,2,32,2048]{4,3,2,1,0:T(8,128)}, u32[]{:S(2)}, u32[]{:S(2)}) collective-permute-start(f32[2,2,2,32,2048]{4,3,2,1,0:T(8,128)} %dynamic-slice_bitcast_fusion.5), channel_id=1, source_target_pairs={{0,16},{8,24},{16,0},{24,8},{1,17},{9,25},{17,1},{25,9},{2,18},{10... | collective-permute-start | bytes 6291464 | tf_op jit(solution)/shard_map/ppermute | solution.py:46
  447.1 72.6 %all-to-all-start.3 = ((bf16[8,144,1024]{2,1,0:T(8,128)(2,1)}), bf16[8,144,1024]{2,1,0:T(8,128)(2,1)}, u32[]{:S(2)}, u32[]{:S(2)}) async-start(bf16[8,144,1024]{2,1,0:T(8,128)(2,1)} %shard_map.310), calls=%async_computation.3 | async-start | bytes 4718592 | tf_op jit(solution)/shard_map/all_to_all | solution.py:762
  478.6 31.3 %collective-permute-start.20 = (f32[2,2,32,2048]{3,2,1,0:T(8,128)S(1)}, f32[2,2,32,2048]{3,2,1,0:T(8,128)}, u32[]{:S(2)}, u32[]{:S(2)}) collective-permute-start(f32[2,2,32,2048]{3,2,1,0:T(8,128)S(1)} %dynamic-slice_bitcast_fusion.8), channel_id=1, source_target_pairs={{0,16},{8,24},{16,0},{24,8},{1,17},{9,25},{17,1},{25,9},{2,18},{10... | collective-permute-start | bytes 3145736 | tf_op jit(solution)/shard_map/ppermute | solution.py:46
  484.4 29.5 %collective-permute-start.5 = (f32[2,2,32,2048]{3,2,1,0:T(8,128)}, f32[2,2,32,2048]{3,2,1,0:T(8,128)}, u32[]{:S(2)}, u32[]{:S(2)}) collective-permute-start(f32[2,2,32,2048]{3,2,1,0:T(8,128)} %dynamic-slice_bitcast_fusion.9), channel_id=1, source_target_pairs={{0,1},{1,0},{2,3},{3,2},{4,5},{5,4},{6,7},{7,6},{8,9},{9,8},{10,11... | collective-permute-start | bytes 3145736 | tf_op jit(solution)/shard_map/ppermute | solution.py:46
  512.6 107.8 %collective-permute-start.21 = (f32[2,32,2048]{2,1,0:T(8,128)}, f32[2,32,2048]{2,1,0:T(8,128)}, u32[]{:S(2)}, u32[]{:S(2)}) collective-permute-start(f32[2,32,2048]{2,1,0:T(8,128)} %dynamic-slice_bitcast_fusion.12), channel_id=1, source_target_pairs={{0,4},{1,5},{2,6},{3,7},{4,0},{5,1},{6,2},{7,3},{8,12},{9,13},{10,... | collective-permute-start | bytes 1572872 | tf_op jit(solution)/shard_map/ppermute | solution.py:46
  517.2 111.6 %collective-permute-start.6 = (f32[2,32,2048]{2,1,0:T(8,128)}, f32[2,32,2048]{2,1,0:T(8,128)}, u32[]{:S(2)}, u32[]{:S(2)}) collective-permute-start(f32[2,32,2048]{2,1,0:T(8,128)} %dynamic-slice_bitcast_fusion.13), channel_id=1, source_target_pairs={{0,4},{1,5},{2,6},{3,7},{4,0},{5,1},{6,2},{7,3},{8,12},{9,13},{10,... | collective-permute-start | bytes 1572872 | tf_op jit(solution)/shard_map/ppermute | solution.py:46
  612.8 27.0 %collective-permute-start.8 = (f32[2,2,2,2,32,1152]{5,4,3,2,1,0:T(8,128)}, f32[2,2,2,2,32,1152]{5,4,3,2,1,0:T(8,128)}, u32[]{:S(2)}, u32[]{:S(2)}) collective-permute-start(f32[2,2,2,2,32,1152]{5,4,3,2,1,0:T(8,128)} %dynamic-slice_bitcast_fusion.3), channel_id=1, source_target_pairs={{0,8},{8,0},{16,24},{24,16},{1,9},{9,1},{17,25},{25,17},{2,10},{10... | collective-permute-start | bytes 7077896 | tf_op jit(solution)/shard_map/ppermute | solution.py:46
  616.3 27.9 %collective-permute-start.13 = (f32[2,2,2,2,32,1280]{5,4,3,2,1,0:T(8,128)}, f32[2,2,2,2,32,1280]{5,4,3,2,1,0:T(8,128)}, u32[]{:S(2)}, u32[]{:S(2)}) collective-permute-start(f32[2,2,2,2,32,1280]{5,4,3,2,1,0:T(8,128)} %dynamic-slice_bitcast_fusion.2), channel_id=1, source_target_pairs={{0,8},{8,0},{16,24},{24,16},{1,9},{9,1},{17,25},{25,17},{2,10},{10... | collective-permute-start | bytes 7864328 | tf_op jit(solution)/shard_map/ppermute | solution.py:46
  625.0 14.7 %collective-permute-start.22 = (f32[32,2048]{1,0:T(8,128)S(1)}, f32[32,2048]{1,0:T(8,128)S(1)}, u32[]{:S(2)}, u32[]{:S(2)}) collective-permute-start(f32[32,2048]{1,0:T(8,128)S(1)} %dynamic-slice_bitcast_fusion.16), channel_id=1, source_target_pairs={{0,2},{1,3},{2,0},{3,1},{4,6},{5,7},{6,4},{7,5},{8,10},{9,11},{10,... | collective-permute-start | bytes 786440 | tf_op jit(solution)/shard_map/ppermute | solution.py:46
  634.1 13.5 %collective-permute-start.7 = (f32[32,2048]{1,0:T(8,128)S(1)}, f32[32,2048]{1,0:T(8,128)S(1)}, u32[]{:S(2)}, u32[]{:S(2)}) collective-permute-start(f32[32,2048]{1,0:T(8,128)S(1)} %dynamic-slice_bitcast_fusion.17), channel_id=1, source_target_pairs={{0,2},{1,3},{2,0},{3,1},{4,6},{5,7},{6,4},{7,5},{8,10},{9,11},{10,... | collective-permute-start | bytes 786440 | tf_op jit(solution)/shard_map/ppermute | solution.py:46
  642.8 26.2 %collective-permute-start.9 = (f32[2,2,2,32,1152]{4,3,2,1,0:T(8,128)S(1)}, f32[2,2,2,32,1152]{4,3,2,1,0:T(8,128)S(1)}, u32[]{:S(2)}, u32[]{:S(2)}) collective-permute-start(f32[2,2,2,32,1152]{4,3,2,1,0:T(8,128)S(1)} %dynamic-slice_bitcast_fusion.7), channel_id=1, source_target_pairs={{0,16},{8,24},{16,0},{24,8},{1,17},{9,25},{17,1},{25,9},{2,18},{10... | collective-permute-start | bytes 3538952 | tf_op jit(solution)/shard_map/ppermute | solution.py:46
  646.3 31.8 %collective-permute-start.14 = (f32[2,2,2,32,1280]{4,3,2,1,0:T(8,128)S(1)}, f32[2,2,2,32,1280]{4,3,2,1,0:T(8,128)S(1)}, u32[]{:S(2)}, u32[]{:S(2)}) collective-permute-start(f32[2,2,2,32,1280]{4,3,2,1,0:T(8,128)S(1)} %dynamic-slice_bitcast_fusion.6), channel_id=1, source_target_pairs={{0,1},{1,0},{2,3},{3,2},{4,5},{5,4},{6,7},{7,6},{8,9},{9,8},{10,11... | collective-permute-start | bytes 3932168 | tf_op jit(solution)/shard_map/ppermute | solution.py:46
  669.1 18.6 %collective-permute-start.10 = (f32[2,2,32,1152]{3,2,1,0:T(8,128)S(1)}, f32[2,2,32,1152]{3,2,1,0:T(8,128)S(1)}, u32[]{:S(2)}, u32[]{:S(2)}) collective-permute-start(f32[2,2,32,1152]{3,2,1,0:T(8,128)S(1)} %dynamic-slice_bitcast_fusion.11), channel_id=1, source_target_pairs={{0,1},{1,0},{2,3},{3,2},{4,5},{5,4},{6,7},{7,6},{8,9},{9,8},{10,11... | collective-permute-start | bytes 1769480 | tf_op jit(solution)/shard_map/ppermute | solution.py:46
  687.8 21.0 %collective-permute-start.11 = (f32[2,32,1152]{2,1,0:T(8,128)S(1)}, f32[2,32,1152]{2,1,0:T(8,128)S(1)}, u32[]{:S(2)}, u32[]{:S(2)}) collective-permute-start(f32[2,32,1152]{2,1,0:T(8,128)S(1)} %dynamic-slice_bitcast_fusion.15), channel_id=1, source_target_pairs={{0,4},{1,5},{2,6},{3,7},{4,0},{5,1},{6,2},{7,3},{8,12},{9,13},{10,... | collective-permute-start | bytes 884744 | tf_op jit(solution)/shard_map/ppermute | solution.py:46
  689.6 25.5 %collective-permute-start.16 = (f32[2,32,1280]{2,1,0:T(8,128)S(1)}, f32[2,32,1280]{2,1,0:T(8,128)S(1)}, u32[]{:S(2)}, u32[]{:S(2)}) collective-permute-start(f32[2,32,1280]{2,1,0:T(8,128)S(1)} %dynamic-slice_bitcast_fusion.14), channel_id=1, source_target_pairs={{0,4},{1,5},{2,6},{3,7},{4,0},{5,1},{6,2},{7,3},{8,12},{9,13},{10,... | collective-permute-start | bytes 983048 | tf_op jit(solution)/shard_map/ppermute | solution.py:46
  (55 other events, 856.0 us)
Sparse Core Ops, SparseCore 0:
  11.5 67.3 all-gather.2
  82.5 85.8 all-gather.4

commit v3 on v2

--- a/solution.py
+++ b/solution.py
@@ -38,31 +38,9 @@
     return lax.axis_size(axis).bit_length() - 1
 
 
-def halve(values, axis, bit, dim, sent_type):
-    mine = (lax.axis_index(axis) >> bit) & 1
-    kept = lax.dynamic_index_in_dim(values, mine, dim, keepdims=False)
-    away = lax.dynamic_index_in_dim(values, 1 - mine, dim, keepdims=False).astype(sent_type)
+def swap(values, axis, bit):
     count = lax.axis_size(axis)
-    away = lax.ppermute(away, axis, [(place, place ^ (1 << bit)) for place in range(count)])
-    return kept + away.astype(jnp.float32)
-
-
-def sum_to_owner(values, y_first):
-    dp_bits, ctx_bits = bit_count("dp"), bit_count("ctx")
-    x_bits = dp_bits - 1
-    names = [("dp", bit) for bit in reversed(range(dp_bits))]
-    names += [("ctx", bit) for bit in reversed(range(ctx_bits))]
-    rows = values.shape[0] >> len(names)
-    values = values.reshape((2,) * len(names) + (rows, values.shape[1]))
-    y_part = [("dp", bit) for bit in reversed(range(1, dp_bits))]
-    x_part = [("ctx", bit) for bit in reversed(range(x_bits))]
-    z_part = [("ctx", bit) for bit in reversed(range(x_bits, ctx_bits))]
-    order = [("dp", 0)] + (y_part + x_part if y_first else x_part + y_part) + z_part
-    for item in order:
-        sent_type = jnp.float32
-        values = halve(values, item[0], item[1], names.index(item), sent_type)
-        names.remove(item)
-    return values
+    return lax.ppermute(values, axis, [(place, place ^ (1 << bit)) for place in range(count)])
 
 
 def sum_small(values, shared):
@@ -121,7 +99,7 @@
     return at_row, at_column
 
 
-def kernel_call(body, grid, in_specs, out_specs, out_shape, scratch=()):
+def kernel_call(body, grid, in_specs, out_specs, out_shape, scratch=(), aliases=None):
     return pl.pallas_call(
         body,
         grid=grid,
@@ -129,18 +107,23 @@
         out_specs=out_specs,
         out_shape=out_shape,
         scratch_shapes=list(scratch),
+        input_output_aliases=aliases or {},
         compiler_params=pltpu.CompilerParams(
             dimension_semantics=("arbitrary",) * len(grid), vmem_limit_bytes=VMEM_BYTES
         ),
     )
 
 
-def per_row(*shape):
-    return pl.BlockSpec((1,) + shape, lambda row, *_: (row,) + (0,) * len(shape))
+def per_row(*shape, first=0):
+    return pl.BlockSpec((1,) + shape, lambda row, *_: (row + first,) + (0,) * len(shape))
 
 
 def whole(*shape):
     return pl.BlockSpec(shape, lambda *_: (0,) * len(shape))
+
+
+def untouched():
+    return pl.BlockSpec(memory_space=pl.ANY)
 
 
 def shape_of(shape, dtype):
@@ -178,21 +161,24 @@
 
     normed = normalize(x_ref[0])
     normed_ref[0] = normed
-    rim = dot(normalize(rim_ref[0]), weight_ref[:, :channels])
-    wide_ref[0:8] = rim[8:16].astype(jnp.bfloat16).astype(jnp.float32)
+    normed = jnp.concatenate([normalize(rim_ref[0]), normed], axis=0)
     part = 768 if channels % 768 == 0 else LANES
     for start in range(0, channels, part):
         piece = dot(normed, weight_ref[:, start : start + part]).astype(jnp.bfloat16)
-        wide_ref[8:, start : start + part] = piece.astype(jnp.float32)
-    raw = dot(normed, weight_ref[:, channels:])
+        wide_ref[:, start : start + part] = piece[8:].astype(jnp.float32)
+    raw = dot(normed, weight_ref[:, channels:])[16:]
     raw_ref[0] = raw
+
+    same = [
+        jnp.broadcast_to(marks_ref[0, :, tap : tap + 1], (length, LANES)) for tap in range(3)
+    ]
 
     def convolve(tile, carry):
         at = pl.ds(pl.multiple_of(tile * LANES, LANES), LANES)
         pre = jnp.broadcast_to(conv_ref[4:5, at], (length, LANES))
         for tap in range(3):
             taken = wide_ref[5 + tap : 5 + tap + length, at]
-            pre = pre + conv_ref[tap : tap + 1, at] * taken * marks_ref[0, :, tap : tap + 1]
+            pre = pre + conv_ref[tap : tap + 1, at] * taken * same[tap]
         pre = pre + conv_ref[3:4, at] * wide_ref[8:, at]
         act_ref[0, :, at] = (pre * jax.nn.sigmoid(pre)).astype(jnp.bfloat16)
         wide_out_ref[0, :, at] = jnp.concatenate(
@@ -267,17 +253,19 @@
             y_ref[0, rows, at] = total
 
 
-def carry_forward_kernel(received_ref, low_ref, incoming_ref):
+def carry_forward_kernel(received_ref, held_ref, low_ref, incoming_ref, kept_ref):
     blocks, state = low_ref.shape[0], low_ref.shape[1]
     carried = jnp.zeros(low_ref.shape[1:], jnp.float32)
     for block in range(blocks):
         incoming_ref[block] = carried
         low_ref[block] = carried.astype(jnp.bfloat16)
         passing = received_ref[block, state : state + 1]
-        carried = passing * carried + received_ref[block, :state].astype(jnp.float32)
-
-
-def carry_backward_kernel(received_ref, passing_ref, incoming_ref, send_ref):
+        carried = passing * carried + received_ref[block, :state]
+
+
+def carry_backward_kernel(
+    received_ref, passing_ref, incoming_ref, inner_ref, mixed_ref, gate_ref, send_ref, *kept_refs
+):
     blocks, state = received_ref.shape[0], received_ref.shape[1]
     carried = jnp.zeros(received_ref.shape[1:], jnp.float32)
     for block in reversed(range(blocks)):
@@ -425,33 +413,110 @@
     grad_c_ref[0] = dot(grad_scores, b_state, TN)
 
 
-def exit_kernel(
-    act_ref,
-    wide_ref,
-    grad_ssd_ref,
-    inner_x_ref,
-    inner_b_ref,
-    inner_c_ref,
-    outer_c_ref,
-    leaving_ref,
-    row_term_ref,
-    raw_ref,
-    step_ref,
-    decay_ref,
-    marks_ref,
-    conv_ref,
-    heads_ref,
-    skip_ref,
-    spread_ref,
-    grad_mixer_ref,
-    tail_ref,
-    rim_ref,
-    grad_conv_ref,
-    grad_heads_ref,
-    grad_act_ref,
-    shift_ref,
-    taken_ref,
-):
+def share_kernel(widths, chosen_ref, left_ref, right_ref, *refs):
+    outs = refs[-len(widths) :]
+    start = 0
+    for out_ref, width in zip(outs, widths):
+        out_ref[0] = dot(left_ref[...], right_ref[:, start : start + width], TN)
+        start += width
+
+
+def share_of_product(left, right, chosen, widths, held=None):
+    dp_count = lax.axis_size("dp")
+    left = left.reshape(-1, left.shape[2])
+    right = right.reshape(-1, right.shape[2])
+    tokens, rows = left.shape[0], left.shape[1] // dp_count
+    held = [] if held is None else [held]
+    results = pl.pallas_call(
+        functools.partial(share_kernel, widths),
+        grid_spec=pltpu.PrefetchScalarGridSpec(
+            num_scalar_prefetch=1,
+            grid=(dp_count // 2,),
+            in_specs=[
+                pl.BlockSpec((tokens, rows), lambda y, chosen: (0, 2 * y + chosen[0])),
+                pl.BlockSpec(right.shape, lambda y, chosen: (0, 0)),
+            ]
+            + [untouched()] * len(held),
+            out_specs=[untouched()] * len(held)
+            + [pl.BlockSpec((1, rows, width), lambda y, chosen: (y, 0, 0)) for width in widths],
+        ),
+        out_shape=[shape_of(item.shape, item.dtype) for item in held]
+        + [shape_of((dp_count // 2, rows, width), jnp.float32) for width in widths],
+        input_output_aliases={3: 0} if held else {},
+        compiler_params=pltpu.CompilerParams(vmem_limit_bytes=VMEM_BYTES),
+    )(chosen.reshape(1), left, right, *held)
+    return results[len(held) :], results[0] if held else None
+
+
+def share_parts(left, right, widths, held=None):
+    mine = lax.axis_index("dp") & 1
+    away, _ = share_of_product(left, right, 1 - mine, widths)
+    away = [swap(piece, "dp", 0) for piece in away]
+    kept, held = share_of_product(left, right, mine, widths, held)
+    return list(zip(kept, away)), held
+
+
+class HalvedSum:
+    def __init__(self, parts, y_first):
+        dp_bits, ctx_bits = bit_count("dp"), bit_count("ctx")
+        x_bits = dp_bits - 1
+        self.names = [("dp", bit) for bit in reversed(range(1, dp_bits))]
+        self.names += [("ctx", bit) for bit in reversed(range(ctx_bits))]
+        split = (2,) * len(self.names)
+        self.kept, self.arrived = (part.reshape(split + (-1, part.shape[2])) for part in parts)
+        y_part = [("dp", bit) for bit in reversed(range(1, dp_bits))]
+        x_part = [("ctx", bit) for bit in reversed(range(x_bits))]
+        z_part = [("ctx", bit) for bit in range(x_bits, ctx_bits)]
+        self.order = (y_part + x_part if y_first else x_part + y_part) + z_part
+
+    def step(self):
+        if not self.order:
+            return
+        axis, bit = self.order.pop(0)
+        dim = self.names.index((axis, bit))
+        self.names.remove((axis, bit))
+        mine = (lax.axis_index(axis) >> bit) & 1
+
+        def half(member):
+            first, second = (
+                lax.dynamic_index_in_dim(part, member, dim, keepdims=False)
+                for part in (self.kept, self.arrived)
+            )
+            return first + second
+
+        away = swap(half(1 - mine), axis, bit)
+        self.kept, self.arrived = half(mine), away
+
+    def finish(self):
+        while self.order:
+            self.step()
+        return self.kept + self.arrived
+
+
+def exit_kernel(held_count, *refs):
+    ins, rest = refs[:17], refs[17:]
+    outs, scratch = rest[-8 - held_count : -3 - held_count], rest[-3:]
+    (
+        act_ref,
+        wide_ref,
+        grad_ssd_ref,
+        inner_x_ref,
+        inner_b_ref,
+        inner_c_ref,
+        outer_c_ref,
+        leaving_ref,
+        row_term_ref,
+        raw_ref,
+        step_ref,
+        decay_ref,
+        marks_ref,
+        conv_ref,
+        heads_ref,
+        skip_ref,
+        spread_ref,
+    ) = ins
+    grad_mixer_ref, tail_ref, rim_ref, grad_conv_ref, grad_heads_ref = outs
+    grad_act_ref, shift_ref, taken_ref = scratch
     row = pl.program_id(0)
     length, channels = act_ref.shape[1], act_ref.shape[2]
     inner = spread_ref.shape[1]
@@ -496,13 +561,19 @@
     grad_heads_ref[0:1] += jnp.sum(grad_later * step, axis=0, keepdims=True) * rate
     grad_heads_ref[1:2] += jnp.sum(grad_raw, axis=0, keepdims=True)
 
+    same = [
+        jnp.broadcast_to(marks_ref[0, :, tap : tap + 1], (length, LANES)) for tap in range(3)
+    ]
+    shift_ref[0:8] = jnp.zeros((8, LANES), jnp.float32)
+    shift_ref[length + 8 :] = jnp.zeros((8, LANES), jnp.float32)
+
     def convolve(tile, carry):
         at = pl.ds(pl.multiple_of(tile * LANES, LANES), LANES)
         taken_ref[...] = wide_ref[0, :, at].astype(jnp.float32)
         pre = jnp.broadcast_to(conv_ref[4:5, at], (length, LANES))
         for tap in range(3):
             taken = taken_ref[13 + tap : 13 + tap + length]
-            pre = pre + conv_ref[tap : tap + 1, at] * taken * marks_ref[0, :, tap : tap + 1]
+            pre = pre + conv_ref[tap : tap + 1, at] * taken * same[tap]
         pre = pre + conv_ref[3:4, at] * taken_ref[16:]
         sigmoid = jax.nn.sigmoid(pre)
         grad_pre = grad_act_ref[:, at] * (sigmoid * (1.0 + pre * (1.0 - sigmoid)))
@@ -510,10 +581,8 @@
         grad_conv_ref[3:4, at] += jnp.sum(grad_pre * taken_ref[16:], axis=0, keepdims=True)
         grad_in = grad_pre * conv_ref[3:4, at]
         rim = jnp.zeros((8, LANES), jnp.float32)
-        shift_ref[0:8] = jnp.zeros((8, LANES), jnp.float32)
-        shift_ref[length + 8 :] = jnp.zeros((8, LANES), jnp.float32)
         for tap in range(3):
-            masked = grad_pre * marks_ref[0, :, tap : tap + 1]
+            masked = grad_pre * same[tap]
             taken = taken_ref[13 + tap : 13 + tap + length]
             grad_conv_ref[tap : tap + 1, at] += jnp.sum(masked * taken, axis=0, keepdims=True)
             shift_ref[8 : length + 8] = masked * conv_ref[tap : tap + 1, at]
@@ -659,16 +728,18 @@
     )(activated, step_size, decay_sum, marks, segment_rows)
     tile = min(lanes, 2 * LANES)
     by_lane = lambda rows: pl.BlockSpec((ctx_count, rows, tile), lambda place: (0, 0, place))
-    incoming_low, incoming = kernel_call(
+    incoming_low, incoming, within = kernel_call(
         carry_forward_kernel,
         (lanes // tile,),
-        [by_lane(state_dim + 8)],
-        [by_lane(state_dim), by_lane(state_dim)],
+        [by_lane(state_dim + 8), untouched()],
+        [by_lane(state_dim), by_lane(state_dim), untouched()],
         [
             shape_of((ctx_count, state_dim, lanes), bf16),
             shape_of((ctx_count, state_dim, lanes), f32),
-        ],
-    )(received)
+            shape_of(within.shape, f32),
+        ],
+        aliases={1: 2},
+    )(received, within)
     incoming_low = lax.all_to_all(incoming_low, "ctx", 0, 0, tiled=True)
     incoming_low = incoming_low.reshape(seq_count, groups, state_dim, lanes)
 
@@ -748,99 +819,139 @@
         ],
         [pltpu.VMEM((length, length), f32)],
     )(activated, grad_ssd, step_size, decay_sum, marks, segment_rows)
-    sent = kernel_call(
+    sent, inner_x, mixed, grad_gate = kernel_call(
         carry_backward_kernel,
         (lanes // tile,),
         [
             by_lane(state_dim),
             pl.BlockSpec((ctx_count, 8, tile), lambda place: (0, state_dim // 8, place)),
             by_lane(state_dim),
-        ],
-        by_lane(state_dim + 16),
-        shape_of((ctx_count, state_dim + 16, lanes), bf16),
-    )(grad_received, received, incoming)
+            untouched(),
+            untouched(),
+            untouched(),
+        ],
+        [by_lane(state_dim + 16), untouched(), untouched(), untouched()],
+        [
+            shape_of((ctx_count, state_dim + 16, lanes), bf16),
+            shape_of(inner_x.shape, f32),
+            shape_of(mixed.shape, bf16),
+            shape_of(grad_gate.shape, bf16),
+        ],
+        aliases={3: 1, 4: 2, 5: 3},
+    )(grad_received, received, incoming, inner_x, mixed, grad_gate)
     leaving = lax.all_to_all(sent, "ctx", 0, 0, tiled=True)
     leaving = leaving.reshape(seq_count, groups, state_dim + 16, lanes)
-
-    def join(left, right):
-        return jnp.einsum("nay,nag->yg", left, right, preferred_element_type=f32)
 
     input_float = tokens.astype(f32)
     output = (
         input_float
         + jnp.einsum("exp,pk->exk", mixed, output_weight, preferred_element_type=f32)
     ).astype(bf16)
-    out_sum = sum_to_owner(join(mixed, cotangent).reshape(devices * own_rows, -1), False)
-    gate_sum = sum_to_owner(join(normed, grad_gate), True)
     gate_normed = jnp.einsum("hou,qu->hoq", grad_gate, gate_weight, preferred_element_type=f32)
-
-    grad_mixer, tail, rim, grad_conv, grad_heads = kernel_call(
-        exit_kernel,
-        (seq_count,),
-        [
-            per_row(length, channels),
-            per_row(length + 16, channels),
-            per_row(length, inner_width),
-            per_row(length, inner_width),
-            per_row(length, state_dim),
-            per_row(length, state_dim),
-            per_row(length, state_dim),
-            per_row(groups, state_dim + 16, lanes),
-            per_row(length, LANES),
-            per_row(length, LANES),
-            per_row(length, LANES),
-            per_row(length, LANES),
-            per_row(length, 8),
-            whole(8, channels),
-            whole(8, LANES),
-            whole(8, inner_width),
-            whole(LANES, inner_width),
-        ],
-        [
-            per_row(length, wide_width),
-            per_row(8, channels),
-            per_row(8, channels),
-            whole(8, channels),
-            whole(8, LANES),
-        ],
-        [
+    gate_parts, _ = share_parts(normed, grad_gate, [inner_width])
+    out_parts, _ = share_parts(mixed, cotangent, [model_width])
+    first_sums = [HalvedSum(gate_parts[0], True), HalvedSum(out_parts[0], False)]
+    for item in first_sums:
+        item.step()
+
+    def exit_rows(first, count, held, previous):
+        at_row = functools.partial(per_row, first=first)
+        shapes = [
             shape_of((seq_count, length, wide_width), bf16),
             shape_of((seq_count, 8, channels), f32),
             shape_of((seq_count, 8, channels), f32),
             shape_of((8, channels), f32),
             shape_of((8, LANES), f32),
-        ],
-        [
-            pltpu.VMEM((length, channels), f32),
-            pltpu.VMEM((length + 16, LANES), f32),
-            pltpu.VMEM((length + 16, LANES), f32),
-        ],
-    )(
-        activated,
-        wide_in,
-        grad_ssd,
-        inner_x,
-        inner_b,
-        inner_c,
-        outer_c,
-        leaving,
-        row_term,
-        step_raw,
-        step_size,
-        decay_sum,
-        marks,
-        conv_rows,
-        head_rows,
-        skip_row,
-        spread,
-    )
+        ]
+        aliases = {17 + place: place for place in range(len(previous))}
+        aliases.update(
+            {17 + len(previous) + place: 5 + place for place in range(len(held))}
+        )
+        return kernel_call(
+            functools.partial(exit_kernel, len(held)),
+            (count,),
+            [
+                at_row(length, channels),
+                at_row(length + 16, channels),
+                at_row(length, inner_width),
+                at_row(length, inner_width),
+                at_row(length, state_dim),
+                at_row(length, state_dim),
+                at_row(length, state_dim),
+                at_row(groups, state_dim + 16, lanes),
+                at_row(length, LANES),
+                at_row(length, LANES),
+                at_row(length, LANES),
+                at_row(length, LANES),
+                at_row(length, 8),
+                whole(8, channels),
+                whole(8, LANES),
+                whole(8, inner_width),
+                whole(LANES, inner_width),
+            ]
+            + [untouched()] * (len(previous) + len(held)),
+            [
+                at_row(length, wide_width),
+                at_row(8, channels),
+                at_row(8, channels),
+                whole(8, channels),
+                whole(8, LANES),
+            ]
+            + [untouched()] * len(held),
+            shapes + [shape_of(item.shape, item.dtype) for item in held],
+            [
+                pltpu.VMEM((length, channels), f32),
+                pltpu.VMEM((length + 16, LANES), f32),
+                pltpu.VMEM((length + 16, LANES), f32),
+            ],
+            aliases=aliases,
+        )(
+            activated,
+            wide_in,
+            grad_ssd,
+            inner_x,
+            inner_b,
+            inner_c,
+            outer_c,
+            leaving,
+            row_term,
+            step_raw,
+            step_size,
+            decay_sum,
+            marks,
+            conv_rows,
+            head_rows,
+            skip_row,
+            spread,
+            *previous,
+            *held,
+        )
+
+    held = [item.kept for item in first_sums] + [gate_normed, output]
+    *previous, first_conv, first_heads, kept_gate, kept_out, gate_normed, output = exit_rows(
+        0, seq_count // 2, held, []
+    )
+    for item, kept in zip(first_sums, (kept_gate, kept_out)):
+        item.kept = kept
+        item.step()
+    grad_mixer, tail, rim, grad_conv, grad_heads, kept_gate, kept_out = exit_rows(
+        seq_count // 2, seq_count - seq_count // 2, [item.kept for item in first_sums], previous
+    )
+    for item, kept in zip(first_sums, (kept_gate, kept_out)):
+        item.kept = kept
+        item.step()
+    grad_conv, grad_heads = grad_conv + first_conv, grad_heads + first_heads
     rim_back = shifted(rim[:, : taps - 1].astype(bf16), "ctx", -1).astype(f32)
     tail = tail.at[:, 9 - taps :].add(rim_back).astype(bf16)
     grad_mixer = grad_mixer.at[:, length - 8 :, :channels].set(tail)
-    grad_mixer_weight = join(normed, grad_mixer)
     middle = wide_width // 256 * 128
-    left_sum = sum_to_owner(grad_mixer_weight[:, :middle], True)
-    right_sum = sum_to_owner(grad_mixer_weight[:, middle:], False)
+    (left_parts, right_parts), gate_normed = share_parts(
+        normed, grad_mixer, [middle, wide_width - middle], gate_normed
+    )
+    left_sum, right_sum = HalvedSum(left_parts, True), HalvedSum(right_parts, False)
+    gate_sum, out_sum, left_sum, right_sum = (
+        item.finish() for item in (*first_sums, left_sum, right_sum)
+    )
     grad_normed = gate_normed + jnp.einsum(
         "hou,qu->hoq", grad_mixer, mixer_weight, preferred_element_type=f32
     )

time: 738 us -> 709 us (0.961)
  blocking collectives: 111 us -> 0 us
  waiting for transfers between devices: 218 us -> 316 us
  local copies, waits for them, and re-layouts: 86.4 us -> 41.7 us
  Pallas kernels: 168 us -> 197 us
  matrix products: 40.9 us -> 22.9 us
  other arithmetic: 43.7 us -> 54.5 us
    all_to_all x1 -> x0, blocking collectives: 111 us -> none  [local(): lax.all_to_all(sent.reshape(ctx_count, state_dim + 8, lanes), 'ctx', 0, 0...]
    all_to_all x0 -> x1, waiting for transfers between devices: none -> 103 us  [local(): lax.all_to_all(sent.reshape(ctx_count, state_dim + 8, lanes), 'ctx', 0, 0...]
    pallas_call x1 -> x8, Pallas kernels: 46.5 us -> 83.6 us  [the longest x2 45.3 us: exit_rows(): kernel_call(functools.partial(exit_kernel, len(held)), (count,), [at_row(...]
    ppermute x20, waiting for transfers between devices: 92.3 us -> 63.3 us  [swap(): lax.ppermute(values, axis, [(place, place ^ 1 << bit) for place in range(...]
    squeeze x20 -> x0, local copies, waits for them, and re-layouts: 20.5 us -> none  [halve(): lax.dynamic_index_in_dim(values, 1 - mine, dim, keepdims=False)]
    dot_general x3 -> x0, matrix products: 19.3 us -> none  [join(): return jnp.einsum('nay,nag->yg', left, right, preferred_element_type=f32)]
    all_to_all x1, waiting for transfers between devices: 23.7 us -> 35 us  [local(): incoming_low = lax.all_to_all(incoming_low, 'ctx', 0, 0, tiled=True)]
    another operation x2 -> x1, local copies, waits for them, and re-layouts: 10.2 us -> 0.12 us  [the longest x1 10.1 us: sum_to_owner(): values = values.reshape((2,) * len(names) + (rows, values.shape[1]))]
  transfers between devices with their start and end apart: 33 -> 34, of which waited for: 15 -> 20; matrix products, arithmetic and copies ran while one was open for 18% -> 13% of each run, Pallas kernels for 17% -> 16%
where the time goes in v3:
time: 709 us; the launch traced here: 700 us
  waiting for transfers between devices  316 us (45%)
  Pallas kernels  197 us (28%)
  other arithmetic  54.5 us (8%)
  starting transfers between devices  53.3 us (8%)
  local copies, waits for them, and re-layouts  41.7 us (6%)
  matrix products  22.9 us (3%)
  between operations  15.3 us (2%)
    all_to_all x1, waiting for transfers between devices, local(): lax.all_to_all(sent.reshape(ctx_count, state_dim + 8, lanes), 'ctx', 0, 0...  103 us
    all_gather x1, waiting for transfers between devices, local(): mixer_weight = lax.all_gather(first_send, ('dp', 'ctx'), axis=0, tiled=True)  66.2 us
    ppermute x20, waiting for transfers between devices, swap(): lax.ppermute(values, axis, [(place, place ^ 1 << bit) for place in range(...  63.3 us
    pallas_call x2, Pallas kernels, exit_rows(): kernel_call(functools.partial(exit_kernel, len(held)), (count,), [at_row(...  45.3 us
    pallas_call x1, Pallas kernels, local(): kernel_call(functools.partial(middle_kernel, groups), (seq_count, length...  42.8 us
    pallas_call x6, Pallas kernels, share_of_product(): pl.pallas_call(functools.partial(share_kernel, widths), grid_spec=pltpu.P...  38.2 us
    all_to_all x1, waiting for transfers between devices, local(): incoming_low = lax.all_to_all(incoming_low, 'ctx', 0, 0, tiled=True)  35 us
    pallas_call x1, Pallas kernels, local(): kernel_call(functools.partial(entry_kernel, heads_count), (seq_count,), [...  34.2 us
  transfers between devices with their start and end apart: 34, of which 20 were waited for; matrix products, arithmetic and copies ran while one was open for 13% of the time, Pallas kernels for 16%

profile of v3, /device:TPU:0, one launch (start us, length us, event | category | flops | bytes accessed | tf_op | source)
XLA Modules:
  0.0 700.3 jit_solution(2799896014415067455)
XLA Ops:
  12.7 66.2 %all-gather.3.cloned.1.call-done.weight_ref = bf16[1024,2432]{1,0:T(8,128)(2,1)} async-done(((bf16[32,2432]{1,0:T(8,128)(2,1)}), bf16[1024,2432]{1,0:T(8,128)(2,1)}) %all-gather.3.cloned.1.call-update) | async-done | bytes 4980752 | tf_op jit(solution)/shard_map/all_gather | solution.py:647
  97.7 34.2 %shard_map.305 = (bf16[4,256,1024]{2,1,0:T(8,128)(2,1)}, bf16[4,272,2304]{2,1,0:T(8,128)(2,1)}, bf16[4,256,2304]{2,1,0:T(8,128)(2,1)}, f32[4,256,128]{2,1,0:T(8,...) custom-call(bf16[4,256,1024]{2,1,0:T(8,128)(2,1)} %x_ref.1, ...), custom_call_target="tpu_custom_call" | custom-call | tf_op jit(solution)/shard_map/pallas_call | solution.py:679
  137.0 10.7 %shard_map.306.held_ref = f32[4,256,2048]{2,1,0:T(8,128)} custom-call(bf16[4,256,2304]{2,1,0:T(8,128)(2,1)} %get-tuple-element.90.act_ref.refs_0_, f32[4,256,128]{2,1,0:T(8,128)} %get-tuple-element.95.step_ref.refs_10_, f32[4,256,128]{2,1,0:T(8,128)} %get-tuple-element.96.decay_ref.refs_11_, f32[4,256,8]{2,1,0:T(8,128)} %stack.55.marks_ref.refs_12_, ...), custom_call_target="tpu_custom_call" | custom-call | tf_op jit(solution)/shard_map/pallas_call | solution.py:716
  147.7 102.5 %all-to-all-done.received_ref.passing_ref = f32[8,136,1024]{2,1,0:T(8,128)} async-done(((f32[8,136,1024]{2,1,0:T(8,128)}), f32[8,136,1024]{2,1,0:T(8,128)}, u32[]{:S(2)}, u32[]{:S(2)}) %all-to-all-start) | async-done | bytes 4456480 | tf_op jit(solution)/shard_map/all_to_all | solution.py:713
  266.0 7.1 %reshape.332.out_weight_ref = bf16[2048,1024]{1,0:T(8,128)(2,1)} reshape(bf16[1024,2048]{1,0:T(8,128)(2,1)} %get-tuple-element.241) | data formatting | bytes 8388608 | tf_op jit(solution)/shard_map/reshape | solution.py:654
  273.1 35.0 %all-to-all-done.1 = bf16[8,128,1024]{2,1,0:T(8,128)(2,1)S(1)} async-done(((bf16[8,128,1024]{2,1,0:T(8,128)(2,1)}), bf16[8,128,1024]{2,1,0:T(8,128)(2,1)S(1)}, u32[]{:S(2)}, u32[]{:S(2)}) %all-to-all-start.1) | async-done | bytes 2097184 | tf_op jit(solution)/shard_map/all_to_all | solution.py:743
  309.5 42.8 %shard_map.308 = (bf16[4,256,2048]{2,1,0:T(8,128)(2,1)}, bf16[4,256,2048]{2,1,0:T(8,128)(2,1)}, bf16[4,256,2048]{2,1,0:T(8,128)(2,1)}, bf16[4,2,128,1024]{3,2,1,...) custom-call(bf16[4,256,1024]{2,1,0:T(8,128)(2,1)} %cotangent_ref.1, ...), custom_call_target="tpu_custom_call" | custom-call | tf_op jit(solution)/shard_map/pallas_call | solution.py:748
  356.0 15.2 %shard_map.309 = (f32[4,256,2048]{2,1,0:T(8,128)}, f32[4,256,128]{2,1,0:T(8,128)}, f32[4,256,128]{2,1,0:T(8,128)}) custom-call(bf16[4,256,2304]{2,1,0:T(8,128)(2,1)} %get-tuple-element.90.act_ref.refs_0_, bf16[4,256,2048]{2,1,0:T(8,128)(2,1)} %get-tuple-element.99.grad_ssd_ref.refs_2_, f32[4,256,128]{2,1,0:T(8,128)} %get-tuple-element.95.step_ref.refs_10_, ...), custom_call_target="tpu_custom_call" | custom-call | tf_op jit(solution)/shard_map/pallas_call | solution.py:803
  371.2 33.2 %all-to-all-done.2.received_ref = bf16[8,128,1024]{2,1,0:T(8,128)(2,1)S(1)} async-done(((bf16[8,128,1024]{2,1,0:T(8,128)(2,1)}), bf16[8,128,1024]{2,1,0:T(8,128)(2,1)S(1)}, u32[]{:S(2)}, u32[]{:S(2)}) %all-to-all-start.2) | async-done | bytes 2097184 | tf_op jit(solution)/shard_map/all_to_all | solution.py:800
  416.7 6.3 shard_map.312
  429.4 7.1 %reshape.370 = bf16[2048,1024,1]{1,0,2:T(8,128)(2,1)} reshape(bf16[1024,2048]{1,0:T(8,128)(2,1)} %get-tuple-element.241) | data formatting | bytes 8388608 | tf_op jit(solution)/shard_map/reshape | solution.py:654
  438.4 6.3 shard_map.311
  450.6 6.9 fusion.14
  483.0 22.7 %shard_map.315 = (bf16[4,256,2432]{2,1,0:T(8,128)(2,1)}, f32[4,8,2304]{2,1,0:T(8,128)}, f32[4,8,2304]{2,1,0:T(8,128)}, f32[8,2304]{1,0:T(8,128)}, f32[8,128]{1,0...) custom-call(bf16[4,256,2304]{2,1,0:T(8,128)(2,1)} %get-tuple-element, ...), custom_call_target="tpu_custom_call", output_to_operand_aliasing={{5}: (17, {}), {6}: (18, {}), {7}: (19, {}), {8}: (20, {})} | custom-call | tf_op jit(solution)/shard_map/pallas_call | solution.py:870
  505.8 7.4 %collective-permute-done.4 = f32[2,2,2,32,2048]{4,3,1,0,2:T(8,128)} collective-permute-done((f32[2,2,2,32,2048]{4,3,1,0,2:T(8,128)}, f32[2,2,2,32,2048]{4,3,1,0,2:T(8,128)}, u32[]{:S(2)}, u32[]{:S(2)}) %collective-permute-start.4) | collective-permute-done | bytes 2097184 | tf_op jit(solution)/shard_map/ppermute | solution.py:43
  520.5 22.6 %shard_map.316 = (bf16[4,256,2432]{2,1,0:T(8,128)(2,1)}, f32[4,8,2304]{2,1,0:T(8,128)}, f32[4,8,2304]{2,1,0:T(8,128)}, f32[8,2304]{1,0:T(8,128)}, f32[8,128]{1,0...) custom-call(bf16[4,256,2304]{2,1,0:T(8,128)(2,1)} %get-tuple-element, ...), custom_call_target="tpu_custom_call", output_to_operand_aliasing={{0}: (17, {}), {1}: (18, {}), {2}: (19, {}), {5}: (20, {}),... | custom-call | tf_op jit(solution)/shard_map/pallas_call | solution.py:870
  551.8 7.0 %shard_map.317 = (f32[4,256,1024]{2,1,0:T(8,128)}, f32[2,256,1152]{2,1,0:T(8,128)}, f32[2,256,1280]{2,1,0:T(8,128)}) custom-call(s32[1]{0:T(128)} %bitcast.12.chosen_ref, bf16[1024,1024]{1,0:T(8,128)(2,1)} %bitcast.194, bf16[1024,2432]{1,0:T(8,128)(2,1)} %bitcast.196, f32[4,256,1024]{2,1,0:T(8,128)} %get-tuple-element.123.refs_0_), custom_call_target="tpu_custom_call", output_to_operand_aliasing={{0}: (3, {})} | custom-call | tf_op jit(solution)/shard_map/pallas_call | solution.py:430
  558.8 11.1 %fusion.9 = (f32[1024]{0:T(1024)S(1)}, f32[4,256]{1,0:T(4,128)S(1)}, f32[4,256,1024]{2,1,0:T(8,128)}) fusion(bf16[4,256,1024]{2,1,0:T(8,128)(2,1)} %x_ref.1, f32[4,256]{1,0:T(4,128)S(1)} %add_rsqrt_fusion, f32[4,256,1024]{2,1,0:T(8,128)} %get-tuple-element.124, f32[1024]{0:T(1024)S(1)} %slice.242, bf16[4,256,2432]{2,1,0:T(8,128)(2,1)S(1)} %copy-done, ...), kind=kOutput, calls=%fused_computation.12 | convolution fusion | flops 5108660224 | bytes 20463616 | tf_op jit(solution)/shard_map/hou,qu->hoq/dot_general | solution.py:955
  582.6 7.0 shard_map.318
  591.8 6.2 fusion.8
  598.0 7.1 %collective-permute-done.27 = f32[552]{0:T(1024)S(1)} collective-permute-done((f32[552]{0:T(1024)S(1)}, f32[552]{0:T(1024)S(1)}, u32[]{:S(2)}, u32[]{:S(2)}) %collective-permute-start.27) | collective-permute-done | bytes 2240 | tf_op jit(solution)/shard_map/ppermute | solution.py:57
  613.1 10.3 %collective-permute-done.21 = f32[2,64,1024]{2,1,0:T(8,128)} collective-permute-done((f32[2,64,1024]{2,1,0:T(8,128)}, f32[2,64,1024]{2,1,0:T(8,128)}, u32[]{:S(2)}, u32[]{:S(2)}) %collective-permute-start.21) | collective-permute-done | bytes 524320 | tf_op jit(solution)/shard_map/ppermute | solution.py:43
  638.2 12.1 %collective-permute-done.11 = f32[2,2,2,32,1152]{4,3,0,1,2:T(8,128)S(1)} collective-permute-done((f32[2,2,2,32,1152]{4,3,0,1,2:T(8,128)S(1)}, f32[2,2,2,32,1152]{4,3,0,1,2:T(8,128)S(1)}, u32[]{:S(2)}, u32[]{:S(2)}) %collective-permute-start.11) | collective-permute-done | bytes 1179680 | tf_op jit(solution)/shard_map/ppermute | solution.py:43
  651.8 11.0 %collective-permute-done.16 = f32[2,2,2,32,1280]{4,3,1,2,0:T(8,128)S(1)} collective-permute-done((f32[2,2,2,32,1280]{4,3,1,2,0:T(8,128)S(1)}, f32[2,2,2,32,1280]{4,3,1,2,0:T(8,128)S(1)}, u32[]{:S(2)}, u32[]{:S(2)}) %collective-permute-start.16) | collective-permute-done | bytes 1310752 | tf_op jit(solution)/shard_map/ppermute | solution.py:43
  (274 shorter events, 186.9 us)
Async XLA Ops:
  7.2 71.8 %all-gather.3.cloned.1.call-start = ((), (), s32[]{:S(2)}) async-start(), calls=%async_computation.4 | async-start | bytes 5136384 | tf_op jit(solution)/shard_map/all_gather | solution.py:647
  10.9 248.9 %all-gather.5.cloned.1.call-start = ((), (), s32[]{:S(2)}) async-start(), calls=%async_computation.5 | async-start | bytes 8650752 | tf_op jit(solution)/shard_map/all_gather | solution.py:652
  83.1 13.8 %collective-permute-start = (bf16[4,16,1024]{2,1,0:T(8,128)(2,1)S(1)}, bf16[4,16,1024]{2,1,0:T(8,128)(2,1)S(1)}, u32[]{:S(2)}, u32[]{:S(2)}) collective-permute-start(bf16[4,16,1024]{2,1,0:T(8,128)(2,1)S(1)} %slice.195), channel_id=1, source_target_pairs={{0,1},{1,2},{2,3},{3,4},{4,5},{5,6},{6,7},{8,9},{9,10},{10,11},{11... | collective-permute-start | bytes 393224 | tf_op jit(solution)/shard_map/ppermute | solution.py:34
  131.8 118.4 %all-to-all-start = ((f32[8,136,1024]{2,1,0:T(8,128)}), f32[8,136,1024]{2,1,0:T(8,128)}, u32[]{:S(2)}, u32[]{:S(2)}) async-start(f32[8,136,1024]{2,1,0:T(8,128)} %bitcast.211), calls=%async_computation | async-start | bytes 8912896 | tf_op jit(solution)/shard_map/all_to_all | solution.py:713
  255.6 52.5 %all-to-all-start.1 = ((bf16[8,128,1024]{2,1,0:T(8,128)(2,1)}), bf16[8,128,1024]{2,1,0:T(8,128)(2,1)S(1)}, u32[]{:S(2)}, u32[]{:S(2)}) async-start(bf16[8,128,1024]{2,1,0:T(8,128)(2,1)} %get-tuple-element.98), calls=%async_computation.1 | async-start | bytes 4194304 | tf_op jit(solution)/shard_map/all_to_all | solution.py:743
  352.3 52.1 %all-to-all-start.2 = ((bf16[8,128,1024]{2,1,0:T(8,128)(2,1)}), bf16[8,128,1024]{2,1,0:T(8,128)(2,1)S(1)}, u32[]{:S(2)}, u32[]{:S(2)}) async-start(bf16[8,128,1024]{2,1,0:T(8,128)(2,1)} %bitcast.214), calls=%async_computation.2 | async-start | bytes 4194304 | tf_op jit(solution)/shard_map/all_to_all | solution.py:800
  416.7 33.8 %collective-permute-start.3 = (f32[2,512,1024]{2,1,0:T(8,128)}, f32[2,512,1024]{2,1,0:T(8,128)}, u32[]{:S(2)}, u32[]{:S(2)}) collective-permute-start(f32[2,512,1024]{2,1,0:T(8,128)} %shard_map.314), channel_id=1, source_target_pairs={{0,8},{8,0},{16,24},{24,16},{1,9},{9,1},{17,25},{25,17},{2,10},{10... | collective-permute-start | bytes 12582920 | tf_op jit(solution)/shard_map/ppermute | solution.py:43
  423.0 36.5 %collective-permute-start.2 = (f32[2,256,2048]{2,1,0:T(8,128)}, f32[2,256,2048]{2,1,0:T(8,128)}, u32[]{:S(2)}, u32[]{:S(2)}) collective-permute-start(f32[2,256,2048]{2,1,0:T(8,128)} %shard_map.312), channel_id=1, source_target_pairs={{0,8},{8,0},{16,24},{24,16},{1,9},{9,1},{17,25},{25,17},{2,10},{10... | collective-permute-start | bytes 12582920 | tf_op jit(solution)/shard_map/ppermute | solution.py:43
  423.5 58.1 %all-to-all-start.3 = ((bf16[8,144,1024]{2,1,0:T(8,128)(2,1)}), bf16[8,144,1024]{2,1,0:T(8,128)(2,1)S(1)}, u32[]{:S(2)}, u32[]{:S(2)}) async-start(bf16[8,144,1024]{2,1,0:T(8,128)(2,1)} %get-tuple-element.109), calls=%async_computation.3 | async-start | bytes 4718592 | tf_op jit(solution)/shard_map/all_to_all | solution.py:842
  457.5 59.7 %collective-permute-start.5 = (f32[2,2,2,64,1024]{4,3,2,1,0:T(8,128)}, f32[2,2,2,64,1024]{4,3,2,1,0:T(8,128)}, u32[]{:S(2)}, u32[]{:S(2)}) collective-permute-start(f32[2,2,2,64,1024]{4,3,2,1,0:T(8,128)} %get-tuple-element.239), channel_id=1, source_target_pairs={{0,1},{1,0},{2,3},{3,2},{4,5},{5,4},{6,7},{7,6},{8,9},{9,8},{10,11... | collective-permute-start | bytes 6291464 | tf_op jit(solution)/shard_map/ppermute | solution.py:43
  466.0 47.2 %collective-permute-start.4 = (f32[2,2,2,32,2048]{4,3,1,0,2:T(8,128)}, f32[2,2,2,32,2048]{4,3,1,0,2:T(8,128)}, u32[]{:S(2)}, u32[]{:S(2)}) collective-permute-start(f32[2,2,2,32,2048]{4,3,1,0,2:T(8,128)} %fusion.16), channel_id=1, source_target_pairs={{0,16},{8,24},{16,0},{24,8},{1,17},{9,25},{17,1},{25,9},{2,18},{10... | collective-permute-start | bytes 6291464 | tf_op jit(solution)/shard_map/ppermute | solution.py:43
  578.6 27.3 %collective-permute-start.20 = (f32[2,2,64,1024]{3,2,1,0:T(8,128)}, f32[2,2,64,1024]{3,2,1,0:T(8,128)}, u32[]{:S(2)}, u32[]{:S(2)}) collective-permute-start(f32[2,2,64,1024]{3,2,1,0:T(8,128)} %get-tuple-element.243), channel_id=1, source_target_pairs={{0,16},{8,24},{16,0},{24,8},{1,17},{9,25},{17,1},{25,9},{2,18},{10... | collective-permute-start | bytes 3145736 | tf_op jit(solution)/shard_map/ppermute | solution.py:43
  580.1 31.1 %collective-permute-start.7 = (f32[2,2,32,2048]{3,2,1,0:T(8,128)}, f32[2,2,32,2048]{3,2,1,0:T(8,128)}, u32[]{:S(2)}, u32[]{:S(2)}) collective-permute-start(f32[2,2,32,2048]{3,2,1,0:T(8,128)} %get-tuple-element.245), channel_id=1, source_target_pairs={{0,1},{1,0},{2,3},{3,2},{4,5},{5,4},{6,7},{7,6},{8,9},{9,8},{10,11... | collective-permute-start | bytes 3145736 | tf_op jit(solution)/shard_map/ppermute | solution.py:43
  589.6 35.4 %collective-permute-start.10 = (f32[2,256,1152]{2,1,0:T(8,128)}, f32[2,256,1152]{2,1,0:T(8,128)}, u32[]{:S(2)}, u32[]{:S(2)}) collective-permute-start(f32[2,256,1152]{2,1,0:T(8,128)} %get-tuple-element.127), channel_id=1, source_target_pairs={{0,8},{8,0},{16,24},{24,16},{1,9},{9,1},{17,25},{25,17},{2,10},{10... | collective-permute-start | bytes 7077896 | tf_op jit(solution)/shard_map/ppermute | solution.py:43
  589.6 38.1 %collective-permute-start.15 = (f32[2,256,1280]{2,1,0:T(8,128)}, f32[2,256,1280]{2,1,0:T(8,128)}, u32[]{:S(2)}, u32[]{:S(2)}) collective-permute-start(f32[2,256,1280]{2,1,0:T(8,128)} %get-tuple-element.129), channel_id=1, source_target_pairs={{0,8},{8,0},{16,24},{24,16},{1,9},{9,1},{17,25},{25,17},{2,10},{10... | collective-permute-start | bytes 7864328 | tf_op jit(solution)/shard_map/ppermute | solution.py:43
  590.4 14.8 %collective-permute-start.27 = (f32[552]{0:T(1024)S(1)}, f32[552]{0:T(1024)S(1)}, u32[]{:S(2)}, u32[]{:S(2)}) collective-permute-start(f32[552]{0:T(1024)S(1)} %pad_maximum_fusion.8), channel_id=1, source_target_pairs={{0,1},{1,0},{2,3},{3,2},{4,5},{5,4},{6,7},{7,6},{8,9},{9,8},{10,11... | collective-permute-start | bytes 6632 | tf_op jit(solution)/shard_map/ppermute | solution.py:57
  608.2 15.2 %collective-permute-start.21 = (f32[2,64,1024]{2,1,0:T(8,128)}, f32[2,64,1024]{2,1,0:T(8,128)}, u32[]{:S(2)}, u32[]{:S(2)}) collective-permute-start(f32[2,64,1024]{2,1,0:T(8,128)} %get-tuple-element.257), channel_id=1, source_target_pairs={{0,2},{1,3},{2,0},{3,1},{4,6},{5,7},{6,4},{7,5},{8,10},{9,11},{10,... | collective-permute-start | bytes 1572872 | tf_op jit(solution)/shard_map/ppermute | solution.py:43
  612.5 25.4 %collective-permute-start.8 = (f32[2,32,2048]{2,1,0:T(8,128)S(1)}, f32[2,32,2048]{2,1,0:T(8,128)S(1)}, u32[]{:S(2)}, u32[]{:S(2)}) collective-permute-start(f32[2,32,2048]{2,1,0:T(8,128)S(1)} %get-tuple-element.259), channel_id=1, source_target_pairs={{0,2},{1,3},{2,0},{3,1},{4,6},{5,7},{6,4},{7,5},{8,10},{9,11},{10,... | collective-permute-start | bytes 1572872 | tf_op jit(solution)/shard_map/ppermute | solution.py:43
  624.4 50.9 %collective-permute-start.22 = (f32[64,1024]{1,0:T(8,128)S(1)}, f32[64,1024]{1,0:T(8,128)S(1)}, u32[]{:S(2)}, u32[]{:S(2)}) collective-permute-start(f32[64,1024]{1,0:T(8,128)S(1)} %fusion.26), channel_id=1, source_target_pairs={{0,4},{1,5},{2,6},{3,7},{4,0},{5,1},{6,2},{7,3},{8,12},{9,13},{10,... | collective-permute-start | bytes 786440 | tf_op jit(solution)/shard_map/ppermute | solution.py:43
  627.1 23.2 %collective-permute-start.11 = (f32[2,2,2,32,1152]{4,3,0,1,2:T(8,128)S(1)}, f32[2,2,2,32,1152]{4,3,0,1,2:T(8,128)S(1)}, u32[]{:S(2)}, u32[]{:S(2)}) collective-permute-start(f32[2,2,2,32,1152]{4,3,0,1,2:T(8,128)S(1)} %fusion.18), channel_id=1, source_target_pairs={{0,16},{8,24},{16,0},{24,8},{1,17},{9,25},{17,1},{25,9},{2,18},{10... | collective-permute-start | bytes 3538952 | tf_op jit(solution)/shard_map/ppermute | solution.py:43
  631.0 31.8 %collective-permute-start.16 = (f32[2,2,2,32,1280]{4,3,1,2,0:T(8,128)S(1)}, f32[2,2,2,32,1280]{4,3,1,2,0:T(8,128)S(1)}, u32[]{:S(2)}, u32[]{:S(2)}) collective-permute-start(f32[2,2,2,32,1280]{4,3,1,2,0:T(8,128)S(1)} %fusion.17), channel_id=1, source_target_pairs={{0,1},{1,0},{2,3},{3,2},{4,5},{5,4},{6,7},{7,6},{8,9},{9,8},{10,11... | collective-permute-start | bytes 3932168 | tf_op jit(solution)/shard_map/ppermute | solution.py:43
  637.9 25.7 %collective-permute-start.9 = (f32[32,2048]{1,0:T(8,128)S(1)}, f32[32,2048]{1,0:T(8,128)S(1)}, u32[]{:S(2)}, u32[]{:S(2)}) collective-permute-start(f32[32,2048]{1,0:T(8,128)S(1)} %fusion.27), channel_id=1, source_target_pairs={{0,4},{1,5},{2,6},{3,7},{4,0},{5,1},{6,2},{7,3},{8,12},{9,13},{10,... | collective-permute-start | bytes 786440 | tf_op jit(solution)/shard_map/ppermute | solution.py:43
  650.5 19.2 %collective-permute-start.12 = (f32[2,2,32,1152]{3,2,0,1:T(8,128)S(1)}, f32[2,2,32,1152]{3,2,0,1:T(8,128)S(1)}, u32[]{:S(2)}, u32[]{:S(2)}) collective-permute-start(f32[2,2,32,1152]{3,2,0,1:T(8,128)S(1)} %get-tuple-element.269), channel_id=1, source_target_pairs={{0,1},{1,0},{2,3},{3,2},{4,5},{5,4},{6,7},{7,6},{8,9},{9,8},{10,11... | collective-permute-start | bytes 1769480 | tf_op jit(solution)/shard_map/ppermute | solution.py:43
  663.0 10.7 %collective-permute-start.17 = (f32[2,2,32,1280]{3,2,0,1:T(8,128)S(1)}, f32[2,2,32,1280]{3,2,0,1:T(8,128)S(1)}, u32[]{:S(2)}, u32[]{:S(2)}) collective-permute-start(f32[2,2,32,1280]{3,2,0,1:T(8,128)S(1)} %get-tuple-element.263), channel_id=1, source_target_pairs={{0,16},{8,24},{16,0},{24,8},{1,17},{9,25},{17,1},{25,9},{2,18},{10... | collective-permute-start | bytes 1966088 | tf_op jit(solution)/shard_map/ppermute | solution.py:43
  (50 other events, 819.1 us)
Sparse Core Ops, SparseCore 0:
  11.5 67.3 all-gather.2
  82.5 107.1 all-gather.4

commit v4 on v3

--- a/solution.py
+++ b/solution.py
@@ -141,6 +141,7 @@
     heads_ref,
     spread_ref,
     normed_ref,
+    marks_out_ref,
     wide_out_ref,
     act_ref,
     raw_ref,
@@ -153,6 +154,8 @@
     inner, channels = spread_ref.shape[1], act_ref.shape[2]
     state = (channels - inner) // 2
     gain = gain_ref[0:1]
+    marks = marks_ref[0].T
+    marks_out_ref[0] = marks
 
     def normalize(values):
         values = values.astype(jnp.float32)
@@ -170,7 +173,7 @@
     raw_ref[0] = raw
 
     same = [
-        jnp.broadcast_to(marks_ref[0, :, tap : tap + 1], (length, LANES)) for tap in range(3)
+        jnp.broadcast_to(marks[:, tap : tap + 1], (length, LANES)) for tap in range(3)
     ]
 
     def convolve(tile, carry):
@@ -198,13 +201,13 @@
     decay = dot(lower, step * heads_ref[1:2], precision=lax.Precision.HIGHEST)
     decay_ref[0] = decay
     last = decay[length - 1 : length]
-    end_weight = jnp.exp(last - decay) * marks_ref[0, :, 4:5] * step
+    end_weight = jnp.exp(last - decay) * marks[:, 4:5] * step
     spread = spread_ref[...]
     scaled = (spread_heads(end_weight, spread) * act_ref[0, :, :inner].astype(jnp.float32)).astype(
         jnp.bfloat16
     )
     states = dot(act_ref[0, :, inner : inner + state], scaled, TN)
-    passing = jnp.exp(last) * marks_ref[0, length - 1 : length, 3:4]
+    passing = jnp.exp(last) * marks[length - 1 : length, 3:4]
     passing = spread_heads(jnp.broadcast_to(passing, (8, LANES)), spread)
     groups, lanes = send_ref.shape[1], send_ref.shape[3]
     for group in range(groups):
@@ -264,7 +267,7 @@
 
 
 def carry_backward_kernel(
-    received_ref, passing_ref, incoming_ref, inner_ref, mixed_ref, gate_ref, send_ref, *kept_refs
+    received_ref, passing_ref, incoming_ref, inner_ref, choice_ref, send_ref, *kept_refs
 ):
     blocks, state = received_ref.shape[0], received_ref.shape[1]
     carried = jnp.zeros(received_ref.shape[1:], jnp.float32)
@@ -444,15 +447,14 @@
         + [shape_of((dp_count // 2, rows, width), jnp.float32) for width in widths],
         input_output_aliases={3: 0} if held else {},
         compiler_params=pltpu.CompilerParams(vmem_limit_bytes=VMEM_BYTES),
-    )(chosen.reshape(1), left, right, *held)
+    )(chosen, left, right, *held)
     return results[len(held) :], results[0] if held else None
 
 
-def share_parts(left, right, widths, held=None):
-    mine = lax.axis_index("dp") & 1
-    away, _ = share_of_product(left, right, 1 - mine, widths)
+def share_parts(left, right, widths, choice, held=None):
+    away, _ = share_of_product(left, right, choice[1:], widths)
     away = [swap(piece, "dp", 0) for piece in away]
-    kept, held = share_of_product(left, right, mine, widths, held)
+    kept, held = share_of_product(left, right, choice[:1], widths, held)
     return list(zip(kept, away)), held
 
 
@@ -658,14 +660,18 @@
     gain_vector = small[:, conv.size : conv.size + gains.size].reshape(-1).astype(f32)
     gain_in, gain_out = gain_vector[:model_width], gain_vector[model_width:]
 
-    rim_x, rim_segment = shifted((tokens[:, length - 16 :], segments[:, length - 16 :]), "ctx", 1)
+    rim_send = tokens[:, length - 16 :]
+    tail_segments = segments[:, None, length - 16 :].astype(bf16)
+    rim_send = rim_send.at[:, :1, :16].set(tail_segments)
+    rim_x = shifted(rim_send, "ctx", 1)
+    rim_segment = rim_x[:, 0, :16].astype(jnp.int32)
     rim_segment = jnp.where(lax.axis_index("ctx") == 0, -1, rim_segment)
     wide_segment = jnp.concatenate([rim_segment, segments], axis=1)
     marks = [wide_segment[:, 13 + tap : 13 + tap + length] == segments for tap in range(3)]
     marks.append(segments == rim_segment[:, 15:])
     marks.append(segments == segments[:, length - 1 :])
     marks = [mark.astype(f32) for mark in marks] + [segments.astype(f32)]
-    marks = jnp.stack(marks + [jnp.zeros_like(marks[0])] * 2, axis=2)
+    marks = jnp.stack(marks + [jnp.zeros_like(marks[0])] * 2, axis=1)
     segment_rows = jnp.broadcast_to(segments.astype(f32)[:, None], (seq_count, 8, length))
     head_rows = jnp.stack([heads[2], -jnp.exp(heads[0])])
     head_rows = jnp.pad(head_rows, ((0, 6), (0, LANES - heads_count)))
@@ -676,13 +682,13 @@
     gain_rows = jnp.broadcast_to(gain_in, (8, model_width))
     gate_rows = jnp.broadcast_to(gain_out, (8, inner_width))
 
-    normed, wide_in, activated, step_raw, step_size, decay_sum, sent = kernel_call(
+    normed, marks, wide_in, activated, step_raw, step_size, decay_sum, sent = kernel_call(
         functools.partial(entry_kernel, heads_count),
         (seq_count,),
         [
             per_row(length, model_width),
             per_row(16, model_width),
-            per_row(length, 8),
+            per_row(8, length),
             whole(model_width, wide_width),
             whole(8, model_width),
             whole(8, channels),
@@ -691,6 +697,7 @@
         ],
         [
             per_row(length, model_width),
+            per_row(length, 8),
             per_row(length + 16, channels),
             per_row(length, channels),
             per_row(length, LANES),
@@ -700,6 +707,7 @@
         ],
         [
             shape_of((seq_count, length, model_width), bf16),
+            shape_of((seq_count, length, 8), f32),
             shape_of((seq_count, length + 16, channels), bf16),
             shape_of((seq_count, length, channels), bf16),
             shape_of((seq_count, length, LANES), f32),
@@ -819,7 +827,9 @@
         ],
         [pltpu.VMEM((length, length), f32)],
     )(activated, grad_ssd, step_size, decay_sum, marks, segment_rows)
-    sent, inner_x, mixed, grad_gate = kernel_call(
+    mine = lax.axis_index("dp") & 1
+    choice = jnp.stack([mine, 1 - mine]).astype(jnp.int32)
+    sent, inner_x, choice = kernel_call(
         carry_backward_kernel,
         (lanes // tile,),
         [
@@ -828,17 +838,15 @@
             by_lane(state_dim),
             untouched(),
             untouched(),
-            untouched(),
-        ],
-        [by_lane(state_dim + 16), untouched(), untouched(), untouched()],
+        ],
+        [by_lane(state_dim + 16), untouched(), untouched()],
         [
             shape_of((ctx_count, state_dim + 16, lanes), bf16),
             shape_of(inner_x.shape, f32),
-            shape_of(mixed.shape, bf16),
-            shape_of(grad_gate.shape, bf16),
-        ],
-        aliases={3: 1, 4: 2, 5: 3},
-    )(grad_received, received, incoming, inner_x, mixed, grad_gate)
+            shape_of(choice.shape, jnp.int32),
+        ],
+        aliases={3: 1, 4: 2},
+    )(grad_received, received, incoming, inner_x, choice)
     leaving = lax.all_to_all(sent, "ctx", 0, 0, tiled=True)
     leaving = leaving.reshape(seq_count, groups, state_dim + 16, lanes)
 
@@ -848,8 +856,8 @@
         + jnp.einsum("exp,pk->exk", mixed, output_weight, preferred_element_type=f32)
     ).astype(bf16)
     gate_normed = jnp.einsum("hou,qu->hoq", grad_gate, gate_weight, preferred_element_type=f32)
-    gate_parts, _ = share_parts(normed, grad_gate, [inner_width])
-    out_parts, _ = share_parts(mixed, cotangent, [model_width])
+    gate_parts, _ = share_parts(normed, grad_gate, [inner_width], choice)
+    out_parts, _ = share_parts(mixed, cotangent, [model_width], choice)
     first_sums = [HalvedSum(gate_parts[0], True), HalvedSum(out_parts[0], False)]
     for item in first_sums:
         item.step()
@@ -945,8 +953,8 @@
     tail = tail.at[:, 9 - taps :].add(rim_back).astype(bf16)
     grad_mixer = grad_mixer.at[:, length - 8 :, :channels].set(tail)
     middle = wide_width // 256 * 128
-    (left_parts, right_parts), gate_normed = share_parts(
-        normed, grad_mixer, [middle, wide_width - middle], gate_normed
+    (left_parts, right_parts), mixer_weight = share_parts(
+        normed, grad_mixer, [middle, wide_width - middle], choice, mixer_weight
     )
     left_sum, right_sum = HalvedSum(left_parts, True), HalvedSum(right_parts, False)
     gate_sum, out_sum, left_sum, right_sum = (

time: 709 us -> 707 us (level)
    ppermute x20, waiting for transfers between devices: 63.3 us -> 55.3 us  [swap(): lax.ppermute(values, axis, [(place, place ^ 1 << bit) for place in range(...]
  transfers between devices with their start and end apart: 34 -> 33, of which waited for: 20 -> 19; matrix products, arithmetic and copies ran while one was open for 13% -> 13% of each run, Pallas kernels for 16% -> 17%
where the time goes in v4:
time: 707 us; the launch traced here: 699 us
  waiting for transfers between devices  310 us (44%)
  Pallas kernels  203 us (29%)
  other arithmetic  54.7 us (8%)
  starting transfers between devices  50.8 us (7%)
  local copies, waits for them, and re-layouts  37.9 us (5%)
  matrix products  27.1 us (4%)
  between operations  15.3 us (2%)
    all_to_all x1, waiting for transfers between devices, local(): lax.all_to_all(sent.reshape(ctx_count, state_dim + 8, lanes), 'ctx', 0, 0...  108 us
    all_gather x1, waiting for transfers between devices, local(): mixer_weight = lax.all_gather(first_send, ('dp', 'ctx'), axis=0, tiled=True)  66.2 us
    ppermute x20, waiting for transfers between devices, swap(): lax.ppermute(values, axis, [(place, place ^ 1 << bit) for place in range(...  55.3 us
    pallas_call x2, Pallas kernels, exit_rows(): kernel_call(functools.partial(exit_kernel, len(held)), (count,), [at_row(...  45.3 us
    pallas_call x1, Pallas kernels, local(): kernel_call(functools.partial(middle_kernel, groups), (seq_count, length...  42.9 us
    pallas_call x6, Pallas kernels, share_of_product(): pl.pallas_call(functools.partial(share_kernel, widths), grid_spec=pltpu.P...  42.4 us
    pallas_call x1, Pallas kernels, local(): kernel_call(functools.partial(entry_kernel, heads_count), (seq_count,), [...  35.6 us
    all_to_all x1, waiting for transfers between devices, local(): incoming_low = lax.all_to_all(incoming_low, 'ctx', 0, 0, tiled=True)  35.1 us
  transfers between devices with their start and end apart: 33, of which 19 were waited for; matrix products, arithmetic and copies ran while one was open for 13% of the time, Pallas kernels for 17%

profile of v4, /device:TPU:0, one launch (start us, length us, event | category | flops | bytes accessed | tf_op | source)
XLA Modules:
  0.0 698.9 jit_solution(861485541961873241)
XLA Ops:
  12.8 66.2 %all-gather.3.cloned.1.call-done.weight_ref.refs_0_ = bf16[1024,2432]{1,0:T(8,128)(2,1)} async-done(((bf16[32,2432]{1,0:T(8,128)(2,1)}), bf16[1024,2432]{1,0:T(8,128)(2,1)}) %all-gather.3.cloned.1.call-update) | async-done | bytes 4980752 | tf_op jit(solution)/shard_map/all_gather | solution.py:649
  90.2 35.6 %shard_map.305 = (bf16[4,256,1024]{2,1,0:T(8,128)(2,1)}, f32[4,256,8]{2,1,0:T(8,128)}, bf16[4,272,2304]{2,1,0:T(8,128)(2,1)}, bf16[4,256,2304]{2,1,0:T(8,128)(2,...) custom-call(bf16[4,256,1024]{2,1,0:T(8,128)(2,1)} %x_ref.1, ...), custom_call_target="tpu_custom_call" | custom-call | tf_op jit(solution)/shard_map/pallas_call | solution.py:685
  131.8 10.7 %shard_map.306.held_ref = f32[4,256,2048]{2,1,0:T(8,128)} custom-call(bf16[4,256,2304]{2,1,0:T(8,128)(2,1)} %get-tuple-element.102.act_ref.refs_0_, f32[4,256,128]{2,1,0:T(8,128)} %get-tuple-element.107.step_ref.refs_10_, f32[4,256,128]{2,1,0:T(8,128)} %get-tuple-element.108.decay_ref.refs_11_, f32[4,256,8]{2,1,0:T(8,128)} %get-tuple-element.109.marks_ref.refs_12_, ...), custom_call_target="tpu_custom_call" | custom-call | tf_op jit(solution)/shard_map/pallas_call | solution.py:724
  142.6 107.5 %all-to-all-done.received_ref.passing_ref = f32[8,136,1024]{2,1,0:T(8,128)} async-done(((f32[8,136,1024]{2,1,0:T(8,128)}), f32[8,136,1024]{2,1,0:T(8,128)}, u32[]{:S(2)}, u32[]{:S(2)}) %all-to-all-start) | async-done | bytes 4456480 | tf_op jit(solution)/shard_map/all_to_all | solution.py:721
  265.8 7.1 %reshape.364.out_weight_ref = bf16[2048,1024]{1,0:T(8,128)(2,1)} reshape(bf16[1024,2048]{1,0:T(8,128)(2,1)} %get-tuple-element.185) | data formatting | bytes 8388608 | tf_op jit(solution)/shard_map/reshape | solution.py:656
  273.0 35.1 %all-to-all-done.1 = bf16[8,128,1024]{2,1,0:T(8,128)(2,1)S(1)} async-done(((bf16[8,128,1024]{2,1,0:T(8,128)(2,1)}), bf16[8,128,1024]{2,1,0:T(8,128)(2,1)S(1)}, u32[]{:S(2)}, u32[]{:S(2)}) %all-to-all-start.1) | async-done | bytes 2097184 | tf_op jit(solution)/shard_map/all_to_all | solution.py:751
  309.4 42.9 %shard_map.308 = (bf16[4,256,2048]{2,1,0:T(8,128)(2,1)}, bf16[4,256,2048]{2,1,0:T(8,128)(2,1)}, bf16[4,256,2048]{2,1,0:T(8,128)(2,1)}, bf16[4,2,128,1024]{3,2,1,...) custom-call(bf16[4,256,1024]{2,1,0:T(8,128)(2,1)} %cotangent_ref.1, ...), custom_call_target="tpu_custom_call" | custom-call | tf_op jit(solution)/shard_map/pallas_call | solution.py:756
  356.5 15.2 %shard_map.309 = (f32[4,256,2048]{2,1,0:T(8,128)}, f32[4,256,128]{2,1,0:T(8,128)}, f32[4,256,128]{2,1,0:T(8,128)}) custom-call(bf16[4,256,2304]{2,1,0:T(8,128)(2,1)} %get-tuple-element.102.act_ref.refs_0_, bf16[4,256,2048]{2,1,0:T(8,128)(2,1)} %get-tuple-element.112.grad_ssd_ref.refs_2_, f32[4,256,128]{2,1,0:T(8,128)} %get-tuple-element.107.step_ref.refs_10_, ...), custom_call_target="tpu_custom_call" | custom-call | tf_op jit(solution)/shard_map/pallas_call | solution.py:811
  371.8 32.6 %all-to-all-done.2.received_ref = bf16[8,128,1024]{2,1,0:T(8,128)(2,1)S(1)} async-done(((bf16[8,128,1024]{2,1,0:T(8,128)(2,1)}), bf16[8,128,1024]{2,1,0:T(8,128)(2,1)S(1)}, u32[]{:S(2)}, u32[]{:S(2)}) %all-to-all-start.2) | async-done | bytes 2097184 | tf_op jit(solution)/shard_map/all_to_all | solution.py:808
  412.2 7.0 shard_map.312
  419.1 6.5 shard_map.314
  432.1 6.5 shard_map.313
  438.5 6.9 shard_map.311
  468.0 7.1 %reshape.400 = bf16[2048,1024,1]{1,0,2:T(8,128)(2,1)} reshape(bf16[1024,2048]{1,0:T(8,128)(2,1)} %get-tuple-element.185) | data formatting | bytes 8388608 | tf_op jit(solution)/shard_map/reshape | solution.py:656
  477.0 9.9 %fusion.10.refs_20_ = bf16[4,256,1024]{2,1,0:T(8,128)(2,1)} fusion(bf16[4,256,1024]{2,1,0:T(8,128)(2,1)} %x_ref.1, bf16[4,256,2048]{2,1,0:T(8,128)(2,1)} %get-tuple-element.125, bf16[2048,1024,1]{1,0,2:T(8,128)(2,1)} %reshape.400), kind=kOutput, calls=%fused_computation.13 | convolution fusion | flops 4298113024 | bytes 12582912 | tf_op jit(solution)/shard_map/exp,pk->exk/dot_general | solution.py:856
  488.3 22.7 %shard_map.315 = (bf16[4,256,2432]{2,1,0:T(8,128)(2,1)}, f32[4,8,2304]{2,1,0:T(8,128)}, f32[4,8,2304]{2,1,0:T(8,128)}, f32[8,2304]{1,0:T(8,128)}, f32[8,128]{1,0...) custom-call(bf16[4,256,2304]{2,1,0:T(8,128)(2,1)} %get-tuple-element, ...), custom_call_target="tpu_custom_call", output_to_operand_aliasing={{5}: (17, {}), {6}: (18, {}), {7}: (19, {}), {8}: (20, {})} | custom-call | tf_op jit(solution)/shard_map/pallas_call | solution.py:878
  518.3 22.6 %shard_map.316 = (bf16[4,256,2432]{2,1,0:T(8,128)(2,1)}, f32[4,8,2304]{2,1,0:T(8,128)}, f32[4,8,2304]{2,1,0:T(8,128)}, f32[8,2304]{1,0:T(8,128)}, f32[8,128]{1,0...) custom-call(bf16[4,256,2304]{2,1,0:T(8,128)(2,1)} %get-tuple-element, ...), custom_call_target="tpu_custom_call", output_to_operand_aliasing={{0}: (17, {}), {1}: (18, {}), {2}: (19, {}), {5}: (20, {}),... | custom-call | tf_op jit(solution)/shard_map/pallas_call | solution.py:878
  549.6 7.8 %shard_map.317 = (bf16[1024,2432]{1,0:T(8,128)(2,1)}, f32[2,256,1152]{2,1,0:T(8,128)}, f32[2,256,1280]{2,1,0:T(8,128)}) custom-call(s32[1]{0:T(128)} %get-tuple-element.231.chosen_ref, bf16[1024,1024]{1,0:T(8,128)(2,1)} %bitcast.189, bf16[1024,2432]{1,0:T(8,128)(2,1)} %bitcast.191, ...), custom_call_target="tpu_custom_call", output_to_operand_aliasing={{0}: (3, {})} | custom-call | tf_op jit(solution)/shard_map/pallas_call | solution.py:433
  557.4 11.1 %fusion.9 = (f32[1024]{0:T(1024)S(1)}, f32[4,256]{1,0:T(4,128)S(1)}, f32[4,256,1024]{2,1,0:T(8,128)}) fusion(bf16[4,256,1024]{2,1,0:T(8,128)(2,1)} %x_ref.1, f32[4,256]{1,0:T(4,128)S(1)} %add_rsqrt_fusion, f32[4,256,1024]{2,1,0:T(8,128)} %get-tuple-element.127, f32[1024]{0:T(1024)S(1)} %slice.288, bf16[4,256,2432]{2,1,0:T(8,128)(2,1)S(1)} %copy-done, ...), kind=kOutput, calls=%fused_computation.12 | convolution fusion | flops 5108660224 | bytes 20463616 | tf_op jit(solution)/shard_map/hou,qu->hoq/dot_general | solution.py:963
  581.3 7.7 %shard_map.318 = (f32[2,256,1152]{2,1,0:T(8,128)}, f32[2,256,1280]{2,1,0:T(8,128)}) custom-call(s32[1]{0:T(128)} %get-tuple-element.232.chosen_ref, bf16[1024,1024]{1,0:T(8,128)(2,1)} %bitcast.190, bf16[1024,2432]{1,0:T(8,128)(2,1)} %bitcast.192), custom_call_target="tpu_custom_call" | custom-call | tf_op jit(solution)/shard_map/pallas_call | solution.py:433
  597.4 6.3 collective-permute-done.26
  611.7 10.3 %collective-permute-done.20 = f32[2,64,1024]{2,1,0:T(8,128)} collective-permute-done((f32[2,64,1024]{2,1,0:T(8,128)}, f32[2,64,1024]{2,1,0:T(8,128)}, u32[]{:S(2)}, u32[]{:S(2)}) %collective-permute-start.20) | collective-permute-done | bytes 524320 | tf_op jit(solution)/shard_map/ppermute | solution.py:43
  636.8 12.1 %collective-permute-done.10 = f32[2,2,2,32,1152]{4,3,0,1,2:T(8,128)S(1)} collective-permute-done((f32[2,2,2,32,1152]{4,3,0,1,2:T(8,128)S(1)}, f32[2,2,2,32,1152]{4,3,0,1,2:T(8,128)S(1)}, u32[]{:S(2)}, u32[]{:S(2)}) %collective-permute-start.10) | collective-permute-done | bytes 1179680 | tf_op jit(solution)/shard_map/ppermute | solution.py:43
  650.8 10.6 %collective-permute-done.15 = f32[2,2,2,32,1280]{4,3,1,2,0:T(8,128)S(1)} collective-permute-done((f32[2,2,2,32,1280]{4,3,1,2,0:T(8,128)S(1)}, f32[2,2,2,32,1280]{4,3,1,2,0:T(8,128)S(1)}, u32[]{:S(2)}, u32[]{:S(2)}) %collective-permute-start.15) | collective-permute-done | bytes 1310752 | tf_op jit(solution)/shard_map/ppermute | solution.py:43
  (271 shorter events, 175.5 us)
Async XLA Ops:
  7.2 71.8 %all-gather.3.cloned.1.call-start = ((), (), s32[]{:S(2)}) async-start(), calls=%async_computation.4 | async-start | bytes 5136384 | tf_op jit(solution)/shard_map/all_gather | solution.py:649
  11.0 248.8 %all-gather.5.cloned.1.call-start = ((), (), s32[]{:S(2)}) async-start(), calls=%async_computation.5 | async-start | bytes 8650752 | tf_op jit(solution)/shard_map/all_gather | solution.py:654
  125.8 124.3 %all-to-all-start = ((f32[8,136,1024]{2,1,0:T(8,128)}), f32[8,136,1024]{2,1,0:T(8,128)}, u32[]{:S(2)}, u32[]{:S(2)}) async-start(f32[8,136,1024]{2,1,0:T(8,128)} %bitcast.206), calls=%async_computation | async-start | bytes 8912896 | tf_op jit(solution)/shard_map/all_to_all | solution.py:721
  255.5 52.6 %all-to-all-start.1 = ((bf16[8,128,1024]{2,1,0:T(8,128)(2,1)}), bf16[8,128,1024]{2,1,0:T(8,128)(2,1)S(1)}, u32[]{:S(2)}, u32[]{:S(2)}) async-start(bf16[8,128,1024]{2,1,0:T(8,128)(2,1)} %get-tuple-element.111), calls=%async_computation.1 | async-start | bytes 4194304 | tf_op jit(solution)/shard_map/all_to_all | solution.py:751
  352.3 52.1 %all-to-all-start.2 = ((bf16[8,128,1024]{2,1,0:T(8,128)(2,1)}), bf16[8,128,1024]{2,1,0:T(8,128)(2,1)S(1)}, u32[]{:S(2)}, u32[]{:S(2)}) async-start(bf16[8,128,1024]{2,1,0:T(8,128)(2,1)} %bitcast.209), calls=%async_computation.2 | async-start | bytes 4194304 | tf_op jit(solution)/shard_map/all_to_all | solution.py:808
  419.1 26.4 %collective-permute-start.1 = (f32[2,256,2048]{2,1,0:T(8,128)}, f32[2,256,2048]{2,1,0:T(8,128)}, u32[]{:S(2)}, u32[]{:S(2)}) collective-permute-start(f32[2,256,2048]{2,1,0:T(8,128)} %shard_map.312), channel_id=1, source_target_pairs={{0,8},{8,0},{16,24},{24,16},{1,9},{9,1},{17,25},{25,17},{2,10},{10... | collective-permute-start | bytes 12582920 | tf_op jit(solution)/shard_map/ppermute | solution.py:43
  425.6 28.9 %collective-permute-start.2 = (f32[2,512,1024]{2,1,0:T(8,128)}, f32[2,512,1024]{2,1,0:T(8,128)}, u32[]{:S(2)}, u32[]{:S(2)}) collective-permute-start(f32[2,512,1024]{2,1,0:T(8,128)} %shard_map.314), channel_id=1, source_target_pairs={{0,8},{8,0},{16,24},{24,16},{1,9},{9,1},{17,25},{25,17},{2,10},{10... | collective-permute-start | bytes 12582920 | tf_op jit(solution)/shard_map/ppermute | solution.py:43
  426.1 60.8 %all-to-all-start.3 = ((bf16[8,144,1024]{2,1,0:T(8,128)(2,1)}), bf16[8,144,1024]{2,1,0:T(8,128)(2,1)S(1)}, u32[]{:S(2)}, u32[]{:S(2)}) async-start(bf16[8,144,1024]{2,1,0:T(8,128)(2,1)} %get-tuple-element.120), calls=%async_computation.3 | async-start | bytes 4718592 | tf_op jit(solution)/shard_map/all_to_all | solution.py:850
  453.1 58.0 %collective-permute-start.3 = (f32[2,2,2,32,2048]{4,3,1,0,2:T(8,128)}, f32[2,2,2,32,2048]{4,3,1,0,2:T(8,128)}, u32[]{:S(2)}, u32[]{:S(2)}) collective-permute-start(f32[2,2,2,32,2048]{4,3,1,0,2:T(8,128)} %fusion.16), channel_id=1, source_target_pairs={{0,16},{8,24},{16,0},{24,8},{1,17},{9,25},{17,1},{25,9},{2,18},{10... | collective-permute-start | bytes 6291464 | tf_op jit(solution)/shard_map/ppermute | solution.py:43
  459.9 55.2 %collective-permute-start.4 = (f32[2,2,2,64,1024]{4,3,2,1,0:T(8,128)}, f32[2,2,2,64,1024]{4,3,2,1,0:T(8,128)}, u32[]{:S(2)}, u32[]{:S(2)}) collective-permute-start(f32[2,2,2,64,1024]{4,3,2,1,0:T(8,128)} %get-tuple-element.183), channel_id=1, source_target_pairs={{0,1},{1,0},{2,3},{3,2},{4,5},{5,4},{6,7},{7,6},{8,9},{9,8},{10,11... | collective-permute-start | bytes 6291464 | tf_op jit(solution)/shard_map/ppermute | solution.py:43
  577.2 27.3 %collective-permute-start.19 = (f32[2,2,64,1024]{3,2,1,0:T(8,128)}, f32[2,2,64,1024]{3,2,1,0:T(8,128)}, u32[]{:S(2)}, u32[]{:S(2)}) collective-permute-start(f32[2,2,64,1024]{3,2,1,0:T(8,128)} %get-tuple-element.187), channel_id=1, source_target_pairs={{0,16},{8,24},{16,0},{24,8},{1,17},{9,25},{17,1},{25,9},{2,18},{10... | collective-permute-start | bytes 3145736 | tf_op jit(solution)/shard_map/ppermute | solution.py:43
  578.7 31.1 %collective-permute-start.6 = (f32[2,2,32,2048]{3,2,1,0:T(8,128)}, f32[2,2,32,2048]{3,2,1,0:T(8,128)}, u32[]{:S(2)}, u32[]{:S(2)}) collective-permute-start(f32[2,2,32,2048]{3,2,1,0:T(8,128)} %get-tuple-element.189), channel_id=1, source_target_pairs={{0,1},{1,0},{2,3},{3,2},{4,5},{5,4},{6,7},{7,6},{8,9},{9,8},{10,11... | collective-permute-start | bytes 3145736 | tf_op jit(solution)/shard_map/ppermute | solution.py:43
  589.1 34.5 %collective-permute-start.9 = (f32[2,256,1152]{2,1,0:T(8,128)}, f32[2,256,1152]{2,1,0:T(8,128)}, u32[]{:S(2)}, u32[]{:S(2)}) collective-permute-start(f32[2,256,1152]{2,1,0:T(8,128)} %get-tuple-element.139), channel_id=1, source_target_pairs={{0,8},{8,0},{16,24},{24,16},{1,9},{9,1},{17,25},{25,17},{2,10},{10... | collective-permute-start | bytes 7077896 | tf_op jit(solution)/shard_map/ppermute | solution.py:43
  589.1 37.3 %collective-permute-start.14 = (f32[2,256,1280]{2,1,0:T(8,128)}, f32[2,256,1280]{2,1,0:T(8,128)}, u32[]{:S(2)}, u32[]{:S(2)}) collective-permute-start(f32[2,256,1280]{2,1,0:T(8,128)} %get-tuple-element.141), channel_id=1, source_target_pairs={{0,8},{8,0},{16,24},{24,16},{1,9},{9,1},{17,25},{25,17},{2,10},{10... | collective-permute-start | bytes 7864328 | tf_op jit(solution)/shard_map/ppermute | solution.py:43
  589.8 13.9 %collective-permute-start.26 = (f32[552]{0:T(1024)S(1)}, f32[552]{0:T(1024)S(1)}, u32[]{:S(2)}, u32[]{:S(2)}) collective-permute-start(f32[552]{0:T(1024)S(1)} %pad_maximum_fusion.8), channel_id=1, source_target_pairs={{0,1},{1,0},{2,3},{3,2},{4,5},{5,4},{6,7},{7,6},{8,9},{9,8},{10,11... | collective-permute-start | bytes 6632 | tf_op jit(solution)/shard_map/ppermute | solution.py:57
  606.8 15.2 %collective-permute-start.20 = (f32[2,64,1024]{2,1,0:T(8,128)}, f32[2,64,1024]{2,1,0:T(8,128)}, u32[]{:S(2)}, u32[]{:S(2)}) collective-permute-start(f32[2,64,1024]{2,1,0:T(8,128)} %get-tuple-element.201), channel_id=1, source_target_pairs={{0,2},{1,3},{2,0},{3,1},{4,6},{5,7},{6,4},{7,5},{8,10},{9,11},{10,... | collective-permute-start | bytes 1572872 | tf_op jit(solution)/shard_map/ppermute | solution.py:43
  611.1 25.4 %collective-permute-start.7 = (f32[2,32,2048]{2,1,0:T(8,128)S(1)}, f32[2,32,2048]{2,1,0:T(8,128)S(1)}, u32[]{:S(2)}, u32[]{:S(2)}) collective-permute-start(f32[2,32,2048]{2,1,0:T(8,128)S(1)} %get-tuple-element.203), channel_id=1, source_target_pairs={{0,2},{1,3},{2,0},{3,1},{4,6},{5,7},{6,4},{7,5},{8,10},{9,11},{10,... | collective-permute-start | bytes 1572872 | tf_op jit(solution)/shard_map/ppermute | solution.py:43
  623.0 51.1 %collective-permute-start.21 = (f32[64,1024]{1,0:T(8,128)S(1)}, f32[64,1024]{1,0:T(8,128)S(1)}, u32[]{:S(2)}, u32[]{:S(2)}) collective-permute-start(f32[64,1024]{1,0:T(8,128)S(1)} %fusion.26), channel_id=1, source_target_pairs={{0,4},{1,5},{2,6},{3,7},{4,0},{5,1},{6,2},{7,3},{8,12},{9,13},{10,... | collective-permute-start | bytes 786440 | tf_op jit(solution)/shard_map/ppermute | solution.py:43
  625.7 23.2 %collective-permute-start.10 = (f32[2,2,2,32,1152]{4,3,0,1,2:T(8,128)S(1)}, f32[2,2,2,32,1152]{4,3,0,1,2:T(8,128)S(1)}, u32[]{:S(2)}, u32[]{:S(2)}) collective-permute-start(f32[2,2,2,32,1152]{4,3,0,1,2:T(8,128)S(1)} %fusion.18), channel_id=1, source_target_pairs={{0,16},{8,24},{16,0},{24,8},{1,17},{9,25},{17,1},{25,9},{2,18},{10... | collective-permute-start | bytes 3538952 | tf_op jit(solution)/shard_map/ppermute | solution.py:43
  629.6 31.8 %collective-permute-start.15 = (f32[2,2,2,32,1280]{4,3,1,2,0:T(8,128)S(1)}, f32[2,2,2,32,1280]{4,3,1,2,0:T(8,128)S(1)}, u32[]{:S(2)}, u32[]{:S(2)}) collective-permute-start(f32[2,2,2,32,1280]{4,3,1,2,0:T(8,128)S(1)} %fusion.17), channel_id=1, source_target_pairs={{0,1},{1,0},{2,3},{3,2},{4,5},{5,4},{6,7},{7,6},{8,9},{9,8},{10,11... | collective-permute-start | bytes 3932168 | tf_op jit(solution)/shard_map/ppermute | solution.py:43
  636.5 25.8 %collective-permute-start.8 = (f32[32,2048]{1,0:T(8,128)S(1)}, f32[32,2048]{1,0:T(8,128)S(1)}, u32[]{:S(2)}, u32[]{:S(2)}) collective-permute-start(f32[32,2048]{1,0:T(8,128)S(1)} %fusion.27), channel_id=1, source_target_pairs={{0,4},{1,5},{2,6},{3,7},{4,0},{5,1},{6,2},{7,3},{8,12},{9,13},{10,... | collective-permute-start | bytes 786440 | tf_op jit(solution)/shard_map/ppermute | solution.py:43
  649.1 19.2 %collective-permute-start.11 = (f32[2,2,32,1152]{3,2,0,1:T(8,128)S(1)}, f32[2,2,32,1152]{3,2,0,1:T(8,128)S(1)}, u32[]{:S(2)}, u32[]{:S(2)}) collective-permute-start(f32[2,2,32,1152]{3,2,0,1:T(8,128)S(1)} %get-tuple-element.213), channel_id=1, source_target_pairs={{0,1},{1,0},{2,3},{3,2},{4,5},{5,4},{6,7},{7,6},{8,9},{9,8},{10,11... | collective-permute-start | bytes 1769480 | tf_op jit(solution)/shard_map/ppermute | solution.py:43
  661.6 10.7 %collective-permute-start.16 = (f32[2,2,32,1280]{3,2,0,1:T(8,128)S(1)}, f32[2,2,32,1280]{3,2,0,1:T(8,128)S(1)}, u32[]{:S(2)}, u32[]{:S(2)}) collective-permute-start(f32[2,2,32,1280]{3,2,0,1:T(8,128)S(1)} %get-tuple-element.207), channel_id=1, source_target_pairs={{0,16},{8,24},{16,0},{24,8},{1,17},{9,25},{17,1},{25,9},{2,18},{10... | collective-permute-start | bytes 1966088 | tf_op jit(solution)/shard_map/ppermute | solution.py:43
  672.4 9.6 %collective-permute-start.17 = (f32[2,32,1280]{2,1,0:T(8,128)S(1)}, f32[2,32,1280]{2,1,0:T(8,128)S(1)}, u32[]{:S(2)}, u32[]{:S(2)}) collective-permute-start(f32[2,32,1280]{2,1,0:T(8,128)S(1)} %get-tuple-element.205), channel_id=1, source_target_pairs={{0,2},{1,3},{2,0},{3,1},{4,6},{5,7},{6,4},{7,5},{8,10},{9,11},{10,... | collective-permute-start | bytes 983048 | tf_op jit(solution)/shard_map/ppermute | solution.py:43
  (47 other events, 857.2 us)
Sparse Core Ops, SparseCore 0:
  11.5 67.3 all-gather.2
  82.5 106.1 all-gather.4

commit v5 on v4

--- a/solution.py
+++ b/solution.py
@@ -267,7 +267,7 @@
 
 
 def carry_backward_kernel(
-    received_ref, passing_ref, incoming_ref, inner_ref, choice_ref, send_ref, *kept_refs
+    received_ref, passing_ref, incoming_ref, inner_ref, choice_ref, gate_ref, send_ref, *kept_refs
 ):
     blocks, state = received_ref.shape[0], received_ref.shape[1]
     carried = jnp.zeros(received_ref.shape[1:], jnp.float32)
@@ -452,7 +452,7 @@
 
 
 def share_parts(left, right, widths, choice, held=None):
-    away, _ = share_of_product(left, right, choice[1:], widths)
+    away, choice = share_of_product(left, right, choice[1:], widths, choice)
     away = [swap(piece, "dp", 0) for piece in away]
     kept, held = share_of_product(left, right, choice[:1], widths, held)
     return list(zip(kept, away)), held
@@ -827,9 +827,10 @@
         ],
         [pltpu.VMEM((length, length), f32)],
     )(activated, grad_ssd, step_size, decay_sum, marks, segment_rows)
+    gate_normed = jnp.einsum("hou,qu->hoq", grad_gate, gate_weight, preferred_element_type=f32)
     mine = lax.axis_index("dp") & 1
     choice = jnp.stack([mine, 1 - mine]).astype(jnp.int32)
-    sent, inner_x, choice = kernel_call(
+    sent, inner_x, choice, gate_normed = kernel_call(
         carry_backward_kernel,
         (lanes // tile,),
         [
@@ -838,24 +839,27 @@
             by_lane(state_dim),
             untouched(),
             untouched(),
-        ],
-        [by_lane(state_dim + 16), untouched(), untouched()],
+            untouched(),
+        ],
+        [by_lane(state_dim + 16), untouched(), untouched(), untouched()],
         [
             shape_of((ctx_count, state_dim + 16, lanes), bf16),
             shape_of(inner_x.shape, f32),
             shape_of(choice.shape, jnp.int32),
-        ],
-        aliases={3: 1, 4: 2},
-    )(grad_received, received, incoming, inner_x, choice)
+            shape_of(gate_normed.shape, f32),
+        ],
+        aliases={3: 1, 4: 2, 5: 3},
+    )(grad_received, received, incoming, inner_x, choice, gate_normed)
     leaving = lax.all_to_all(sent, "ctx", 0, 0, tiled=True)
     leaving = leaving.reshape(seq_count, groups, state_dim + 16, lanes)
 
     input_float = tokens.astype(f32)
     output = (
         input_float
-        + jnp.einsum("exp,pk->exk", mixed, output_weight, preferred_element_type=f32)
+        + jnp.dot(
+            mixed.reshape(-1, inner_width), output_weight, preferred_element_type=f32
+        ).reshape(tokens.shape)
     ).astype(bf16)
-    gate_normed = jnp.einsum("hou,qu->hoq", grad_gate, gate_weight, preferred_element_type=f32)
     gate_parts, _ = share_parts(normed, grad_gate, [inner_width], choice)
     out_parts, _ = share_parts(mixed, cotangent, [model_width], choice)
     first_sums = [HalvedSum(gate_parts[0], True), HalvedSum(out_parts[0], False)]

time: 707 us -> 715 us (1.011)
    all_to_all x1, waiting for transfers between devices: 32.6 us -> 23.5 us  [local(): lax.all_to_all(sent.reshape(ctx_count, state_dim, lanes), 'ctx', 0, 0, ti...]
  transfers between devices with their start and end apart: 33 -> 33, of which waited for: 19 -> 21; matrix products, arithmetic and copies ran while one was open for 13% -> 13% of each run, Pallas kernels for 17% -> 16%
where the time goes in v5:
time: 715 us; the launch traced here: 707 us
  waiting for transfers between devices  314 us (44%)
  Pallas kernels  203 us (28%)
  other arithmetic  54.5 us (8%)
  starting transfers between devices  53.3 us (7%)
  local copies, waits for them, and re-layouts  38.5 us (5%)
  matrix products  29.3 us (4%)
  between operations  15 us (2%)
    all_to_all x1, waiting for transfers between devices, local(): lax.all_to_all(sent.reshape(ctx_count, state_dim + 8, lanes), 'ctx', 0, 0...  108 us
    all_gather x1, waiting for transfers between devices, local(): mixer_weight = lax.all_gather(first_send, ('dp', 'ctx'), axis=0, tiled=True)  66.2 us
    ppermute x20, waiting for transfers between devices, swap(): lax.ppermute(values, axis, [(place, place ^ 1 << bit) for place in range(...  59.3 us
    pallas_call x2, Pallas kernels, exit_rows(): kernel_call(functools.partial(exit_kernel, len(held)), (count,), [at_row(...  45.3 us
    pallas_call x1, Pallas kernels, local(): kernel_call(functools.partial(middle_kernel, groups), (seq_count, length...  42.9 us
    pallas_call x6, Pallas kernels, share_of_product(): pl.pallas_call(functools.partial(share_kernel, widths), grid_spec=pltpu.P...  42.4 us
    pallas_call x1, Pallas kernels, local(): kernel_call(functools.partial(entry_kernel, heads_count), (seq_count,), [...  35.6 us
    all_to_all x1, waiting for transfers between devices, local(): incoming_low = lax.all_to_all(incoming_low, 'ctx', 0, 0, tiled=True)  35.1 us
  transfers between devices with their start and end apart: 33, of which 21 were waited for; matrix products, arithmetic and copies ran while one was open for 13% of the time, Pallas kernels for 16%

profile of v5, /device:TPU:0, one launch (start us, length us, event | category | flops | bytes accessed | tf_op | source)
XLA Modules:
  0.0 707.1 jit_solution(14029239246785447005)
XLA Ops:
  12.8 66.2 %all-gather.3.cloned.1.call-done.weight_ref.refs_0_ = bf16[1024,2432]{1,0:T(8,128)(2,1)} async-done(((bf16[32,2432]{1,0:T(8,128)(2,1)}), bf16[1024,2432]{1,0:T(8,128)(2,1)}) %all-gather.3.cloned.1.call-update) | async-done | bytes 4980752 | tf_op jit(solution)/shard_map/all_gather | solution.py:649
  90.2 35.6 %shard_map.305 = (bf16[4,256,1024]{2,1,0:T(8,128)(2,1)}, f32[4,256,8]{2,1,0:T(8,128)}, bf16[4,272,2304]{2,1,0:T(8,128)(2,1)}, bf16[4,256,2304]{2,1,0:T(8,128)(2,...) custom-call(bf16[4,256,1024]{2,1,0:T(8,128)(2,1)} %x_ref.1, ...), custom_call_target="tpu_custom_call" | custom-call | tf_op jit(solution)/shard_map/pallas_call | solution.py:685
  131.9 10.7 %shard_map.306.held_ref = f32[4,256,2048]{2,1,0:T(8,128)} custom-call(bf16[4,256,2304]{2,1,0:T(8,128)(2,1)} %get-tuple-element.108.act_ref.refs_0_, f32[4,256,128]{2,1,0:T(8,128)} %get-tuple-element.113.step_ref.refs_10_, f32[4,256,128]{2,1,0:T(8,128)} %get-tuple-element.114.decay_ref.refs_11_, f32[4,256,8]{2,1,0:T(8,128)} %get-tuple-element.115.marks_ref.refs_12_, ...), custom_call_target="tpu_custom_call" | custom-call | tf_op jit(solution)/shard_map/pallas_call | solution.py:724
  142.6 107.5 %all-to-all-done.received_ref.passing_ref = f32[8,136,1024]{2,1,0:T(8,128)} async-done(((f32[8,136,1024]{2,1,0:T(8,128)}), f32[8,136,1024]{2,1,0:T(8,128)}, u32[]{:S(2)}, u32[]{:S(2)}) %all-to-all-start) | async-done | bytes 4456480 | tf_op jit(solution)/shard_map/all_to_all | solution.py:721
  265.6 7.1 %reshape.368.out_weight_ref = bf16[2048,1024]{1,0:T(8,128)(2,1)} reshape(bf16[1024,2048]{1,0:T(8,128)(2,1)} %get-tuple-element.197) | data formatting | bytes 8388608 | tf_op jit(solution)/shard_map/reshape | solution.py:656
  272.7 35.1 %all-to-all-done.1 = bf16[8,128,1024]{2,1,0:T(8,128)(2,1)S(1)} async-done(((bf16[8,128,1024]{2,1,0:T(8,128)(2,1)}), bf16[8,128,1024]{2,1,0:T(8,128)(2,1)S(1)}, u32[]{:S(2)}, u32[]{:S(2)}) %all-to-all-start.1) | async-done | bytes 2097184 | tf_op jit(solution)/shard_map/all_to_all | solution.py:751
  309.1 42.9 %shard_map.308 = (bf16[4,256,2048]{2,1,0:T(8,128)(2,1)}, bf16[4,256,2048]{2,1,0:T(8,128)(2,1)}, bf16[4,256,2048]{2,1,0:T(8,128)(2,1)}, bf16[4,2,128,1024]{3,2,1,...) custom-call(bf16[4,256,1024]{2,1,0:T(8,128)(2,1)} %cotangent_ref.1, ...), custom_call_target="tpu_custom_call" | custom-call | tf_op jit(solution)/shard_map/pallas_call | solution.py:756
  357.0 15.4 %shard_map.309 = (f32[4,256,2048]{2,1,0:T(8,128)}, f32[4,256,128]{2,1,0:T(8,128)}, f32[4,256,128]{2,1,0:T(8,128)}) custom-call(bf16[4,256,2304]{2,1,0:T(8,128)(2,1)} %get-tuple-element.108.act_ref.refs_0_, bf16[4,256,2048]{2,1,0:T(8,128)(2,1)} %get-tuple-element.118.grad_ssd_ref.refs_2_, f32[4,256,128]{2,1,0:T(8,128)} %get-tuple-element.113.step_ref.refs_10_, ...), custom_call_target="tpu_custom_call" | custom-call | tf_op jit(solution)/shard_map/pallas_call | solution.py:811
  372.4 8.3 %fusion.12.gate_ref = f32[4,256,1024]{2,1,0:T(8,128)} fusion(bf16[4,256,2048]{2,1,0:T(8,128)(2,1)S(1)} %copy-done.3, bf16[1024,4096]{1,0:T(8,128)(2,1)} %all-gather.5.cloned.1.call-done), kind=kOutput, calls=%fused_computation.15 | convolution fusion | flops 4294967296 | bytes 12582912 | tf_op jit(solution)/shard_map/hou,qu->hoq/dot_general | solution.py:830
  380.7 23.5 %all-to-all-done.2.received_ref = bf16[8,128,1024]{2,1,0:T(8,128)(2,1)} async-done(((bf16[8,128,1024]{2,1,0:T(8,128)(2,1)}), bf16[8,128,1024]{2,1,0:T(8,128)(2,1)}, u32[]{:S(2)}, u32[]{:S(2)}) %all-to-all-start.2) | async-done | bytes 2097184 | tf_op jit(solution)/shard_map/all_to_all | solution.py:808
  412.9 7.0 shard_map.311
  453.6 7.0 fusion.14
  463.1 7.1 %reshape.404 = bf16[2048,1024,1]{1,0,2:T(8,128)(2,1)} reshape(bf16[1024,2048]{1,0:T(8,128)(2,1)} %get-tuple-element.197) | data formatting | bytes 8388608 | tf_op jit(solution)/shard_map/reshape | solution.py:656
  472.1 9.9 %fusion.10.refs_20_ = bf16[4,256,1024]{2,1,0:T(8,128)(2,1)} fusion(bf16[4,256,1024]{2,1,0:T(8,128)(2,1)} %x_ref.1, bf16[4,256,2048]{2,1,0:T(8,128)(2,1)} %get-tuple-element.133, bf16[2048,1024,1]{1,0,2:T(8,128)(2,1)} %reshape.404), kind=kOutput, calls=%fused_computation.13 | convolution fusion | flops 4298113024 | bytes 12582912 | tf_op jit(solution)/shard_map/dot_general | solution.py:859
  486.6 22.7 %shard_map.315 = (bf16[4,256,2432]{2,1,0:T(8,128)(2,1)}, f32[4,8,2304]{2,1,0:T(8,128)}, f32[4,8,2304]{2,1,0:T(8,128)}, f32[8,2304]{1,0:T(8,128)}, f32[8,128]{1,0...) custom-call(bf16[4,256,2304]{2,1,0:T(8,128)(2,1)} %get-tuple-element, ...), custom_call_target="tpu_custom_call", output_to_operand_aliasing={{5}: (17, {}), {6}: (18, {}), {7}: (19, {}), {8}: (20, {})} | custom-call | tf_op jit(solution)/shard_map/pallas_call | solution.py:882
  516.6 22.6 %shard_map.316 = (bf16[4,256,2432]{2,1,0:T(8,128)(2,1)}, f32[4,8,2304]{2,1,0:T(8,128)}, f32[4,8,2304]{2,1,0:T(8,128)}, f32[8,2304]{1,0:T(8,128)}, f32[8,128]{1,0...) custom-call(bf16[4,256,2304]{2,1,0:T(8,128)(2,1)} %get-tuple-element, ...), custom_call_target="tpu_custom_call", output_to_operand_aliasing={{0}: (17, {}), {1}: (18, {}), {2}: (19, {}), {5}: (20, {}),... | custom-call | tf_op jit(solution)/shard_map/pallas_call | solution.py:882
  547.6 7.9 %shard_map.317 = (s32[2]{0:T(128)}, f32[2,256,1152]{2,1,0:T(8,128)}, f32[2,256,1280]{2,1,0:T(8,128)}) custom-call(s32[1]{0:T(128)} %slice.260.chosen_ref, bf16[1024,1024]{1,0:T(8,128)(2,1)} %bitcast.192, bf16[1024,2432]{1,0:T(8,128)(2,1)} %bitcast.194, s32[2]{0:T(128)} %copy.169.refs_0_), custom_call_target="tpu_custom_call", output_to_operand_aliasing={{0}: (3, {})} | custom-call | tf_op jit(solution)/shard_map/pallas_call | solution.py:433
  555.5 7.6 %shard_map.318 = (bf16[1024,2432]{1,0:T(8,128)(2,1)}, f32[2,256,1152]{2,1,0:T(8,128)}, f32[2,256,1280]{2,1,0:T(8,128)}) custom-call(s32[1]{0:T(128)} %bitcast.225, bf16[1024,1024]{1,0:T(8,128)(2,1)} %bitcast.193, bf16[1024,2432]{1,0:T(8,128)(2,1)} %bitcast.195, ...), custom_call_target="tpu_custom_call", output_to_operand_aliasing={{0}: (3, {})} | custom-call | tf_op jit(solution)/shard_map/pallas_call | solution.py:433
  563.0 11.1 %fusion.9 = (f32[1024]{0:T(1024)S(1)}, f32[4,256]{1,0:T(4,128)S(1)}, f32[4,256,1024]{2,1,0:T(8,128)}) fusion(bf16[4,256,1024]{2,1,0:T(8,128)(2,1)} %x_ref.1, f32[4,256]{1,0:T(4,128)S(1)} %add_rsqrt_fusion, f32[4,256,1024]{2,1,0:T(8,128)} %get-tuple-element.138, f32[1024]{0:T(1024)S(1)} %slice.294, bf16[4,256,2432]{2,1,0:T(8,128)(2,1)S(1)} %bitcast.197, ...), kind=kOutput, calls=%fused_computation.12 | convolution fusion | flops 5108660224 | bytes 20463616 | tf_op jit(solution)/shard_map/hou,qu->hoq/dot_general | solution.py:967
  593.2 7.1 fusion.8
  600.3 9.8 %collective-permute-done.26 = f32[552]{0:T(1024)S(1)} collective-permute-done((f32[552]{0:T(1024)S(1)}, f32[552]{0:T(1024)S(1)}, u32[]{:S(2)}, u32[]{:S(2)}) %collective-permute-start.26) | collective-permute-done | bytes 2240 | tf_op jit(solution)/shard_map/ppermute | solution.py:57
  616.9 10.3 %collective-permute-done.20 = f32[2,64,1024]{2,1,0:T(8,128)} collective-permute-done((f32[2,64,1024]{2,1,0:T(8,128)}, f32[2,64,1024]{2,1,0:T(8,128)}, u32[]{:S(2)}, u32[]{:S(2)}) %collective-permute-start.20) | collective-permute-done | bytes 524320 | tf_op jit(solution)/shard_map/ppermute | solution.py:43
  643.6 12.6 %collective-permute-done.10 = f32[2,2,2,32,1152]{4,3,0,1,2:T(8,128)S(1)} collective-permute-done((f32[2,2,2,32,1152]{4,3,0,1,2:T(8,128)S(1)}, f32[2,2,2,32,1152]{4,3,0,1,2:T(8,128)S(1)}, u32[]{:S(2)}, u32[]{:S(2)}) %collective-permute-start.10) | collective-permute-done | bytes 1179680 | tf_op jit(solution)/shard_map/ppermute | solution.py:43
  657.5 10.7 %collective-permute-done.15 = f32[2,2,2,32,1280]{4,3,1,2,0:T(8,128)S(1)} collective-permute-done((f32[2,2,2,32,1280]{4,3,1,2,0:T(8,128)S(1)}, f32[2,2,2,32,1280]{4,3,1,2,0:T(8,128)S(1)}, u32[]{:S(2)}, u32[]{:S(2)}) %collective-permute-start.15) | collective-permute-done | bytes 1310752 | tf_op jit(solution)/shard_map/ppermute | solution.py:43
  (267 shorter events, 186.6 us)
Async XLA Ops:
  7.2 71.8 %all-gather.3.cloned.1.call-start = ((), (), s32[]{:S(2)}) async-start(), calls=%async_computation.4 | async-start | bytes 5136384 | tf_op jit(solution)/shard_map/all_gather | solution.py:649
  11.0 248.5 %all-gather.5.cloned.1.call-start = ((), (), s32[]{:S(2)}) async-start(), calls=%async_computation.5 | async-start | bytes 8650752 | tf_op jit(solution)/shard_map/all_gather | solution.py:654
  125.8 124.3 %all-to-all-start = ((f32[8,136,1024]{2,1,0:T(8,128)}), f32[8,136,1024]{2,1,0:T(8,128)}, u32[]{:S(2)}, u32[]{:S(2)}) async-start(f32[8,136,1024]{2,1,0:T(8,128)} %bitcast.209), calls=%async_computation | async-start | bytes 8912896 | tf_op jit(solution)/shard_map/all_to_all | solution.py:721
  255.5 52.3 %all-to-all-start.1 = ((bf16[8,128,1024]{2,1,0:T(8,128)(2,1)}), bf16[8,128,1024]{2,1,0:T(8,128)(2,1)S(1)}, u32[]{:S(2)}, u32[]{:S(2)}) async-start(bf16[8,128,1024]{2,1,0:T(8,128)(2,1)} %get-tuple-element.117), calls=%async_computation.1 | async-start | bytes 4194304 | tf_op jit(solution)/shard_map/all_to_all | solution.py:751
  352.0 52.2 %all-to-all-start.2 = ((bf16[8,128,1024]{2,1,0:T(8,128)(2,1)}), bf16[8,128,1024]{2,1,0:T(8,128)(2,1)}, u32[]{:S(2)}, u32[]{:S(2)}) async-start(bf16[8,128,1024]{2,1,0:T(8,128)(2,1)} %bitcast.212), calls=%async_computation.2 | async-start | bytes 4194304 | tf_op jit(solution)/shard_map/all_to_all | solution.py:808
  419.9 18.0 %collective-permute-start.1 = (f32[2,256,2048]{2,1,0:T(8,128)}, f32[2,256,2048]{2,1,0:T(8,128)}, u32[]{:S(2)}, u32[]{:S(2)}) collective-permute-start(f32[2,256,2048]{2,1,0:T(8,128)} %get-tuple-element.132), channel_id=1, source_target_pairs={{0,8},{8,0},{16,24},{24,16},{1,9},{9,1},{17,25},{25,17},{2,10},{10... | collective-permute-start | bytes 12582920 | tf_op jit(solution)/shard_map/ppermute | solution.py:43
  426.4 27.2 %collective-permute-start.2 = (f32[2,512,1024]{2,1,0:T(8,128)}, f32[2,512,1024]{2,1,0:T(8,128)}, u32[]{:S(2)}, u32[]{:S(2)}) collective-permute-start(f32[2,512,1024]{2,1,0:T(8,128)} %get-tuple-element.135), channel_id=1, source_target_pairs={{0,8},{8,0},{16,24},{24,16},{1,9},{9,1},{17,25},{25,17},{2,10},{10... | collective-permute-start | bytes 12582920 | tf_op jit(solution)/shard_map/ppermute | solution.py:43
  426.9 58.3 %all-to-all-start.3 = ((bf16[8,144,1024]{2,1,0:T(8,128)(2,1)}), bf16[8,144,1024]{2,1,0:T(8,128)(2,1)S(1)}, u32[]{:S(2)}, u32[]{:S(2)}) async-start(bf16[8,144,1024]{2,1,0:T(8,128)(2,1)} %get-tuple-element.127), calls=%async_computation.3 | async-start | bytes 4718592 | tf_op jit(solution)/shard_map/all_to_all | solution.py:853
  445.6 63.7 %collective-permute-start.3 = (f32[2,2,2,32,2048]{4,3,1,0,2:T(8,128)}, f32[2,2,2,32,2048]{4,3,1,0,2:T(8,128)}, u32[]{:S(2)}, u32[]{:S(2)}) collective-permute-start(f32[2,2,2,32,2048]{4,3,1,0,2:T(8,128)} %fusion.16), channel_id=1, source_target_pairs={{0,16},{8,24},{16,0},{24,8},{1,17},{9,25},{17,1},{25,9},{2,18},{10... | collective-permute-start | bytes 6291464 | tf_op jit(solution)/shard_map/ppermute | solution.py:43
  460.6 52.7 %collective-permute-start.4 = (f32[2,2,2,64,1024]{4,3,2,1,0:T(8,128)}, f32[2,2,2,64,1024]{4,3,2,1,0:T(8,128)}, u32[]{:S(2)}, u32[]{:S(2)}) collective-permute-start(f32[2,2,2,64,1024]{4,3,2,1,0:T(8,128)} %get-tuple-element.195), channel_id=1, source_target_pairs={{0,1},{1,0},{2,3},{3,2},{4,5},{5,4},{6,7},{7,6},{8,9},{9,8},{10,11... | collective-permute-start | bytes 6291464 | tf_op jit(solution)/shard_map/ppermute | solution.py:43
  584.2 26.7 %collective-permute-start.19 = (f32[2,2,64,1024]{3,2,1,0:T(8,128)}, f32[2,2,64,1024]{3,2,1,0:T(8,128)S(1)}, u32[]{:S(2)}, u32[]{:S(2)}) collective-permute-start(f32[2,2,64,1024]{3,2,1,0:T(8,128)} %get-tuple-element.199), channel_id=1, source_target_pairs={{0,16},{8,24},{16,0},{24,8},{1,17},{9,25},{17,1},{25,9},{2,18},{10... | collective-permute-start | bytes 3145736 | tf_op jit(solution)/shard_map/ppermute | solution.py:43
  585.1 30.0 %collective-permute-start.6 = (f32[2,2,32,2048]{3,2,1,0:T(8,128)}, f32[2,2,32,2048]{3,2,1,0:T(8,128)}, u32[]{:S(2)}, u32[]{:S(2)}) collective-permute-start(f32[2,2,32,2048]{3,2,1,0:T(8,128)} %get-tuple-element.201), channel_id=1, source_target_pairs={{0,1},{1,0},{2,3},{3,2},{4,5},{5,4},{6,7},{7,6},{8,9},{9,8},{10,11... | collective-permute-start | bytes 3145736 | tf_op jit(solution)/shard_map/ppermute | solution.py:43
  585.9 44.4 %collective-permute-start.9 = (f32[2,256,1152]{2,1,0:T(8,128)}, f32[2,256,1152]{2,1,0:T(8,128)}, u32[]{:S(2)}, u32[]{:S(2)}) collective-permute-start(f32[2,256,1152]{2,1,0:T(8,128)} %get-tuple-element.151), channel_id=1, source_target_pairs={{0,8},{8,0},{16,24},{24,16},{1,9},{9,1},{17,25},{25,17},{2,10},{10... | collective-permute-start | bytes 7077896 | tf_op jit(solution)/shard_map/ppermute | solution.py:43
  586.0 47.1 %collective-permute-start.14 = (f32[2,256,1280]{2,1,0:T(8,128)}, f32[2,256,1280]{2,1,0:T(8,128)}, u32[]{:S(2)}, u32[]{:S(2)}) collective-permute-start(f32[2,256,1280]{2,1,0:T(8,128)} %get-tuple-element.153), channel_id=1, source_target_pairs={{0,8},{8,0},{16,24},{24,16},{1,9},{9,1},{17,25},{25,17},{2,10},{10... | collective-permute-start | bytes 7864328 | tf_op jit(solution)/shard_map/ppermute | solution.py:43
  591.6 18.5 %collective-permute-start.26 = (f32[552]{0:T(1024)S(1)}, f32[552]{0:T(1024)S(1)}, u32[]{:S(2)}, u32[]{:S(2)}) collective-permute-start(f32[552]{0:T(1024)S(1)} %pad_maximum_fusion.8), channel_id=1, source_target_pairs={{0,1},{1,0},{2,3},{3,2},{4,5},{5,4},{6,7},{7,6},{8,9},{9,8},{10,11... | collective-permute-start | bytes 6632 | tf_op jit(solution)/shard_map/ppermute | solution.py:57
  612.0 15.2 %collective-permute-start.20 = (f32[2,64,1024]{2,1,0:T(8,128)}, f32[2,64,1024]{2,1,0:T(8,128)}, u32[]{:S(2)}, u32[]{:S(2)}) collective-permute-start(f32[2,64,1024]{2,1,0:T(8,128)} %get-tuple-element.213), channel_id=1, source_target_pairs={{0,2},{1,3},{2,0},{3,1},{4,6},{5,7},{6,4},{7,5},{8,10},{9,11},{10,... | collective-permute-start | bytes 1572872 | tf_op jit(solution)/shard_map/ppermute | solution.py:43
  616.4 25.4 %collective-permute-start.7 = (f32[2,32,2048]{2,1,0:T(8,128)S(1)}, f32[2,32,2048]{2,1,0:T(8,128)S(1)}, u32[]{:S(2)}, u32[]{:S(2)}) collective-permute-start(f32[2,32,2048]{2,1,0:T(8,128)S(1)} %get-tuple-element.215), channel_id=1, source_target_pairs={{0,2},{1,3},{2,0},{3,1},{4,6},{5,7},{6,4},{7,5},{8,10},{9,11},{10,... | collective-permute-start | bytes 1572872 | tf_op jit(solution)/shard_map/ppermute | solution.py:43
  628.1 53.1 %collective-permute-start.21 = (f32[64,1024]{1,0:T(8,128)S(1)}, f32[64,1024]{1,0:T(8,128)S(1)}, u32[]{:S(2)}, u32[]{:S(2)}) collective-permute-start(f32[64,1024]{1,0:T(8,128)S(1)} %fusion.26), channel_id=1, source_target_pairs={{0,4},{1,5},{2,6},{3,7},{4,0},{5,1},{6,2},{7,3},{8,12},{9,13},{10,... | collective-permute-start | bytes 786440 | tf_op jit(solution)/shard_map/ppermute | solution.py:43
  632.5 23.8 %collective-permute-start.10 = (f32[2,2,2,32,1152]{4,3,0,1,2:T(8,128)S(1)}, f32[2,2,2,32,1152]{4,3,0,1,2:T(8,128)S(1)}, u32[]{:S(2)}, u32[]{:S(2)}) collective-permute-start(f32[2,2,2,32,1152]{4,3,0,1,2:T(8,128)S(1)} %fusion.18), channel_id=1, source_target_pairs={{0,16},{8,24},{16,0},{24,8},{1,17},{9,25},{17,1},{25,9},{2,18},{10... | collective-permute-start | bytes 3538952 | tf_op jit(solution)/shard_map/ppermute | solution.py:43
  636.4 31.8 %collective-permute-start.15 = (f32[2,2,2,32,1280]{4,3,1,2,0:T(8,128)S(1)}, f32[2,2,2,32,1280]{4,3,1,2,0:T(8,128)S(1)}, u32[]{:S(2)}, u32[]{:S(2)}) collective-permute-start(f32[2,2,2,32,1280]{4,3,1,2,0:T(8,128)S(1)} %fusion.17), channel_id=1, source_target_pairs={{0,1},{1,0},{2,3},{3,2},{4,5},{5,4},{6,7},{7,6},{8,9},{9,8},{10,11... | collective-permute-start | bytes 3932168 | tf_op jit(solution)/shard_map/ppermute | solution.py:43
  641.8 27.2 %collective-permute-start.8 = (f32[32,2048]{1,0:T(8,128)S(1)}, f32[32,2048]{1,0:T(8,128)S(1)}, u32[]{:S(2)}, u32[]{:S(2)}) collective-permute-start(f32[32,2048]{1,0:T(8,128)S(1)} %fusion.27), channel_id=1, source_target_pairs={{0,4},{1,5},{2,6},{3,7},{4,0},{5,1},{6,2},{7,3},{8,12},{9,13},{10,... | collective-permute-start | bytes 786440 | tf_op jit(solution)/shard_map/ppermute | solution.py:43
  656.4 19.2 %collective-permute-start.11 = (f32[2,2,32,1152]{3,2,0,1:T(8,128)S(1)}, f32[2,2,32,1152]{3,2,0,1:T(8,128)S(1)}, u32[]{:S(2)}, u32[]{:S(2)}) collective-permute-start(f32[2,2,32,1152]{3,2,0,1:T(8,128)S(1)} %get-tuple-element.225), channel_id=1, source_target_pairs={{0,1},{1,0},{2,3},{3,2},{4,5},{5,4},{6,7},{7,6},{8,9},{9,8},{10,11... | collective-permute-start | bytes 1769480 | tf_op jit(solution)/shard_map/ppermute | solution.py:43
  668.4 10.7 %collective-permute-start.16 = (f32[2,2,32,1280]{3,2,0,1:T(8,128)S(1)}, f32[2,2,32,1280]{3,2,0,1:T(8,128)S(1)}, u32[]{:S(2)}, u32[]{:S(2)}) collective-permute-start(f32[2,2,32,1280]{3,2,0,1:T(8,128)S(1)} %get-tuple-element.219), channel_id=1, source_target_pairs={{0,16},{8,24},{16,0},{24,8},{1,17},{9,25},{17,1},{25,9},{2,18},{10... | collective-permute-start | bytes 1966088 | tf_op jit(solution)/shard_map/ppermute | solution.py:43
  679.2 12.0 %collective-permute-start.17 = (f32[2,32,1280]{2,1,0:T(8,128)S(1)}, f32[2,32,1280]{2,1,0:T(8,128)S(1)}, u32[]{:S(2)}, u32[]{:S(2)}) collective-permute-start(f32[2,32,1280]{2,1,0:T(8,128)S(1)} %get-tuple-element.217), channel_id=1, source_target_pairs={{0,2},{1,3},{2,0},{3,1},{4,6},{5,7},{6,4},{7,5},{8,10},{9,11},{10,... | collective-permute-start | bytes 983048 | tf_op jit(solution)/shard_map/ppermute | solution.py:43
  (44 other events, 880.9 us)
Sparse Core Ops, SparseCore 0:
  11.5 67.3 all-gather.2
  82.5 106.1 all-gather.4
